TPU v7x, 32 devices: a whole 2x2x4 slice. The times are simulated.
32 devices in a mesh: blk: 16 (over z, y, core), rep: 2 (over x).
Axes of the slice: x: 2, y: 2, z: 4, core: 2. Of those that a mesh axis runs over, the one named last changes fastest.
Arguments:
- cell_values: bfloat16 [2, 1024, 6, 192], P('rep', 'blk'), may hold values from -6 to 6
- table_ids: int32 [2, 1024], P('rep', 'blk'), may hold values from 0 to 15, as said below
- train_mask: int32 [2, 1024], P('rep', 'blk'), may hold values from 0 to 1, as said below
- feat_count: int32 [2, 16], P('rep'), may hold values from 3 to 6, as said below
- w_attn: bfloat16 [1536, 192], P(('blk', 'rep'))
- w_mlp: bfloat16 [768, 192], P(('blk', 'rep')), may hold values from -0.4375 to 0.4375
- vectors: bfloat16 [1536], P(('blk', 'rep'))
- cotangent: bfloat16 [2, 1024, 6, 192], P('rep', 'blk'), may hold values from -6 to 6
Outputs:
- layer_out: bfloat16 [2, 1024, 6, 192], P('rep', 'blk')
- cell_grads: float32 [2, 1024, 6, 192], P('rep', 'blk')
- attn_grads: float32 [1536, 192], P(('blk', 'rep'))
- mlp_grads: float32 [768, 192], P(('blk', 'rep'))
- vector_grads: float32 [1536], P(('blk', 'rep'))
Inputs may be any that keep to these rules, and one draw needn't show every extreme that they name: `table_ids`: within a pack the numbers never fall from row to row and each appears; one table runs from the first device's 64 rows to the last device's. `train_mask`: the first row of every table is 1. `feat_count`: some table of each pack has all 6.
All inputs are finite; a program needn't handle non-finite values.
Results may differ from a plain program's by a relative error of at most 0.03.
Values may be sent and summed in bfloat16 or wider, within the bound.
No kernel may reach another device: no remote copies, remote signals or barrier semaphores. Data moves between devices by JAX's collectives and lax.ppermute only.
A program may use at most 448 MiB of HBM per device.

v0:
```python
import jax
import jax.numpy as jnp
from jax import lax
from jax.sharding import PartitionSpec as P

D = 192
HEADS = 6
HEAD_DIM = 32
HIDDEN_SIZE = 384
FEAT = 6
TABLES = 16


norm_eps = 1e-05
neg_fill = -1e30


def shifted(block, axis, distance):
    devices = range(lax.axis_size(axis))
    route = [((i - distance) % len(devices), i) for i in devices]
    return lax.ppermute(block, axis, route)


def for_sending(shard):
    return jax.tree.map(lambda a: a.astype(jnp.bfloat16) if a.dtype == jnp.float32 else a, shard)


def layer_norm(inputs, gain_row, shift_row):
    centre = inputs - jnp.mean(inputs, axis=-1, keepdims=True)
    spread = jnp.mean(centre * centre, axis=-1, keepdims=True)
    return centre * lax.rsqrt(spread + norm_eps) * gain_row + shift_row


def norm_back(inputs, gain_row, shift_row, grad_out):
    _, pull_back = jax.vjp(layer_norm, inputs, gain_row, shift_row)
    return pull_back(grad_out)


def matmul(left_side, right_side):
    return jnp.dot(left_side, right_side, preferred_element_type=jnp.float32)


def matmul_t(left_side, right_side):
    return jnp.einsum("na,ba->nb", left_side, right_side, preferred_element_type=jnp.float32)


def outer_sum(left_side, right_side):
    return jnp.einsum("na,nb->ab", left_side, right_side, preferred_element_type=jnp.float32)


def to_heads(inputs, row_count):
    return inputs.reshape(row_count, FEAT, HEADS, HEAD_DIM)


def softmax_rows(scores):
    top_score = jnp.max(scores, axis=-1, keepdims=True)
    powers = jnp.exp(scores - top_score)
    return powers / jnp.sum(powers, axis=-1, keepdims=True)


def local(cell_values, table_ids, train_mask, feat_count, w_attn, w_mlp, vectors, cotangent):
    bf16 = jnp.bfloat16
    f32 = jnp.float32
    row_count = cell_values.shape[1]
    cell_count = row_count * FEAT
    score_scale = HEAD_DIM ** (-0.5)
    flat_cells = cell_values[0].reshape(cell_count, D)
    table_row = table_ids[0]
    train_row = train_mask[0]
    feat_counts = feat_count[0]
    gathered = (
        lax.all_gather(w_attn, ("blk", "rep"), axis=0, tiled=True),
        lax.all_gather(w_mlp, ("blk", "rep"), axis=0, tiled=True),
        lax.all_gather(vectors, ("blk", "rep"), axis=0, tiled=True),
    )
    attn_mats = gathered[0].reshape(8, D, D)
    mlp_mats = gathered[1]
    vector_rows = gathered[2].astype(f32).reshape(8, D)
    counted = jnp.sum(
        jnp.where(table_row[:, None] == jnp.arange(TABLES)[None, :], feat_counts[None, :], 0),
        axis=1,
    )
    valid_feat = jnp.arange(FEAT)[None, :] < counted[:, None]
    feat_query = to_heads(matmul(flat_cells, attn_mats[0]).astype(bf16), row_count)
    feat_key = to_heads(matmul(flat_cells, attn_mats[1]).astype(bf16), row_count)
    feat_value = to_heads(matmul(flat_cells, attn_mats[2]).astype(bf16), row_count)
    feat_scores = (
        jnp.einsum("rfhe,rghe->rhfg", feat_query, feat_key, preferred_element_type=f32)
        * score_scale
    )
    feat_scores = jnp.where(valid_feat[:, None, None, :], feat_scores, neg_fill)
    feat_probs = softmax_rows(feat_scores)
    feat_probs_low = feat_probs.astype(bf16)
    feat_mixed = jnp.einsum(
        "rhfg,rghe->rfhe", feat_probs_low, feat_value, preferred_element_type=f32
    )
    feat_mixed = feat_mixed.reshape(cell_count, D).astype(bf16)
    mixed_one = flat_cells.astype(f32) + matmul(feat_mixed, attn_mats[3]) + vector_rows[6]
    normed_one = layer_norm(mixed_one, vector_rows[0], vector_rows[3])
    normed_low = normed_one.astype(bf16)
    item_query = to_heads(matmul(normed_low, attn_mats[4]).astype(bf16), row_count)
    item_key = to_heads(matmul(normed_low, attn_mats[5]).astype(bf16), row_count)
    item_value = to_heads(matmul(normed_low, attn_mats[6]).astype(bf16), row_count)
    table_float = table_row.astype(f32)
    key_tags = jnp.where(train_row > 0, table_row, -1).astype(bf16)
    key_tag_float = key_tags.astype(f32)
    run_max = jnp.full((FEAT, HEADS, row_count), neg_fill, f32)
    scores = (
        jnp.einsum(
            "rfhe,jfhe->fhrj",
            item_query,
            lax.all_gather(item_key, "blk", axis=0, tiled=True),
            preferred_element_type=f32,
        )
        * score_scale
    )
    allowed = (
        table_float[:, None]
        == lax.all_gather(key_tags, "blk", axis=0, tiled=True).astype(f32)[None, :]
    )
    scores, allowed = (jnp.where(allowed[None, None], scores, neg_fill), allowed)
    new_max = jnp.maximum(run_max, jnp.max(scores, axis=-1))
    powers = jnp.where(allowed[None, None], jnp.exp(scores - new_max[..., None]), 0.0)
    run_total = jnp.sum(powers, axis=-1)
    run_acc = jnp.einsum(
        "fhrj,jfhe->fhre",
        powers.astype(bf16),
        lax.all_gather(item_value, "blk", axis=0, tiled=True),
        preferred_element_type=f32,
    )
    run_max, run_total, run_acc = (new_max, run_total, run_acc)
    item_out = (run_acc / run_total[..., None]).transpose(2, 0, 1, 3)
    log_total = run_max + jnp.log(run_total)
    item_mixed = item_out.reshape(cell_count, D).astype(bf16)
    mixed_two = normed_one + matmul(item_mixed, attn_mats[7])
    normed_two = layer_norm(mixed_two, vector_rows[1], vector_rows[4])
    normed_two_low = normed_two.astype(bf16)
    up_proj = matmul_t(normed_two_low, mlp_mats[:HIDDEN_SIZE])
    hidden = jax.nn.gelu(up_proj).astype(bf16)
    mixed_three = normed_two + matmul(hidden, mlp_mats[HIDDEN_SIZE:]) + vector_rows[7]
    output = layer_norm(mixed_three, vector_rows[2], vector_rows[5])
    grad_out = cotangent[0].reshape(cell_count, D).astype(f32)
    grad_three, gain_two_grad, shift_two_grad = norm_back(
        mixed_three, vector_rows[2], vector_rows[5], grad_out
    )
    down_bias_grad = jnp.sum(grad_three, axis=0)
    grad_down_low = grad_three.astype(bf16)
    down_grad = outer_sum(hidden, grad_down_low)
    grad_hidden = matmul_t(grad_down_low, mlp_mats[HIDDEN_SIZE:])
    _, gelu_pull = jax.vjp(jax.nn.gelu, up_proj)
    grad_up_low = gelu_pull(grad_hidden)[0].astype(bf16)
    up_grad = outer_sum(grad_up_low, normed_two_low)
    grad_normed_two = grad_three + matmul(grad_up_low, mlp_mats[:HIDDEN_SIZE])
    grad_two, gain_one_grad, shift_one_grad = norm_back(
        mixed_two, vector_rows[1], vector_rows[4], grad_normed_two
    )
    grad_two_low = grad_two.astype(bf16)
    item_out_grad = outer_sum(item_mixed, grad_two_low)
    item_grad_out = to_heads(matmul_t(grad_two_low, attn_mats[7]).astype(bf16), row_count)
    delta_rows = jnp.sum(item_grad_out.astype(f32) * item_out, axis=-1)
    log_rows = log_total.transpose(2, 0, 1)
    zero_heads = jnp.zeros((row_count, FEAT, HEADS, HEAD_DIM), f32)

    def pair_block(kv_grads, queries, grads_in, log_in, delta_in, tables_in, query_grad, weight):
        grad_key, grad_value = kv_grads
        scores = (
            jnp.einsum("jfhe,kfhe->fhjk", queries, item_key, preferred_element_type=f32)
            * score_scale
        )
        allowed = tables_in[:, None] == key_tag_float[None, :]
        scores = jnp.where(allowed[None, None], scores, neg_fill)
        probs_now = (
            jnp.where(
                allowed[None, None], jnp.exp(scores - log_in.transpose(1, 2, 0)[..., None]), 0.0
            )
            * weight
        )
        grad_value = grad_value + jnp.einsum(
            "fhjk,jfhe->kfhe", probs_now.astype(bf16), grads_in, preferred_element_type=f32
        )
        grad_probs = jnp.einsum("jfhe,kfhe->fhjk", grads_in, item_value, preferred_element_type=f32)
        grad_scores = (probs_now * (grad_probs - delta_in.transpose(1, 2, 0)[..., None])).astype(
            bf16
        )
        grad_key = grad_key + jnp.einsum(
            "fhjk,jfhe->kfhe", grad_scores, queries, preferred_element_type=f32
        )
        query_grad = query_grad + jnp.einsum(
            "fhjk,kfhe->jfhe", grad_scores, item_key, preferred_element_type=f32
        )
        return ((grad_key, grad_value), query_grad)

    half_cycle = lax.axis_size("blk") // 2
    kv_start, own_grad = pair_block(
        (zero_heads, zero_heads),
        item_query,
        item_grad_out,
        log_rows,
        delta_rows,
        table_float,
        zero_heads,
        1.0,
    )
    own_rows = (item_query, item_grad_out)
    own_sums = (log_rows, delta_rows, table_float)

    def cycle_turn(turn, state):
        kv_grads, rows_ahead, sums_ahead, rows_behind, sums_behind = state
        rows_ahead = shifted((rows_ahead[0], rows_ahead[1]), "blk", 1)
        sums_ahead = jax.tree.map(
            lambda part, own: part.astype(own.dtype),
            shifted(for_sending(sums_ahead), "blk", 1),
            sums_ahead,
        )
        rows_behind = shifted((rows_behind[0], rows_behind[1]), "blk", -1)
        sums_behind = jax.tree.map(
            lambda part, own: part.astype(own.dtype),
            shifted(for_sending(sums_behind), "blk", -1),
            sums_behind,
        )
        weight = (turn < half_cycle).astype(f32)
        kv_grads, grad_ahead = pair_block(
            kv_grads,
            rows_ahead[0],
            rows_ahead[1],
            sums_ahead[0],
            sums_ahead[1],
            sums_ahead[2],
            sums_ahead[3],
            weight,
        )
        kv_grads, grad_behind = pair_block(
            kv_grads,
            rows_behind[0],
            rows_behind[1],
            sums_behind[0],
            sums_behind[1],
            sums_behind[2],
            sums_behind[3],
            1.0,
        )
        return (
            kv_grads,
            rows_ahead,
            sums_ahead[:3] + (grad_ahead,),
            rows_behind,
            sums_behind[:3] + (grad_behind,),
        )

    state = (kv_start, own_rows, own_sums + (own_grad,), own_rows, own_sums + (zero_heads,))
    state = lax.fori_loop(1, half_cycle + 1, cycle_turn, state)
    key_accum, value_accum = state[0]
    query_accum = shifted(
        (state[2][3] + state[4][3]).astype(jnp.bfloat16), "blk", half_cycle
    ).astype(jnp.float32)
    item_query_grad = (query_accum * score_scale).astype(bf16).reshape(cell_count, D)
    item_key_grad = (key_accum * score_scale).astype(bf16).reshape(cell_count, D)
    item_value_grad = value_accum.astype(bf16).reshape(cell_count, D)
    grad_normed_one = (
        grad_two
        + matmul_t(item_query_grad, attn_mats[4])
        + matmul_t(item_key_grad, attn_mats[5])
        + matmul_t(item_value_grad, attn_mats[6])
    )
    grad_one, gain_zero_grad, shift_zero_grad = norm_back(
        mixed_one, vector_rows[0], vector_rows[3], grad_normed_one
    )
    feat_bias_grad = jnp.sum(grad_one, axis=0)
    grad_one_low = grad_one.astype(bf16)
    feat_out_grad = outer_sum(feat_mixed, grad_one_low)
    feat_grad_out = to_heads(matmul_t(grad_one_low, attn_mats[3]).astype(bf16), row_count)
    feat_grad_probs = jnp.einsum(
        "rfhe,rghe->rhfg", feat_grad_out, feat_value, preferred_element_type=f32
    )
    feat_grad_scores = (
        feat_probs
        * (feat_grad_probs - jnp.sum(feat_probs * feat_grad_probs, axis=-1, keepdims=True))
    ).astype(bf16)
    feat_query_grad = (
        (
            jnp.einsum("rhfg,rghe->rfhe", feat_grad_scores, feat_key, preferred_element_type=f32)
            * score_scale
        )
        .astype(bf16)
        .reshape(cell_count, D)
    )
    feat_key_grad = (
        (
            jnp.einsum("rhfg,rfhe->rghe", feat_grad_scores, feat_query, preferred_element_type=f32)
            * score_scale
        )
        .astype(bf16)
        .reshape(cell_count, D)
    )
    feat_value_grad = (
        jnp.einsum("rhfg,rfhe->rghe", feat_probs_low, feat_grad_out, preferred_element_type=f32)
        .astype(bf16)
        .reshape(cell_count, D)
    )
    cell_grad = (
        grad_one
        + matmul_t(feat_query_grad, attn_mats[0])
        + matmul_t(feat_key_grad, attn_mats[1])
        + matmul_t(feat_value_grad, attn_mats[2])
    )
    attn_grad = jnp.stack(
        [
            outer_sum(flat_cells, feat_query_grad),
            outer_sum(flat_cells, feat_key_grad),
            outer_sum(flat_cells, feat_value_grad),
            feat_out_grad,
            outer_sum(normed_low, item_query_grad),
            outer_sum(normed_low, item_key_grad),
            outer_sum(normed_low, item_value_grad),
            item_out_grad,
        ]
    ).reshape(8 * D, D)
    mlp_grad = jnp.concatenate([up_grad, down_grad], axis=0)
    vector_grad = jnp.stack(
        [
            gain_zero_grad,
            gain_one_grad,
            gain_two_grad,
            shift_zero_grad,
            shift_one_grad,
            shift_two_grad,
            feat_bias_grad,
            down_bias_grad,
        ]
    ).reshape(8 * D)
    attn_share, mlp_share, vector_share = (
        lax.psum_scatter(attn_grad, ("blk", "rep"), scatter_dimension=0, tiled=True),
        lax.psum_scatter(mlp_grad, ("blk", "rep"), scatter_dimension=0, tiled=True),
        lax.psum_scatter(vector_grad, ("blk", "rep"), scatter_dimension=0, tiled=True),
    )
    return (
        output.astype(bf16).reshape(1, row_count, FEAT, D),
        cell_grad.reshape(1, row_count, FEAT, D),
        attn_share,
        mlp_share,
        vector_share,
    )


def solution(mesh):
    in_specs = (
        P("rep", "blk", None, None),
        P("rep", "blk"),
        P("rep", "blk"),
        P("rep", None),
        P(("blk", "rep"), None),
        P(("blk", "rep"), None),
        P(("blk", "rep")),
        P("rep", "blk", None, None),
    )
    out_specs = (
        P("rep", "blk", None, None),
        P("rep", "blk", None, None),
        P(("blk", "rep"), None),
        P(("blk", "rep"), None),
        P(("blk", "rep")),
    )
    return jax.shard_map(local, mesh=mesh, in_specs=in_specs, out_specs=out_specs, check_vma=False)
```

profile of v0, /device:TPU:0, one launch (start us, length us, event | category | flops | bytes accessed | tf_op | source)
XLA Modules:
  0.0 907.6 jit_solution(16050907687944918180)
XLA Ops:
  7.2 74.3 %all_gather.18 = bf16[1536,192]{1,0:T(8,128)(2,1)S(1)} all-gather(bf16[48,192]{1,0:T(8,128)(2,1)} %param.14), channel_id=1, replica_groups=mesh['blk'=16,'rep'=2] {'blk','rep'}, dimensions={0}, use_global_device_ids=true | all-gather | bytes 608256 | tf_op jit(solution)/shard_map/all_gather | solution.py:72
  86.3 3.2 fusion.127
  89.5 2.1 fusion.41
  92.6 36.9 %all-reduce = bf16[1536]{0:T(1024)(128)(2,1)S(1)} all-reduce(bf16[1536]{0:T(1024)(128)(2,1)S(1)} %dynamic-update-slice), channel_id=1, replica_groups=mesh['blk'=16,'rep'=2] {'blk','rep'}, use_global_device_ids=true, to_apply=%add | all-reduce | flops 1536 | bytes 6144
  141.1 31.9 %all-reduce.1 = bf16[1024]{0:T(1024)(128)(2,1)S(1)} all-reduce(bf16[1024]{0:T(1024)(128)(2,1)S(1)} %dynamic-update-slice.1), channel_id=1, replica_groups=mesh['blk'=16,'rep'=2] {'blk'}, use_global_device_ids=true, to_apply=%add.1 | all-reduce | flops 1024 | bytes 4096
  176.6 87.8 %all_gather.23 = bf16[768,192]{1,0:T(8,128)(2,1)} all-gather(bf16[24,192]{1,0:T(8,128)(2,1)S(1)} %copy-done.78), channel_id=1, replica_groups=mesh['blk'=16,'rep'=2] {'blk','rep'}, dimensions={0}, use_global_device_ids=true | all-gather | bytes 304128 | tf_op jit(solution)/shard_map/all_gather | solution.py:73
  265.2 9.9 %fusion.24 = (f32[6,6,64]{2,1,0:T(8,128)S(1)}, f32[6,6,64,1024]{3,2,1,0:T(8,128)S(1)}) fusion(pred[64,1024]{1,0:T(8,128)(4,1)S(1)} %broadcast_compare_fusion.2, bf16[64,6,6,32]{0,3,2,1:T(8,128)(2,1)S(1)} %copy.158, bf16[1024,6,6,32]{3,2,1,0:T(8,128)(2,1)} %all-gather.3.cloned.1.call-done), kind=kOutput, calls=%fused_computation.41 | convolution fusion | flops 158070528 | bytes 12018688 | tf_op jit(solution)/shard_map/rfhe,jfhe->fhrj/dot_general | solution.py:109
  275.2 2.9 fusion.25
  280.1 56.9 %all-gather.5.cloned.1.call-done = bf16[1024,6,6,32]{3,2,1,0:T(8,128)(2,1)} async-done(((bf16[64,6,6,32]{3,2,1,0:T(8,128)(2,1)}), bf16[1024,6,6,32]{3,2,1,0:T(8,128)(2,1)}) %all-gather.5.cloned.1.call-update) | async-done | bytes 2359312 | tf_op jit(solution)/shard_map/all_gather | solution.py:128
  337.0 14.4 %fusion.129 = (bf16[64,6,6,32]{0,3,2,1:T(8,128)(2,1)S(1)}, f32[64,6,6,32]{0,3,2,1:T(8,128)}) fusion(f32[64,6,6]{0,2,1:T(8,128)S(1)} %bitcast.229, bf16[1024,6,6,32]{3,2,1,0:T(8,128)(2,1)} %all-gather.5.cloned.1.call-done, f32[6,6,64,1024]{3,2,1,0:T(8,128)} %copy-done, f32[6,6,64]{2,1,0:T(8,128)S(1)} %broadcast_maximum_fusion, ...), kind=kOutput, calls=%fused_computation.225 | convolution fusion | flops 162938880 | bytes 12322816 | tf_op jit(solution)/shard_map/fhrj,jfhe->fhre/dot_general | solution.py:125
  367.9 330.5 %while.40 = (s32[]{:T(128)}, f32[64,6,6,32]{0,3,2,1:T(8,128)S(1)}, f32[64,6,6,32]{0,3,2,1:T(8,128)S(1)}, bf16[64,6,6,32]{0,3,2,1:T(8,128)(2,1)}, bf16[64,6,6,32]...) while((s32[]{:T(128)}, f32[64,6,6,32]{0,3,2,1:T(8,128)S(1)}, ...), condition=%wide.region_17.18_spmd.clone, body=%wide.region_16.17_spmd.clone.sunk | while | flops 97651968 | bytes 18345148 | solution.py:251
  370.0 4.2 collective-permute-start.3
  385.6 6.0 collective-permute-done.7
  393.5 4.0 collective-permute-done.9
  398.1 4.4 collective-permute-start.11
  412.2 4.4 collective-permute-start.3
  428.1 4.8 collective-permute-done.7
  434.7 4.0 collective-permute-done.9
  439.3 4.4 collective-permute-start.11
  453.3 4.4 collective-permute-start.3
  469.2 4.8 collective-permute-done.7
  475.8 4.0 collective-permute-done.9
  480.4 4.4 collective-permute-start.11
  494.5 4.4 collective-permute-start.3
  510.4 4.8 collective-permute-done.7
  517.0 4.0 collective-permute-done.9
  521.6 4.4 collective-permute-start.11
  535.6 4.4 collective-permute-start.3
  551.5 4.8 collective-permute-done.7
  558.1 4.0 collective-permute-done.9
  562.7 4.4 collective-permute-start.11
  576.8 4.4 collective-permute-start.3
  592.7 4.8 collective-permute-done.7
  599.3 4.0 collective-permute-done.9
  603.9 4.4 collective-permute-start.11
  617.9 4.4 collective-permute-start.3
  633.8 4.8 collective-permute-done.7
  640.4 4.0 collective-permute-done.9
  645.0 4.4 collective-permute-start.11
  659.1 4.4 collective-permute-start.3
  675.0 4.8 collective-permute-done.7
  681.6 4.0 collective-permute-done.9
  686.2 4.4 collective-permute-start.11
  703.1 8.6 collective-permute-done.12
  715.7 2.5 multiply_reduce_fusion
  738.6 37.2 %all-reduce.2 = f32[1536]{0:T(1024)S(1)} all-reduce(f32[1536]{0:T(1024)S(1)} %reshape.382), channel_id=4, replica_groups=mesh['blk'=16,'rep'=2] {'blk','rep'}, use_global_device_ids=true, to_apply=%region_31.32.clone | all-reduce | flops 1536 | bytes 12288
  776.4 22.6 %reduce-scatter.7.cloned.1.call-done = f32[24,192]{1,0:T(8,128)} async-done(((f32[768,192]{1,0:T(8,128)}), f32[24,192]{1,0:T(8,128)}) %reduce-scatter.7.cloned.1.call-update) | async-done | bytes 18448
  799.0 101.8 %reduce-scatter.5.cloned.1.call-done = f32[48,192]{1,0:T(8,128)} async-done(((f32[1536,192]{1,0:T(8,128)}), f32[48,192]{1,0:T(8,128)}) %reduce-scatter.5.cloned.1.call-update) | async-done | bytes 36880 | tf_op jit(solution)/shard_map/reduce_scatter | solution.py:332
  (890 shorter events, 255.4 us)
Async XLA Ops:
  7.2 258.1 %all-gather.3.cloned.1.call-start = ((), (), s32[]{:S(2)}) async-start(), calls=%async_computation.2 | async-start | bytes 13369344 | tf_op jit(solution)/shard_map/all_gather | solution.py:112
  132.4 204.5 %all-gather.5.cloned.1.call-start = ((), (), s32[]{:S(2)}) async-start(), calls=%async_computation.3 | async-start | bytes 13369344 | tf_op jit(solution)/shard_map/all_gather | solution.py:128
  134.2 664.8 %reduce-scatter.7.cloned.1.call-start = ((), (), s32[]{:S(2)}) async-start(), calls=%async_computation.5 | async-start | bytes 811008
  368.5 11.2 %collective-permute-start.2 = (bf16[64]{0:T(256)(128)(2,1)}, bf16[64]{0:T(256)(128)(2,1)}, u32[]{:S(2)}, u32[]{:S(2)}) collective-permute-start(bf16[64]{0:T(256)(128)(2,1)} %convert_element_type.494), channel_id=1, source_target_pairs={{30,0},{0,2},{2,4},{4,6},{6,8},{8,10},{10,12},{12,14},{14,16},{16,... | collective-permute-start | bytes 392 | tf_op jit(solution)/shard_map/while/body/eval_jaxpr/ppermute | solution.py:21
  370.0 12.7 %collective-permute-start.3 = (bf16[64]{0:T(256)(128)(2,1)}, bf16[64]{0:T(256)(128)(2,1)}, u32[]{:S(2)}, u32[]{:S(2)}) collective-permute-start(bf16[64]{0:T(256)(128)(2,1)} %convert_element_type.496), channel_id=1, source_target_pairs={{2,0},{4,2},{6,4},{8,6},{10,8},{12,10},{14,12},{16,14},{18,16},{20... | collective-permute-start | bytes 392 | tf_op jit(solution)/shard_map/while/body/eval_jaxpr/ppermute | solution.py:21
  374.2 29.8 %collective-permute-start = (bf16[64,6,6,32]{0,3,2,1:T(8,128)(2,1)}, bf16[64,6,6,32]{0,3,2,1:T(8,128)(2,1)S(1)}, u32[]{:S(2)}, u32[]{:S(2)}) collective-permute-start(bf16[64,6,6,32]{0,3,2,1:T(8,128)(2,1)} %get-tuple-element.674), channel_id=1, source_target_pairs={{2,0},{4,2},{6,4},{8,6},{10,8},{12,10},{14,12},{16,14},{18,16},{20... | collective-permute-start | bytes 442376 | tf_op jit(solution)/shard_map/while/body/eval_jaxpr/ppermute | solution.py:21
  375.5 29.1 %collective-permute-start.4 = (bf16[64,6,6,32]{0,3,2,1:T(8,128)(2,1)}, bf16[64,6,6,32]{0,3,2,1:T(8,128)(2,1)S(1)}, u32[]{:S(2)}, u32[]{:S(2)}) collective-permute-start(bf16[64,6,6,32]{0,3,2,1:T(8,128)(2,1)} %get-tuple-element.675), channel_id=1, source_target_pairs={{2,0},{4,2},{6,4},{8,6},{10,8},{12,10},{14,12},{16,14},{18,16},{20... | collective-permute-start | bytes 442376 | tf_op jit(solution)/shard_map/while/body/eval_jaxpr/ppermute | solution.py:21
  382.7 15.4 %collective-permute-start.6 = (bf16[64,6,6,32]{0,3,2,1:T(8,128)(2,1)S(1)}, bf16[64,6,6,32]{0,3,2,1:T(8,128)(2,1)S(1)}, u32[]{:S(2)}, u32[]{:S(2)}) collective-permute-start(bf16[64,6,6,32]{0,3,2,1:T(8,128)(2,1)S(1)} %copy-done.17), channel_id=1, source_target_pairs={{30,0},{0,2},{2,4},{4,6},{6,8},{8,10},{10,12},{12,14},{14,16},{16,... | collective-permute-start | bytes 442376 | tf_op jit(solution)/shard_map/while/body/eval_jaxpr/ppermute | solution.py:21
  385.1 18.1 %collective-permute-start.8 = (bf16[64,6,6,32]{0,3,2,1:T(8,128)(2,1)}, bf16[64,6,6,32]{0,3,2,1:T(8,128)(2,1)S(1)}, u32[]{:S(2)}, u32[]{:S(2)}) collective-permute-start(bf16[64,6,6,32]{0,3,2,1:T(8,128)(2,1)} %copy-done.5), channel_id=1, source_target_pairs={{30,0},{0,2},{2,4},{4,6},{6,8},{8,10},{10,12},{12,14},{14,16},{16,... | collective-permute-start | bytes 442376 | tf_op jit(solution)/shard_map/while/body/eval_jaxpr/ppermute | solution.py:21
  410.9 11.2 %collective-permute-start.2 = (bf16[64]{0:T(256)(128)(2,1)}, bf16[64]{0:T(256)(128)(2,1)}, u32[]{:S(2)}, u32[]{:S(2)}) collective-permute-start(bf16[64]{0:T(256)(128)(2,1)} %convert_element_type.494), channel_id=1, source_target_pairs={{30,0},{0,2},{2,4},{4,6},{6,8},{8,10},{10,12},{12,14},{14,16},{16,... | collective-permute-start | bytes 392 | tf_op jit(solution)/shard_map/while/body/eval_jaxpr/ppermute | solution.py:21
  412.2 11.7 %collective-permute-start.3 = (bf16[64]{0:T(256)(128)(2,1)}, bf16[64]{0:T(256)(128)(2,1)}, u32[]{:S(2)}, u32[]{:S(2)}) collective-permute-start(bf16[64]{0:T(256)(128)(2,1)} %convert_element_type.496), channel_id=1, source_target_pairs={{2,0},{4,2},{6,4},{8,6},{10,8},{12,10},{14,12},{16,14},{18,16},{20... | collective-permute-start | bytes 392 | tf_op jit(solution)/shard_map/while/body/eval_jaxpr/ppermute | solution.py:21
  416.6 28.5 %collective-permute-start = (bf16[64,6,6,32]{0,3,2,1:T(8,128)(2,1)}, bf16[64,6,6,32]{0,3,2,1:T(8,128)(2,1)S(1)}, u32[]{:S(2)}, u32[]{:S(2)}) collective-permute-start(bf16[64,6,6,32]{0,3,2,1:T(8,128)(2,1)} %get-tuple-element.674), channel_id=1, source_target_pairs={{2,0},{4,2},{6,4},{8,6},{10,8},{12,10},{14,12},{16,14},{18,16},{20... | collective-permute-start | bytes 442376 | tf_op jit(solution)/shard_map/while/body/eval_jaxpr/ppermute | solution.py:21
  418.0 27.9 %collective-permute-start.4 = (bf16[64,6,6,32]{0,3,2,1:T(8,128)(2,1)}, bf16[64,6,6,32]{0,3,2,1:T(8,128)(2,1)S(1)}, u32[]{:S(2)}, u32[]{:S(2)}) collective-permute-start(bf16[64,6,6,32]{0,3,2,1:T(8,128)(2,1)} %get-tuple-element.675), channel_id=1, source_target_pairs={{2,0},{4,2},{6,4},{8,6},{10,8},{12,10},{14,12},{16,14},{18,16},{20... | collective-permute-start | bytes 442376 | tf_op jit(solution)/shard_map/while/body/eval_jaxpr/ppermute | solution.py:21
  423.8 15.4 %collective-permute-start.6 = (bf16[64,6,6,32]{0,3,2,1:T(8,128)(2,1)S(1)}, bf16[64,6,6,32]{0,3,2,1:T(8,128)(2,1)S(1)}, u32[]{:S(2)}, u32[]{:S(2)}) collective-permute-start(bf16[64,6,6,32]{0,3,2,1:T(8,128)(2,1)S(1)} %copy-done.17), channel_id=1, source_target_pairs={{30,0},{0,2},{2,4},{4,6},{6,8},{8,10},{10,12},{12,14},{14,16},{16,... | collective-permute-start | bytes 442376 | tf_op jit(solution)/shard_map/while/body/eval_jaxpr/ppermute | solution.py:21
  427.5 16.9 %collective-permute-start.8 = (bf16[64,6,6,32]{0,3,2,1:T(8,128)(2,1)}, bf16[64,6,6,32]{0,3,2,1:T(8,128)(2,1)S(1)}, u32[]{:S(2)}, u32[]{:S(2)}) collective-permute-start(bf16[64,6,6,32]{0,3,2,1:T(8,128)(2,1)} %copy-done.5), channel_id=1, source_target_pairs={{30,0},{0,2},{2,4},{4,6},{6,8},{8,10},{10,12},{12,14},{14,16},{16,... | collective-permute-start | bytes 442376 | tf_op jit(solution)/shard_map/while/body/eval_jaxpr/ppermute | solution.py:21
  452.1 11.2 %collective-permute-start.2 = (bf16[64]{0:T(256)(128)(2,1)}, bf16[64]{0:T(256)(128)(2,1)}, u32[]{:S(2)}, u32[]{:S(2)}) collective-permute-start(bf16[64]{0:T(256)(128)(2,1)} %convert_element_type.494), channel_id=1, source_target_pairs={{30,0},{0,2},{2,4},{4,6},{6,8},{8,10},{10,12},{12,14},{14,16},{16,... | collective-permute-start | bytes 392 | tf_op jit(solution)/shard_map/while/body/eval_jaxpr/ppermute | solution.py:21
  453.3 11.7 %collective-permute-start.3 = (bf16[64]{0:T(256)(128)(2,1)}, bf16[64]{0:T(256)(128)(2,1)}, u32[]{:S(2)}, u32[]{:S(2)}) collective-permute-start(bf16[64]{0:T(256)(128)(2,1)} %convert_element_type.496), channel_id=1, source_target_pairs={{2,0},{4,2},{6,4},{8,6},{10,8},{12,10},{14,12},{16,14},{18,16},{20... | collective-permute-start | bytes 392 | tf_op jit(solution)/shard_map/while/body/eval_jaxpr/ppermute | solution.py:21
  457.8 28.5 %collective-permute-start = (bf16[64,6,6,32]{0,3,2,1:T(8,128)(2,1)}, bf16[64,6,6,32]{0,3,2,1:T(8,128)(2,1)S(1)}, u32[]{:S(2)}, u32[]{:S(2)}) collective-permute-start(bf16[64,6,6,32]{0,3,2,1:T(8,128)(2,1)} %get-tuple-element.674), channel_id=1, source_target_pairs={{2,0},{4,2},{6,4},{8,6},{10,8},{12,10},{14,12},{16,14},{18,16},{20... | collective-permute-start | bytes 442376 | tf_op jit(solution)/shard_map/while/body/eval_jaxpr/ppermute | solution.py:21
  459.1 27.9 %collective-permute-start.4 = (bf16[64,6,6,32]{0,3,2,1:T(8,128)(2,1)}, bf16[64,6,6,32]{0,3,2,1:T(8,128)(2,1)S(1)}, u32[]{:S(2)}, u32[]{:S(2)}) collective-permute-start(bf16[64,6,6,32]{0,3,2,1:T(8,128)(2,1)} %get-tuple-element.675), channel_id=1, source_target_pairs={{2,0},{4,2},{6,4},{8,6},{10,8},{12,10},{14,12},{16,14},{18,16},{20... | collective-permute-start | bytes 442376 | tf_op jit(solution)/shard_map/while/body/eval_jaxpr/ppermute | solution.py:21
  465.0 15.4 %collective-permute-start.6 = (bf16[64,6,6,32]{0,3,2,1:T(8,128)(2,1)S(1)}, bf16[64,6,6,32]{0,3,2,1:T(8,128)(2,1)S(1)}, u32[]{:S(2)}, u32[]{:S(2)}) collective-permute-start(bf16[64,6,6,32]{0,3,2,1:T(8,128)(2,1)S(1)} %copy-done.17), channel_id=1, source_target_pairs={{30,0},{0,2},{2,4},{4,6},{6,8},{8,10},{10,12},{12,14},{14,16},{16,... | collective-permute-start | bytes 442376 | tf_op jit(solution)/shard_map/while/body/eval_jaxpr/ppermute | solution.py:21
  468.7 16.9 %collective-permute-start.8 = (bf16[64,6,6,32]{0,3,2,1:T(8,128)(2,1)}, bf16[64,6,6,32]{0,3,2,1:T(8,128)(2,1)S(1)}, u32[]{:S(2)}, u32[]{:S(2)}) collective-permute-start(bf16[64,6,6,32]{0,3,2,1:T(8,128)(2,1)} %copy-done.5), channel_id=1, source_target_pairs={{30,0},{0,2},{2,4},{4,6},{6,8},{8,10},{10,12},{12,14},{14,16},{16,... | collective-permute-start | bytes 442376 | tf_op jit(solution)/shard_map/while/body/eval_jaxpr/ppermute | solution.py:21
  494.5 11.7 %collective-permute-start.3 = (bf16[64]{0:T(256)(128)(2,1)}, bf16[64]{0:T(256)(128)(2,1)}, u32[]{:S(2)}, u32[]{:S(2)}) collective-permute-start(bf16[64]{0:T(256)(128)(2,1)} %convert_element_type.496), channel_id=1, source_target_pairs={{2,0},{4,2},{6,4},{8,6},{10,8},{12,10},{14,12},{16,14},{18,16},{20... | collective-permute-start | bytes 392 | tf_op jit(solution)/shard_map/while/body/eval_jaxpr/ppermute | solution.py:21
  498.9 28.5 %collective-permute-start = (bf16[64,6,6,32]{0,3,2,1:T(8,128)(2,1)}, bf16[64,6,6,32]{0,3,2,1:T(8,128)(2,1)S(1)}, u32[]{:S(2)}, u32[]{:S(2)}) collective-permute-start(bf16[64,6,6,32]{0,3,2,1:T(8,128)(2,1)} %get-tuple-element.674), channel_id=1, source_target_pairs={{2,0},{4,2},{6,4},{8,6},{10,8},{12,10},{14,12},{16,14},{18,16},{20... | collective-permute-start | bytes 442376 | tf_op jit(solution)/shard_map/while/body/eval_jaxpr/ppermute | solution.py:21
  500.3 27.9 %collective-permute-start.4 = (bf16[64,6,6,32]{0,3,2,1:T(8,128)(2,1)}, bf16[64,6,6,32]{0,3,2,1:T(8,128)(2,1)S(1)}, u32[]{:S(2)}, u32[]{:S(2)}) collective-permute-start(bf16[64,6,6,32]{0,3,2,1:T(8,128)(2,1)} %get-tuple-element.675), channel_id=1, source_target_pairs={{2,0},{4,2},{6,4},{8,6},{10,8},{12,10},{14,12},{16,14},{18,16},{20... | collective-permute-start | bytes 442376 | tf_op jit(solution)/shard_map/while/body/eval_jaxpr/ppermute | solution.py:21
  506.1 15.4 %collective-permute-start.6 = (bf16[64,6,6,32]{0,3,2,1:T(8,128)(2,1)S(1)}, bf16[64,6,6,32]{0,3,2,1:T(8,128)(2,1)S(1)}, u32[]{:S(2)}, u32[]{:S(2)}) collective-permute-start(bf16[64,6,6,32]{0,3,2,1:T(8,128)(2,1)S(1)} %copy-done.17), channel_id=1, source_target_pairs={{30,0},{0,2},{2,4},{4,6},{6,8},{8,10},{10,12},{12,14},{14,16},{16,... | collective-permute-start | bytes 442376 | tf_op jit(solution)/shard_map/while/body/eval_jaxpr/ppermute | solution.py:21
  509.9 16.9 %collective-permute-start.8 = (bf16[64,6,6,32]{0,3,2,1:T(8,128)(2,1)}, bf16[64,6,6,32]{0,3,2,1:T(8,128)(2,1)S(1)}, u32[]{:S(2)}, u32[]{:S(2)}) collective-permute-start(bf16[64,6,6,32]{0,3,2,1:T(8,128)(2,1)} %copy-done.5), channel_id=1, source_target_pairs={{30,0},{0,2},{2,4},{4,6},{6,8},{8,10},{10,12},{12,14},{14,16},{16,... | collective-permute-start | bytes 442376 | tf_op jit(solution)/shard_map/while/body/eval_jaxpr/ppermute | solution.py:21
  535.6 11.7 %collective-permute-start.3 = (bf16[64]{0:T(256)(128)(2,1)}, bf16[64]{0:T(256)(128)(2,1)}, u32[]{:S(2)}, u32[]{:S(2)}) collective-permute-start(bf16[64]{0:T(256)(128)(2,1)} %convert_element_type.496), channel_id=1, source_target_pairs={{2,0},{4,2},{6,4},{8,6},{10,8},{12,10},{14,12},{16,14},{18,16},{20... | collective-permute-start | bytes 392 | tf_op jit(solution)/shard_map/while/body/eval_jaxpr/ppermute | solution.py:21
  540.1 28.5 %collective-permute-start = (bf16[64,6,6,32]{0,3,2,1:T(8,128)(2,1)}, bf16[64,6,6,32]{0,3,2,1:T(8,128)(2,1)S(1)}, u32[]{:S(2)}, u32[]{:S(2)}) collective-permute-start(bf16[64,6,6,32]{0,3,2,1:T(8,128)(2,1)} %get-tuple-element.674), channel_id=1, source_target_pairs={{2,0},{4,2},{6,4},{8,6},{10,8},{12,10},{14,12},{16,14},{18,16},{20... | collective-permute-start | bytes 442376 | tf_op jit(solution)/shard_map/while/body/eval_jaxpr/ppermute | solution.py:21
  541.4 27.9 %collective-permute-start.4 = (bf16[64,6,6,32]{0,3,2,1:T(8,128)(2,1)}, bf16[64,6,6,32]{0,3,2,1:T(8,128)(2,1)S(1)}, u32[]{:S(2)}, u32[]{:S(2)}) collective-permute-start(bf16[64,6,6,32]{0,3,2,1:T(8,128)(2,1)} %get-tuple-element.675), channel_id=1, source_target_pairs={{2,0},{4,2},{6,4},{8,6},{10,8},{12,10},{14,12},{16,14},{18,16},{20... | collective-permute-start | bytes 442376 | tf_op jit(solution)/shard_map/while/body/eval_jaxpr/ppermute | solution.py:21
  547.3 15.4 %collective-permute-start.6 = (bf16[64,6,6,32]{0,3,2,1:T(8,128)(2,1)S(1)}, bf16[64,6,6,32]{0,3,2,1:T(8,128)(2,1)S(1)}, u32[]{:S(2)}, u32[]{:S(2)}) collective-permute-start(bf16[64,6,6,32]{0,3,2,1:T(8,128)(2,1)S(1)} %copy-done.17), channel_id=1, source_target_pairs={{30,0},{0,2},{2,4},{4,6},{6,8},{8,10},{10,12},{12,14},{14,16},{16,... | collective-permute-start | bytes 442376 | tf_op jit(solution)/shard_map/while/body/eval_jaxpr/ppermute | solution.py:21
  551.0 16.9 %collective-permute-start.8 = (bf16[64,6,6,32]{0,3,2,1:T(8,128)(2,1)}, bf16[64,6,6,32]{0,3,2,1:T(8,128)(2,1)S(1)}, u32[]{:S(2)}, u32[]{:S(2)}) collective-permute-start(bf16[64,6,6,32]{0,3,2,1:T(8,128)(2,1)} %copy-done.5), channel_id=1, source_target_pairs={{30,0},{0,2},{2,4},{4,6},{6,8},{8,10},{10,12},{12,14},{14,16},{16,... | collective-permute-start | bytes 442376 | tf_op jit(solution)/shard_map/while/body/eval_jaxpr/ppermute | solution.py:21
  576.8 11.7 %collective-permute-start.3 = (bf16[64]{0:T(256)(128)(2,1)}, bf16[64]{0:T(256)(128)(2,1)}, u32[]{:S(2)}, u32[]{:S(2)}) collective-permute-start(bf16[64]{0:T(256)(128)(2,1)} %convert_element_type.496), channel_id=1, source_target_pairs={{2,0},{4,2},{6,4},{8,6},{10,8},{12,10},{14,12},{16,14},{18,16},{20... | collective-permute-start | bytes 392 | tf_op jit(solution)/shard_map/while/body/eval_jaxpr/ppermute | solution.py:21
  581.2 28.5 %collective-permute-start = (bf16[64,6,6,32]{0,3,2,1:T(8,128)(2,1)}, bf16[64,6,6,32]{0,3,2,1:T(8,128)(2,1)S(1)}, u32[]{:S(2)}, u32[]{:S(2)}) collective-permute-start(bf16[64,6,6,32]{0,3,2,1:T(8,128)(2,1)} %get-tuple-element.674), channel_id=1, source_target_pairs={{2,0},{4,2},{6,4},{8,6},{10,8},{12,10},{14,12},{16,14},{18,16},{20... | collective-permute-start | bytes 442376 | tf_op jit(solution)/shard_map/while/body/eval_jaxpr/ppermute | solution.py:21
  582.6 27.9 %collective-permute-start.4 = (bf16[64,6,6,32]{0,3,2,1:T(8,128)(2,1)}, bf16[64,6,6,32]{0,3,2,1:T(8,128)(2,1)S(1)}, u32[]{:S(2)}, u32[]{:S(2)}) collective-permute-start(bf16[64,6,6,32]{0,3,2,1:T(8,128)(2,1)} %get-tuple-element.675), channel_id=1, source_target_pairs={{2,0},{4,2},{6,4},{8,6},{10,8},{12,10},{14,12},{16,14},{18,16},{20... | collective-permute-start | bytes 442376 | tf_op jit(solution)/shard_map/while/body/eval_jaxpr/ppermute | solution.py:21
  588.5 15.4 %collective-permute-start.6 = (bf16[64,6,6,32]{0,3,2,1:T(8,128)(2,1)S(1)}, bf16[64,6,6,32]{0,3,2,1:T(8,128)(2,1)S(1)}, u32[]{:S(2)}, u32[]{:S(2)}) collective-permute-start(bf16[64,6,6,32]{0,3,2,1:T(8,128)(2,1)S(1)} %copy-done.17), channel_id=1, source_target_pairs={{30,0},{0,2},{2,4},{4,6},{6,8},{8,10},{10,12},{12,14},{14,16},{16,... | collective-permute-start | bytes 442376 | tf_op jit(solution)/shard_map/while/body/eval_jaxpr/ppermute | solution.py:21
  592.2 16.9 %collective-permute-start.8 = (bf16[64,6,6,32]{0,3,2,1:T(8,128)(2,1)}, bf16[64,6,6,32]{0,3,2,1:T(8,128)(2,1)S(1)}, u32[]{:S(2)}, u32[]{:S(2)}) collective-permute-start(bf16[64,6,6,32]{0,3,2,1:T(8,128)(2,1)} %copy-done.5), channel_id=1, source_target_pairs={{30,0},{0,2},{2,4},{4,6},{6,8},{8,10},{10,12},{12,14},{14,16},{16,... | collective-permute-start | bytes 442376 | tf_op jit(solution)/shard_map/while/body/eval_jaxpr/ppermute | solution.py:21
  617.9 11.7 %collective-permute-start.3 = (bf16[64]{0:T(256)(128)(2,1)}, bf16[64]{0:T(256)(128)(2,1)}, u32[]{:S(2)}, u32[]{:S(2)}) collective-permute-start(bf16[64]{0:T(256)(128)(2,1)} %convert_element_type.496), channel_id=1, source_target_pairs={{2,0},{4,2},{6,4},{8,6},{10,8},{12,10},{14,12},{16,14},{18,16},{20... | collective-permute-start | bytes 392 | tf_op jit(solution)/shard_map/while/body/eval_jaxpr/ppermute | solution.py:21
  622.4 28.5 %collective-permute-start = (bf16[64,6,6,32]{0,3,2,1:T(8,128)(2,1)}, bf16[64,6,6,32]{0,3,2,1:T(8,128)(2,1)S(1)}, u32[]{:S(2)}, u32[]{:S(2)}) collective-permute-start(bf16[64,6,6,32]{0,3,2,1:T(8,128)(2,1)} %get-tuple-element.674), channel_id=1, source_target_pairs={{2,0},{4,2},{6,4},{8,6},{10,8},{12,10},{14,12},{16,14},{18,16},{20... | collective-permute-start | bytes 442376 | tf_op jit(solution)/shard_map/while/body/eval_jaxpr/ppermute | solution.py:21
  623.8 27.9 %collective-permute-start.4 = (bf16[64,6,6,32]{0,3,2,1:T(8,128)(2,1)}, bf16[64,6,6,32]{0,3,2,1:T(8,128)(2,1)S(1)}, u32[]{:S(2)}, u32[]{:S(2)}) collective-permute-start(bf16[64,6,6,32]{0,3,2,1:T(8,128)(2,1)} %get-tuple-element.675), channel_id=1, source_target_pairs={{2,0},{4,2},{6,4},{8,6},{10,8},{12,10},{14,12},{16,14},{18,16},{20... | collective-permute-start | bytes 442376 | tf_op jit(solution)/shard_map/while/body/eval_jaxpr/ppermute | solution.py:21
  629.6 15.4 %collective-permute-start.6 = (bf16[64,6,6,32]{0,3,2,1:T(8,128)(2,1)S(1)}, bf16[64,6,6,32]{0,3,2,1:T(8,128)(2,1)S(1)}, u32[]{:S(2)}, u32[]{:S(2)}) collective-permute-start(bf16[64,6,6,32]{0,3,2,1:T(8,128)(2,1)S(1)} %copy-done.17), channel_id=1, source_target_pairs={{30,0},{0,2},{2,4},{4,6},{6,8},{8,10},{10,12},{12,14},{14,16},{16,... | collective-permute-start | bytes 442376 | tf_op jit(solution)/shard_map/while/body/eval_jaxpr/ppermute | solution.py:21
  633.3 16.9 %collective-permute-start.8 = (bf16[64,6,6,32]{0,3,2,1:T(8,128)(2,1)}, bf16[64,6,6,32]{0,3,2,1:T(8,128)(2,1)S(1)}, u32[]{:S(2)}, u32[]{:S(2)}) collective-permute-start(bf16[64,6,6,32]{0,3,2,1:T(8,128)(2,1)} %copy-done.5), channel_id=1, source_target_pairs={{30,0},{0,2},{2,4},{4,6},{6,8},{8,10},{10,12},{12,14},{14,16},{16,... | collective-permute-start | bytes 442376 | tf_op jit(solution)/shard_map/while/body/eval_jaxpr/ppermute | solution.py:21
  659.1 11.7 %collective-permute-start.3 = (bf16[64]{0:T(256)(128)(2,1)}, bf16[64]{0:T(256)(128)(2,1)}, u32[]{:S(2)}, u32[]{:S(2)}) collective-permute-start(bf16[64]{0:T(256)(128)(2,1)} %convert_element_type.496), channel_id=1, source_target_pairs={{2,0},{4,2},{6,4},{8,6},{10,8},{12,10},{14,12},{16,14},{18,16},{20... | collective-permute-start | bytes 392 | tf_op jit(solution)/shard_map/while/body/eval_jaxpr/ppermute | solution.py:21
  663.5 28.5 %collective-permute-start = (bf16[64,6,6,32]{0,3,2,1:T(8,128)(2,1)}, bf16[64,6,6,32]{0,3,2,1:T(8,128)(2,1)S(1)}, u32[]{:S(2)}, u32[]{:S(2)}) collective-permute-start(bf16[64,6,6,32]{0,3,2,1:T(8,128)(2,1)} %get-tuple-element.674), channel_id=1, source_target_pairs={{2,0},{4,2},{6,4},{8,6},{10,8},{12,10},{14,12},{16,14},{18,16},{20... | collective-permute-start | bytes 442376 | tf_op jit(solution)/shard_map/while/body/eval_jaxpr/ppermute | solution.py:21
  664.9 27.9 %collective-permute-start.4 = (bf16[64,6,6,32]{0,3,2,1:T(8,128)(2,1)}, bf16[64,6,6,32]{0,3,2,1:T(8,128)(2,1)S(1)}, u32[]{:S(2)}, u32[]{:S(2)}) collective-permute-start(bf16[64,6,6,32]{0,3,2,1:T(8,128)(2,1)} %get-tuple-element.675), channel_id=1, source_target_pairs={{2,0},{4,2},{6,4},{8,6},{10,8},{12,10},{14,12},{16,14},{18,16},{20... | collective-permute-start | bytes 442376 | tf_op jit(solution)/shard_map/while/body/eval_jaxpr/ppermute | solution.py:21
  670.8 15.4 %collective-permute-start.6 = (bf16[64,6,6,32]{0,3,2,1:T(8,128)(2,1)S(1)}, bf16[64,6,6,32]{0,3,2,1:T(8,128)(2,1)S(1)}, u32[]{:S(2)}, u32[]{:S(2)}) collective-permute-start(bf16[64,6,6,32]{0,3,2,1:T(8,128)(2,1)S(1)} %copy-done.17), channel_id=1, source_target_pairs={{30,0},{0,2},{2,4},{4,6},{6,8},{8,10},{10,12},{12,14},{14,16},{16,... | collective-permute-start | bytes 442376 | tf_op jit(solution)/shard_map/while/body/eval_jaxpr/ppermute | solution.py:21
  674.5 16.9 %collective-permute-start.8 = (bf16[64,6,6,32]{0,3,2,1:T(8,128)(2,1)}, bf16[64,6,6,32]{0,3,2,1:T(8,128)(2,1)S(1)}, u32[]{:S(2)}, u32[]{:S(2)}) collective-permute-start(bf16[64,6,6,32]{0,3,2,1:T(8,128)(2,1)} %copy-done.5), channel_id=1, source_target_pairs={{30,0},{0,2},{2,4},{4,6},{6,8},{8,10},{10,12},{12,14},{14,16},{16,... | collective-permute-start | bytes 442376 | tf_op jit(solution)/shard_map/while/body/eval_jaxpr/ppermute | solution.py:21
  699.3 12.4 %collective-permute-start.12 = (bf16[64,6,6,32]{0,3,2,1:T(8,128)(2,1)}, bf16[64,6,6,32]{0,3,2,1:T(8,128)(2,1)S(1)}, u32[]{:S(2)}, u32[]{:S(2)}) collective-permute-start(bf16[64,6,6,32]{0,3,2,1:T(8,128)(2,1)} %add_convert_fusion), channel_id=1, source_target_pairs={{16,0},{18,2},{20,4},{22,6},{24,8},{26,10},{28,12},{30,14},{0,16},... | collective-permute-start | bytes 442376 | tf_op jit(solution)/shard_map/ppermute | solution.py:21
  702.8 198.0 %reduce-scatter.5.cloned.1.call-start = ((), (), s32[]{:S(2)}) async-start(), calls=%async_computation.4 | async-start | bytes 1622016 | tf_op jit(solution)/shard_map/reduce_scatter | solution.py:332
  (210 other events, 2415.4 us)
Sparse Core Ops, SparseCore 0:
  132.5 102.9 all-gather.2
  237.8 99.0 all-gather.4
  703.0 96.0 reduce-scatter.6
  804.7 96.1 reduce-scatter.4
where the time goes:
time: 918 us; the launch traced here: 908 us
  blocking collectives  268 us (29%)
  waiting for transfers between devices  261 us (28%)
  other arithmetic  110 us (12%)
  starting transfers between devices  94.3 us (10%)
  matrix products  87.9 us (10%)
  local copies, waits for them, and re-layouts  68.4 us (7%)
  between operations  16 us (2%)
    unnamed x3, blocking collectives  106 us
    reduce_scatter x1, waiting for transfers between devices, local(): lax.psum_scatter(attn_grad, ('blk', 'rep'), scatter_dimension=0, tiled=True)  102 us
    ppermute x97, starting transfers between devices, shifted(): return lax.ppermute(block, axis, route)  94 us
    all_gather x1, blocking collectives, local(): lax.all_gather(w_mlp, ('blk', 'rep'), axis=0, tiled=True)  87.8 us
    ppermute x97, waiting for transfers between devices, shifted(): return lax.ppermute(block, axis, route)  80 us
    all_gather x1, blocking collectives, local(): lax.all_gather(w_attn, ('blk', 'rep'), axis=0, tiled=True)  74.3 us
    convert_element_type x64, other arithmetic, for_sending(): a.astype(jnp.bfloat16)  58.1 us
    all_gather x1, waiting for transfers between devices, local(): lax.all_gather(item_value, 'blk', axis=0, tiled=True)  56.9 us
  transfers between devices with their start and end apart: 101, of which 20 were waited for; matrix products, arithmetic and copies ran while one was open for 22% of the time, Pallas kernels for 0%

commit v1 on v0

v1 whole, which is shorter than its diff:
```python
import functools
import math

import jax
import jax.numpy as jnp
from jax import lax
from jax.experimental import pallas as pl
from jax.experimental.pallas import tpu as pltpu
from jax.sharding import Mesh
from jax.sharding import PartitionSpec as P

D = 192
HEADS = 6
HEAD_DIM = 32
HIDDEN = 384
FEAT = 6
TABLES = 16

Z = 4
SLOTS = 3
SLOT_HEADS = 3
SLOT_COLS = SLOT_HEADS * HEAD_DIM
PAIR = 2 * D
LANES = 128
KEY_TILE = 256

EPS = 1e-05
FAR = -1e30
BLOCKED = -(2.0**100)
SCALE = HEAD_DIM ** (-0.5)
LOG2E = 1.4426950408889634
SCALE2 = SCALE * LOG2E

bf16 = jnp.bfloat16
f32 = jnp.float32
BLK = ("zh", "zl", "y", "core")
FAN = ("zh", "zl", "y", "rep")
TASK_AXES = ("zl", "y")
Z_AXES = ("zh", "zl")
PLANE_AXES = ("y", "rep")
TASK_ORDER = (0, 2, 1, 3)
FAR_ORDER = (0, 3, 2, 1)


def dot(a, b):
    return lax.dot_general(a, b, (((1,), (0,)), ((), ())), preferred_element_type=f32)


def dot_t(a, b):
    return lax.dot_general(a, b, (((1,), (1,)), ((), ())), preferred_element_type=f32)


def t_dot(a, b):
    return lax.dot_general(a, b, (((0,), (0,)), ((), ())), preferred_element_type=f32)


def loop(count, body, carry=None):
    if count > 8:
        return lax.fori_loop(0, count, body, carry)
    for i in range(count):
        carry = body(i, carry)
    return carry


def span(i, size):
    if isinstance(i, int):
        return slice(i * size, (i + 1) * size)
    return pl.ds(pl.multiple_of(i * size, size), size)


def task_place():
    return lax.axis_index("zl") * 2 + lax.axis_index("y")


def partner(step):
    return lax.bitwise_xor(task_place(), TASK_ORDER[step])


def own_feature(t):
    return (3 * t + 1) // 2 if isinstance(t, int) else lax.div(3 * t + 1, 2)


def shared_feature(t):
    return 1 + 3 * (t // 2) if isinstance(t, int) else 1 + 3 * lax.div(t, 2)


def is_odd():
    return lax.axis_index("y") == 1


def normed(z):
    centre = z - jnp.mean(z, axis=-1, keepdims=True)
    rstd = lax.rsqrt(jnp.mean(centre * centre, axis=-1, keepdims=True) + EPS)
    return centre * rstd, rstd


def norm_back(xhat, rstd, gain, grad):
    scaled = grad * gain
    mean_a = jnp.mean(scaled, axis=-1, keepdims=True)
    mean_b = jnp.mean(scaled * xhat, axis=-1, keepdims=True)
    return rstd * (scaled - mean_a - xhat * mean_b)


def col_sum(a):
    return jnp.sum(a, axis=0, keepdims=True)


def head_ones():
    a = lax.broadcasted_iota(jnp.int32, (D, D), 0) // HEAD_DIM
    b = lax.broadcasted_iota(jnp.int32, (D, D), 1) // HEAD_DIM
    return (a == b).astype(bf16)


def row_to_col(row, size):
    a = lax.broadcasted_iota(jnp.int32, (size, size), 0)
    b = lax.broadcasted_iota(jnp.int32, (size, size), 1)
    return jnp.sum(jnp.where(a == b, row, 0.0), axis=1, keepdims=True)


def feat_probs(query, keys, valid, ones, rows):
    prod = (keys * query[None]).reshape(FEAT * rows, D).astype(bf16)
    scores = dot(prod, ones).reshape(FEAT, rows, D)
    scores = [jnp.where(valid[g], scores[g] * SCALE2, FAR) for g in range(FEAT)]
    top = functools.reduce(jnp.maximum, scores)
    powers = [jnp.exp2(s - top) for s in scores]
    total = functools.reduce(jnp.add, powers)
    inv = 1.0 / total
    return [p * inv for p in powers]


def make_pairs(full, pair_s):
    rows = pair_s.shape[1]
    for t in range(Z):
        f, g = own_feature(t) * rows, shared_feature(t) * rows
        pair_s[t] = jnp.concatenate([full[f : f + rows, :], full[g : g + rows, :]], axis=1)


def read_pairs(pair_refs, full_s):
    for s in range(Z):
        t = partner(s)
        both = pair_refs[s][...].astype(f32)
        full_s[own_feature(t)] += both[:, :D]
        full_s[shared_feature(t)] += both[:, D:]


def feat_forward(rows, cells_ref, cot_ref, count_ref, w_ref, vec_ref, xhat_ref, rstd_ref, qkv_ref, fo_ref, prob_ref, *rest):
    x_refs, cot_out, (pair_s, cot_s, half_s) = rest[:Z], rest[Z], rest[Z + 1 :]
    cells = cells_ref[...]
    for m in range(3):
        qkv_ref[m] = dot(cells, w_ref[m * D : (m + 1) * D, :]).astype(bf16)
    counts = count_ref[...]
    valid = [counts > g for g in range(FEAT)]
    ones = head_ones()
    keys = qkv_ref[1].astype(f32).reshape(FEAT, rows, D)
    values = qkv_ref[2].astype(f32).reshape(FEAT, rows, D)
    for f in range(FEAT):
        at = slice(f * rows, (f + 1) * rows)
        probs = feat_probs(qkv_ref[0, at, :].astype(f32), keys, valid, ones, rows)
        for g in range(FEAT):
            prob_ref[f, g] = probs[g]
        mixed = functools.reduce(jnp.add, [probs[g] * values[g] for g in range(FEAT)])
        fo_ref[at, :] = mixed.astype(bf16)
    z1 = cells.astype(f32) + dot(fo_ref[...], w_ref[3 * D : 4 * D, :]) + vec_ref[6:7, :]
    xhat, rstd = normed(z1)
    xhat_ref[...] = xhat
    rstd_ref[...] = jnp.broadcast_to(rstd, rstd_ref.shape)
    x1 = (xhat * vec_ref[0:1, :] + vec_ref[3:4, :]).astype(bf16)
    make_pairs(x1, pair_s)
    cot = cot_ref[...]
    make_pairs(cot, cot_s)
    for t in range(Z):
        f = own_feature(t) * rows
        half_s[t] = jnp.concatenate([cot[f : f + rows // 2, :], cot[f + rows // 2 : f + rows, :]], axis=1)
    cot_out[...] = cot_s[task_place()]
    for s in range(Z):
        x_refs[s][:rows, :] = pair_s[partner(s)]
    x_refs[1][rows:, :] = cot_s[partner(1)]
    for s in (2, 3):
        x_refs[s][rows:, :] = half_s[partner(s)]


def key_order(h_n):
    h, core = lax.axis_index("zh"), lax.axis_index("core")
    if h_n == 2:
        near = [(h, c, s) for c in (core, 1 - core) for s in range(Z)]
        return near + [(1 - h, c, s) for pair in ((0, 1), (2, 3)) for c in (core, 1 - core) for s in pair]
    return [(a, b, s) for a in range(h_n) for b in range(2) for s in range(Z)]


def item_prepare(h_n, w_ref, code_ref, kv_w_ref, kv_wt_ref, q_w_ref, key_bias_ref, hot_ref):
    zero = jnp.zeros((D, SLOT_COLS), bf16)
    lane_pad = jnp.zeros((D, LANES - SLOT_COLS), bf16)
    mats = []
    for m in range(3):
        w = w_ref[m * D : (m + 1) * D, :]
        a, b = w[:, :SLOT_COLS], w[:, SLOT_COLS:]
        mats.append([(a, zero), (b, zero), (zero, jnp.where(is_odd(), b, a))])
    for p in range(SLOTS):
        for side in range(2):
            at = slice(side * D, (side + 1) * D)
            q_w_ref[p, at, :] = jnp.concatenate([mats[0][p][side], lane_pad], axis=1)
            kv_w_ref[p, at, :LANES] = jnp.concatenate([mats[1][p][side], lane_pad], axis=1)
            kv_w_ref[p, at, LANES:] = jnp.concatenate([mats[2][p][side], lane_pad], axis=1)
        kv_wt_ref[p] = kv_w_ref[p].astype(f32).T.astype(bf16)

    rows = code_ref.shape[1]
    per = LANES // rows
    place = lax.broadcasted_iota(jnp.int32, (LANES, LANES), 0) - SLOT_COLS
    tagged = (place >= 0) & (place < TABLES)

    def code_rows(blocks):
        codes = [code_ref[pl.ds((h * Z + partner(s)) * 2 + c, 1), :] for h, c, s in blocks]
        code = jnp.concatenate(codes, axis=1)
        table = jnp.floor(code * 0.5)
        return table.astype(jnp.int32), code - 2.0 * table

    order = key_order(h_n)
    for i in range(len(order) // per):
        table, train = code_rows(order[i * per : (i + 1) * per])
        match = (place == table) & (train > 0.5)
        bias = jnp.where(tagged, jnp.where(match, 0.0, BLOCKED), 0.0)
        key_bias_ref[span(i, LANES), :] = bias.T.astype(bf16)
    own = [(lax.axis_index("zh"), lax.axis_index("core"), s) for s in range(Z)]
    for i in range(Z // per):
        table, _ = code_rows(own[i * per : (i + 1) * per])
        hot = jnp.where(place == table, 1.0, 0.0)
        hot_ref[span(i, LANES), :] = hot.T


def only_head(a, h, keep_rest):
    lane = lax.broadcasted_iota(jnp.int32, a.shape, 1)
    mine = (lane >= h * HEAD_DIM) & (lane < (h + 1) * HEAD_DIM)
    if keep_rest:
        mine = mine | (lane >= SLOT_COLS)
    return jnp.where(mine, a, jnp.zeros_like(a))


def each_tile(part_refs, body):
    base = 0
    for ref in part_refs:
        size = min(KEY_TILE, ref.shape[0])

        def one(i, carry, ref=ref, base=base, size=size):
            start = base + i * size
            if not isinstance(i, int):
                start = pl.multiple_of(start, size)
            body(ref[span(i, size), :], pl.ds(start, size))

        loop(ref.shape[0] // size, one)
        base += ref.shape[0]


def take(refs, count):
    return refs[:count], refs[count:]


def at_slot(ref, slot, count):
    return ref.at[slot * count : (slot + 1) * count] if isinstance(slot, int) else ref


def when(condition, body):
    if isinstance(condition, bool):
        if condition:
            body()
    else:
        pl.when(condition)(body)


def task_columns(slot, h):
    start = slot * SLOT_COLS + h * HEAD_DIM
    return pl.ds(start if isinstance(slot, int) else pl.multiple_of(start, HEAD_DIM), HEAD_DIM)


def slots_of(grid):
    return [pl.program_id(0)] if grid else list(range(SLOTS))


def task_lanes(slot):
    if isinstance(slot, int):
        return slice(0, 2 * LANES) if slot < 2 else slice(PAIR - 2 * LANES, PAIR)
    return slice(0, PAIR)


def task_feature(slot):
    if isinstance(slot, int):
        return slice(slot // 2 * D, (slot // 2 + 1) * D), [False, True, is_odd()][slot]
    upper = jnp.where(slot == 2, lax.axis_index("y"), slot) == 1
    return pl.ds(pl.multiple_of(lax.div(slot, 2) * D, D), D), upper


def head_rows(h):
    return slice(h * HEAD_DIM, (h + 1) * HEAD_DIM)


def item_forward(n_parts, n_query, first, last, grid, *refs):
    parts, refs = take(refs, n_parts)
    (kv_w_all, kv_wt_all, key_bias_ref), refs = take(refs, 3)
    if first:
        (q_w_all, hot_ref), refs = take(refs, 2)
        query_parts = parts[:n_query]
        if grid:
            query_parts, refs = take(refs, 1)
    else:
        (q_all, top_in, total_in, mixed_in), refs = take(refs, 4)
    (p_all, top_ref), refs = take(refs, 2)
    if first:
        (q_all,), refs = take(refs, 1)
    if last:
        (end_ref, inv_ref, mixed_ref), refs = take(refs, 3)
        io_refs, refs = take(refs, 3)
    elif first:
        (total_ref, mixed_ref), refs = take(refs, 2)
    else:
        (end_ref, total_ref, mixed_ref), refs = take(refs, 3)
    k_s, vt_s, s_s = refs
    keys = k_s.shape[1]
    queries = q_all.shape[1]
    tile = LANES
    fold = (tile // 8, 8, queries)
    slots = slots_of(grid)
    heads = [(i, slot, h) for i, slot in enumerate(slots) for h in range(SLOT_HEADS)]

    queries_low = []
    for i, slot in enumerate(slots):
        kv_w = at_slot(kv_w_all, slot, 1)
        kv_wt = at_slot(kv_wt_all, slot, 1)
        lanes = task_lanes(slot)

        def project(x, at):
            k = dot(x[:, lanes], kv_w[0, lanes, :LANES])
            k_s[i, at, :] = (k + key_bias_ref[at, :].astype(f32)).astype(bf16)
            vt_s[i, :, at] = dot_t(kv_wt[0, LANES:, lanes], x[:, lanes]).astype(bf16)

        each_tile(parts, project)
        q_ref = at_slot(q_all, slot, 1)
        if first:
            q_w = at_slot(q_w_all, slot, 1)
            query = [dot(x[:, lanes], q_w[0, lanes, :]) for x in query_parts]
            query = (jnp.concatenate(query, axis=0) * SCALE2 + hot_ref[...]).astype(bf16)
            q_ref[0] = query
        else:
            query = q_ref[0]
        queries_low.append(query)

    tops = []
    for i, slot, h in heads:
        query_h = only_head(queries_low[i], h, True)

        def score(n, top):
            at = span(n, tile)
            s = dot_t(k_s[i, at, :], query_h)
            s_s[i * SLOT_HEADS + h, at, :] = s
            return jnp.maximum(top, jnp.max(s.reshape(fold), axis=0))

        top = loop(keys // tile, score, jnp.full((8, queries), 2.0 * BLOCKED, f32))
        tops.append(jnp.max(top, axis=0, keepdims=True))

    totals = []
    for (i, slot, h), top in zip(heads, tops):
        p_ref = at_slot(p_all, slot, SLOT_HEADS)

        def power(n, total):
            at = span(n, tile)
            p = jnp.exp2(s_s[i * SLOT_HEADS + h, at, :] - top)
            p_ref[h, at, :] = p.astype(bf16)
            return total + jnp.sum(p.reshape(fold), axis=0)

        total = loop(keys // tile, power, jnp.zeros((8, queries), f32))
        totals.append(jnp.sum(total, axis=0, keepdims=True))

    def clear():
        mixed_ref[...] = jnp.zeros_like(mixed_ref)

    if last:
        when(slots[0] == 0, clear)
    for (i, slot, h), top, total in zip(heads, tops, totals):
        mixed = dot(vt_s[i, head_rows(h), :], at_slot(p_all, slot, SLOT_HEADS)[h])
        head = pl.ds(slot * SLOT_HEADS + h, 1)
        cols = task_columns(slot, h)
        top_ref[head, :] = top
        if not first:
            end = jnp.maximum(top, top_in[head, :])
            now, before = jnp.exp2(top - end), jnp.exp2(top_in[head, :] - end)
            total = total * now + total_in[head, :] * before
            mixed = mixed * now + mixed_in[cols, :] * before
            end_ref[head, :] = end
        elif last:
            end_ref[head, :] = top
        if last:
            inv = 1.0 / total
            inv_ref[head, :] = inv
            mixed_ref[cols, :] = mixed * inv
        else:
            total_ref[head, :] = total
            mixed_ref[cols, :] = mixed

    def finish():
        half = queries // 2
        io_refs[0][...] = mixed_ref[:D, :].T.astype(bf16)
        shared = mixed_ref[D : D + SLOT_COLS, :].T.astype(bf16)
        io_refs[1][...] = shared[:half]
        io_refs[2][...] = shared[half:]

    if last:
        when(slots[-1] == SLOTS - 1, finish)


def item_turn(counts, grid, *refs):
    groups = []
    for count in counts:
        parts, refs = take(refs, count)
        groups.append(parts)
    (kv_w_all, kv_wt_all, q_all), refs = take(refs, 3)
    qt_all, refs = refs[0], refs[1:]
    for slot in slots_of(grid):
        at_slot(qt_all, slot, 1)[0] = at_slot(q_all, slot, 1)[0].astype(f32).T.astype(bf16)
        kv_w = at_slot(kv_w_all, slot, 1)
        kv_wt = at_slot(kv_wt_all, slot, 1)
        lanes = task_lanes(slot)
        for g, parts in enumerate(groups):
            xt_ref, v_all, kt_all = refs[3 * g : 3 * g + 3]
            v_ref, kt_ref = at_slot(v_all, slot, 1), at_slot(kt_all, slot, 1)

            def one(x, at):
                v_ref[0, at, :] = dot(x[:, lanes], kv_w[0, lanes, LANES:]).astype(bf16)
                kt_ref[0, :, at] = dot_t(kv_wt[0, :LANES, lanes], x[:, lanes]).astype(bf16)

            def turn(x, at):
                xt_ref[:, at] = x.astype(f32).T.astype(bf16)

            each_tile(parts, one)
            when(slot == 0, lambda: each_tile(parts, turn))


def swap_halves(w):
    other = jnp.concatenate([w[SLOT_COLS:], w[:SLOT_COLS]], axis=0)
    return jnp.where(is_odd(), other, w)


def row_middle(shared, w_ref, m_ref, vec_ref, *refs):
    w7 = w_ref[...]
    if shared:
        (lo_ref, *cot_refs, mine_ref, came_ref), refs = refs[:5], refs[5:]
        x1 = lo_ref[...].astype(f32)[:, D:]
        cot = [ref[...].astype(f32)[:, D:] for ref in cot_refs]
        io = jnp.concatenate([mine_ref[...].astype(f32), came_ref[...].astype(f32)], axis=1).astype(bf16)
        w7 = swap_halves(w7)
    else:
        (lo_ref, hi_ref, *cot_refs, own_ref), refs = refs[: 3 + Z], refs[3 + Z :]
        x1 = jnp.concatenate([lo_ref[:, :D], hi_ref[:, :D]], axis=0).astype(f32)
        wide = [ref[...].astype(f32) for ref in cot_refs[2:]]
        cot = [ref[:, :D].astype(f32) for ref in cot_refs[:2]] + [b for a in wide for b in (a[:, :D], a[:, D:])]
        io = own_ref[...]
    dz2_ref, low_refs, full_refs, dio_refs = refs[0], refs[1:8], refs[8:12], refs[12:]
    io_ref, dt2_ref, x2_ref, du_ref, hid_ref, dm_ref, cot_ref = low_refs
    xhat3_ref, dz3_ref, xhat2_ref, dx2_ref = full_refs
    cot = jnp.concatenate(cot, axis=0)
    cot_ref[...] = cot.astype(bf16)
    io_ref[...] = io
    xhat2, rstd2 = normed(x1 + dot(io, w7))
    xhat2_ref[...] = xhat2
    x2 = xhat2 * vec_ref[1:2, :] + vec_ref[4:5, :]
    x2_low = x2.astype(bf16)
    x2_ref[...] = x2_low
    up_w = m_ref[:HIDDEN, :]
    down_w = m_ref[HIDDEN:, :]
    up = dot_t(x2_low, up_w)
    c0 = 0.7978845608028654
    c1 = 0.044715
    up2 = up * up
    tanh = jnp.tanh(c0 * up * (1.0 + c1 * up2))
    half_one = 0.5 + 0.5 * tanh
    hid = (up * half_one).astype(bf16)
    hid_ref[...] = hid
    slope = half_one + 0.5 * up * (1.0 - tanh * tanh) * (c0 + 3.0 * c0 * c1 * up2)
    z3 = x2 + dot(hid, down_w) + vec_ref[7:8, :]
    xhat3, rstd3 = normed(z3)
    xhat3_ref[...] = xhat3
    dz3 = norm_back(xhat3, rstd3, vec_ref[2:3, :], cot)
    dz3_ref[...] = dz3
    dm = dz3.astype(bf16)
    dm_ref[...] = dm
    du = (dot_t(dm, down_w) * slope).astype(bf16)
    du_ref[...] = du
    dx2 = dz3 + dot(du, up_w)
    dx2_ref[...] = dx2
    dz2 = norm_back(xhat2, rstd2, vec_ref[1:2, :], dx2)
    dz2_ref[...] = dz2
    dt2 = dz2.astype(bf16)
    dt2_ref[...] = dt2
    dio = dot_t(dt2, w7).astype(bf16)
    if shared:
        dio_refs[0][...] = dio[:, :SLOT_COLS]
        dio_refs[1][...] = dio[:, SLOT_COLS:]
    else:
        dio_refs[0][...] = dio


def item_backward(n_groups, n_outs, first, last, grid, *refs):
    groups = []
    for _ in range(n_groups):
        group, refs = take(refs, 5)
        groups.append(group)
    if first:
        dio_refs, refs = take(refs, 3)
    else:
        (dt_ref, dz2_own, dz2_shared), refs = take(refs, 3)
    (qt_all, iot_ref, end_ref, inv_ref, kv_w_all), refs = take(refs, 5)
    if last:
        (q_w_all,), refs = take(refs, 1)
        if grid:
            (xtq_ref,), refs = take(refs, 1)
    if not first:
        (dq_past, g_past), refs = take(refs, 2)
    if grid:
        gw_ref, dx_ref, dxq_ref, dt_ref, dkv_s, ds_s = refs
    else:
        out_refs, refs = take(refs, n_outs)
        if last:
            gw_ref, dx_ref, dkv_s, ds_s = refs
            dxq_ref = dx_ref.at[:, : qt_all.shape[2]]
        else:
            dt_ref, ds_s, dkv_s, dx_ref = refs
    queries = qt_all.shape[2]

    def start():
        if first:
            dt_ref[:D, :] = dio_refs[0][...].astype(f32).T
            shared = jnp.concatenate([dio_refs[1][...], dio_refs[2][...]], axis=0)
            dt_ref[D : D + SLOT_COLS, :] = shared.astype(f32).T
        dx_ref[...] = jnp.zeros_like(dx_ref)
        if grid:
            dxq_ref[...] = jnp.zeros_like(dxq_ref)
        if last:
            gw_ref[...] = jnp.zeros_like(gw_ref)

    slots = slots_of(grid)
    when(slots[0] == 0, start)
    heads = [(i, slot, h) for i, slot in enumerate(slots) for h in range(SLOT_HEADS)]
    blank = jnp.zeros((HEAD_DIM, queries), bf16)
    base = 0
    grads = []
    for xt_ref, v_all, kt_all, p_all, top_ref in groups:
        keys = v_all.shape[1]
        for i, slot, h in heads:
            head = pl.ds(slot * SLOT_HEADS + h, 1)
            cols = task_columns(slot, h)
            scale = jnp.exp2(top_ref[head, :] - end_ref[head, :]) * inv_ref[head, :]
            scaled = dt_ref[cols, :] * scale
            delta = jnp.sum(scaled * iot_ref[cols, :], axis=0, keepdims=True)
            grad = scaled.astype(bf16)
            grads.append(grad)
            alone = jnp.concatenate([grad if j == h else blank for j in range(LANES // HEAD_DIM)], axis=0)
            v_ref, p_ref = at_slot(v_all, slot, 1), at_slot(p_all, slot, SLOT_HEADS)

            def score(n, carry):
                at = span(n, KEY_TILE)
                dp = dot(v_ref[0, at, :], alone)
                ds = (p_ref[h, at, :].astype(f32) * (dp - delta)).astype(bf16)
                ds_s[i * SLOT_HEADS + h, span(base // KEY_TILE + n, KEY_TILE), :] = ds
                return carry

            loop(keys // KEY_TILE, score, 0)
        base += keys

    if first:
        dq_heads = [jnp.zeros((HEAD_DIM, queries), f32)] * len(heads)
    else:
        dq_heads = [dq_past[n] for n in range(len(heads))]
    base = 0
    for g, (xt_ref, v_all, kt_all, p_all, top_ref) in enumerate(groups):
        keys = v_all.shape[1]
        for n, (i, slot, h) in enumerate(heads):
            kt_ref, p_ref = at_slot(kt_all, slot, 1), at_slot(p_all, slot, SLOT_HEADS)
            grad = grads[g * len(heads) + n]
            query_t = at_slot(qt_all, slot, 1)[0, head_rows(h), :]
            rows_k, rows_v = head_rows(h), slice(LANES + h * HEAD_DIM, LANES + (h + 1) * HEAD_DIM)

            def sums(t, dq_t):
                at, put = span(t, KEY_TILE), span(base // KEY_TILE + t, KEY_TILE)
                ds = ds_s[i * SLOT_HEADS + h, put, :]
                dkv_s[i, rows_v, put] = dot_t(grad, p_ref[h, at, :]).astype(bf16)
                dkv_s[i, rows_k, put] = (dot_t(query_t, ds) * (1.0 / LOG2E)).astype(bf16)
                return dq_t + dot(kt_ref[0, head_rows(h), at], ds) if last else dq_t

            dq_heads[n] = loop(keys // KEY_TILE, sums, dq_heads[n])
        base += keys

    unused = jnp.zeros((LANES - SLOT_COLS, base), bf16)
    for i, slot in enumerate(slots):
        kv_w = at_slot(kv_w_all, slot, 1)
        feature, upper = task_feature(slot)
        dkv_s[i, SLOT_COLS:LANES, :] = unused
        dkv_s[i, LANES + SLOT_COLS :, :] = unused
        base = 0
        g_kv = jnp.zeros((D, 2 * LANES), f32) if first else g_past[i]
        for xt_ref, v_all, kt_all, p_all, top_ref in groups:
            keys = v_all.shape[1]

            def back(n, carry):
                put = span(base // KEY_TILE + n, KEY_TILE)
                dx_ref[feature, put] += dot(kv_w[0, feature, :], dkv_s[i, :, put])
                return carry

            loop(keys // KEY_TILE, back, 0)
            if last:
                g_kv = g_kv + dot_t(xt_ref[feature, :], dkv_s[i, :, base : base + keys])
            base += keys
        if not last:
            continue
        rest = jnp.zeros((LANES - SLOT_COLS, queries), f32)
        dq_t = jnp.concatenate(dq_heads[i * SLOT_HEADS : (i + 1) * SLOT_HEADS] + [rest], axis=0)
        found = [(1, g_kv[:, :LANES]), (2, g_kv[:, LANES:])]
        dq = (dq_t * SCALE).astype(bf16)
        dxq_ref[feature, :] += dot(at_slot(q_w_all, slot, 1)[0, feature, :], dq)
        xq = xtq_ref[feature, :] if grid else groups[0][0][feature, :queries]
        found.append((0, dot_t(xq, dq)))
        blank = jnp.zeros((D, SLOT_COLS), f32)
        for m, g in found:
            g = g[:, :SLOT_COLS]
            if upper is not True:
                g_low = jnp.concatenate([g, blank], axis=1)
            if upper is not False:
                g_high = jnp.concatenate([blank, g], axis=1)
            whole = g_high if upper is True else g_low if upper is False else jnp.where(upper, g_high, g_low)
            gw_ref[m * D : (m + 1) * D, :] += whole

    if not grid:
        base = 0
        for n, ref in enumerate(out_refs):
            count = ref.shape[0]
            total = dx_ref[:, base : base + count].T
            if last and n < 2:
                shared = dz2_shared[...] if n == 0 else jnp.zeros((count, D), f32)
                total = total + jnp.concatenate([dz2_own[base : base + count, :], shared], axis=1)
            ref[...] = total.astype(ref.dtype)
            base += count


def item_far(*refs):
    groups = (refs[:2], refs[2:4])
    ds_ref, dkv_ref, dq_ref, g_ref = refs[4:]
    for slot in range(SLOTS):
        feature, _ = task_feature(slot)
        base = 0
        for xt_ref, kt_ref in groups:
            at = slice(base, base + xt_ref.shape[1])
            g = dot_t(xt_ref[feature, :], dkv_ref[slot, :, at])
            g_ref[slot] = g_ref[slot] + g if base else g
            for h in range(SLOT_HEADS):
                n = slot * SLOT_HEADS + h
                dq = dot(kt_ref[slot, head_rows(h), :], ds_ref[n, at, :])
                dq_ref[n] = dq_ref[n] + dq if base else dq
            base += xt_ref.shape[1]


def feat_backward(rows, xhat1_ref, rstd1_ref, cells_ref, qkv_ref, fo_ref, prob_ref, w_ref, vec_ref, *refs):
    dx_refs, refs = refs[:Z], refs[Z:]
    gw_ref, gvec_ref, dz1_ref, dqkv_ref, dk_s, dv_s, dfo_s, dx_s = refs
    xhat1, rstd1 = xhat1_ref[...], rstd1_ref[...]
    dx_s[...] = jnp.zeros_like(dx_s)
    read_pairs(dx_refs, dx_s)
    dx1 = dx_s[...].reshape(FEAT * rows, D)
    gvec_ref[...] = jnp.zeros_like(gvec_ref)
    gvec_ref[0:1, :] = col_sum(dx1 * xhat1)
    gvec_ref[3:4, :] = col_sum(dx1)
    dz1 = norm_back(xhat1, rstd1, vec_ref[0:1, :], dx1)
    gvec_ref[6:7, :] = col_sum(dz1)
    dz1_ref[...] = dz1
    dt1 = dz1.astype(bf16)
    gw_ref[3 * D : 4 * D, :] = t_dot(fo_ref[...], dt1)
    dfo_s[...] = dot_t(dt1, w_ref[3 * D : 4 * D, :])
    ones = head_ones()
    keys = qkv_ref[1].astype(f32).reshape(FEAT, rows, D)
    values = qkv_ref[2].astype(f32).reshape(FEAT, rows, D)
    dk_s[...] = jnp.zeros_like(dk_s)
    dv_s[...] = jnp.zeros_like(dv_s)
    for f in range(FEAT):
        at = slice(f * rows, (f + 1) * rows)
        query = qkv_ref[0, at, :].astype(f32)
        probs = [prob_ref[f, g] for g in range(FEAT)]
        dfo = dfo_s[at, :].astype(bf16).astype(f32)
        prod = (values * dfo[None]).reshape(FEAT * rows, D).astype(bf16)
        dfp = dot(prod, ones).reshape(FEAT, rows, D)
        mean = functools.reduce(jnp.add, [probs[g] * dfp[g] for g in range(FEAT)])
        dq = jnp.zeros((rows, D), f32)
        for g in range(FEAT):
            here = slice(g * rows, (g + 1) * rows)
            ds = probs[g] * (dfp[g] - mean)
            dq = dq + ds * keys[g]
            dk_s[here, :] += ds * query
            dv_s[here, :] += probs[g] * dfo
        dqkv_ref[0, at, :] = (dq * SCALE).astype(bf16)
    dqkv_ref[1] = (dk_s[...] * SCALE).astype(bf16)
    dqkv_ref[2] = dv_s[...].astype(bf16)
    for m in range(3):
        gw_ref[m * D : (m + 1) * D, :] = t_dot(cells_ref[...], dqkv_ref[m])


def cell_out(dz1_ref, dqkv_ref, w_ref, out_ref):
    total = dz1_ref[...]
    for m in range(3):
        total = total + dot_t(dqkv_ref[m], w_ref[m * D : (m + 1) * D, :])
    out_ref[...] = total


def middle_grads(vec_ref, *refs):
    sets, refs = (refs[:11], refs[11:22]), refs[22:]
    (gw_ref, gu_ref, gv_ref, gvec_ref), out_refs = refs[:4], refs[4:]
    outs = []
    for i, (io_ref, dt2_ref, x2_ref, du_ref, hid_ref, dm_ref, cot_ref, *full_refs) in enumerate(sets):
        xhat3, dz3, xhat2, dx2 = [ref[...] for ref in full_refs]
        cot = cot_ref[...].astype(f32)
        outs.append(xhat3 * vec_ref[2:3, :] + vec_ref[5:6, :])
        gw = t_dot(io_ref[...], dt2_ref[...])
        gu = t_dot(du_ref[...], x2_ref[...])
        gv = t_dot(hid_ref[...], dm_ref[...])
        rows = {1: dx2 * xhat2, 2: cot * xhat3, 4: dx2, 5: cot, 7: dz3}
        if i == 0:
            gw_ref[...], gu_ref[...], gv_ref[...] = gw, gu, gv
            gvec_ref[...] = jnp.zeros_like(gvec_ref)
        else:
            gw_ref[...] += swap_halves(gw)
            gu_ref[...] += gu
            gv_ref[...] += gv
        for k, a in rows.items():
            gvec_ref[k : k + 1, :] += col_sum(a)
    rows = out_refs[0].shape[0]
    for s in range(Z):
        own = outs[0][s * rows : (s + 1) * rows]
        if s < Z // 2:
            sides = [own, outs[1][s * rows : (s + 1) * rows]]
        else:
            sides = [own[: rows // 2], own[rows // 2 :]]
        out_refs[s][...] = jnp.concatenate(sides, axis=1).astype(bf16)


def out_collect(*refs):
    pair_refs, out_ref, full_s = refs[:Z], refs[Z], refs[Z + 1]
    rows = full_s.shape[1]
    for s in range(Z):
        t = partner(s)
        both = pair_refs[s][...]
        if s < Z // 2:
            full_s[own_feature(t)] = both[:, :D]
            full_s[shared_feature(t)] = both[:, D:]
        else:
            full_s[own_feature(t), : rows // 2, :] = both[:, :D]
            full_s[own_feature(t), rows // 2 :, :] = both[:, D:]
    out_ref[...] = full_s[...].reshape(out_ref.shape)


ATTN_ROWS = 48
MLP_ROWS = 24
VEC_PART = 48
PACK = 112
HALF = LANES // 2


def pack_rows(attn, mlp, extra):
    low, high = slice(0, LANES), slice(LANES, D)
    last = jnp.concatenate([extra, mlp[16:24, high]], axis=0)
    return jnp.concatenate(
        [
            attn[:, low],
            jnp.concatenate([attn[:16, high], attn[16:32, high]], axis=1),
            jnp.concatenate([attn[32:, high], last], axis=1),
            mlp[:, low],
            jnp.concatenate([mlp[:8, high], mlp[8:16, high]], axis=1),
        ],
        axis=0,
    )


def unpack_rows(block):
    attn_high = jnp.concatenate([block[48:64, :HALF], block[48:64, HALF:], block[64:80, :HALF]], axis=0)
    mlp_high = jnp.concatenate([block[104:, :HALF], block[104:, HALF:], block[72:80, HALF:]], axis=0)
    attn = jnp.concatenate([block[:48], attn_high], axis=1)
    mlp = jnp.concatenate([block[80:104], mlp_high], axis=1)
    return attn, mlp, block[64:72, HALF:]


def share_pack(*refs):
    sources, out_refs, targets, sems = refs[:6], refs[6 : 6 + Z], refs[6 + Z : 12 + Z], refs[12 + Z]
    copies = [pltpu.make_async_copy(a, b, sems.at[i]) for i, (a, b) in enumerate(zip(sources, targets))]
    for c in copies:
        c.start()
    for c in copies:
        c.wait()
    attn, mlp, vec, tab, train, cnt = [ref[...].astype(f32) for ref in targets]
    code = tab * 2.0 + jnp.where(train > 0, 1.0, 0.0)
    lines = [jnp.concatenate([a, jnp.zeros((1, HALF - a.shape[1]), f32)], axis=1) for a in (vec, cnt)]
    extra = jnp.concatenate([lines[0], code, lines[1], jnp.zeros((5, HALF), f32)], axis=0)
    block = pack_rows(attn, mlp, extra).astype(bf16)
    for ref in out_refs:
        ref[...] = block


def hold(*refs):
    for i in range(3):
        refs[3 + i][...] = refs[i][...]


def at_place(z_step, dy, dc, dr):
    place = (
        lax.bitwise_xor(lax.axis_index("zh") * 2 + lax.axis_index("zl"), FAR_ORDER[z_step]),
        (lax.axis_index("y") + dy) % 2,
        (lax.axis_index("core") + dc) % 2,
        (lax.axis_index("rep") + dr) % 2,
    )
    z, y, c, r = place
    return ((z * 2 + y) * 2 + c) * 2 + r, place


def share_unpack(*refs):
    part_refs, refs = refs[:8], refs[8:]
    attn_ref, mlp_ref, vec_ref, code_ref, count_ref, mlp_s, vec_s = refs
    _, _, extra = unpack_rows(part_refs[0][0].astype(f32))
    table = jnp.floor(extra[1:2] * 0.5)
    counts = jnp.zeros(table.shape, f32)
    for k in range(TABLES):
        counts = jnp.where(table == k, extra[2:3, k : k + 1], counts)
    count_ref[...] = jnp.broadcast_to(row_to_col(counts, table.shape[1]), count_ref.shape)
    for i, ref in enumerate(part_refs):
        dc, dy, dr = i // 4, FAR_ORDER[i % 4] // 2, FAR_ORDER[i % 4] % 2
        for s in range(Z):
            attn, mlp, extra = unpack_rows(ref[s].astype(f32))
            index, (z, y, c, r) = at_place(s, dy, dc, dr)
            attn_ref[pl.ds(pl.multiple_of(index * ATTN_ROWS, 16), ATTN_ROWS), :] = attn.astype(bf16)
            mlp_s[pl.ds(pl.multiple_of(index * MLP_ROWS, 8), MLP_ROWS), :] = mlp
            vec_s[c * 2 + r, pl.ds(z * 2 + y, 1), :] = extra[:1]
            if dr == 0:
                code_ref[pl.ds((z * 2 + y) * 2 + c, 1), :] = extra[1:2]
    mlp_ref[...] = mlp_s[...].astype(bf16)
    vec_ref[...] = jnp.concatenate([vec_s[j][:, :VEC_PART] for j in range(4)], axis=1)


ATTN_PACK = 80
MLP_PACK = 40


def each_share(keep_ref, give_ref, block_of):
    for dc in range(2):
        for plane in range(4):
            for s in range(Z):
                index, place = at_place(s, FAR_ORDER[plane] // 2, dc, FAR_ORDER[plane] % 2)
                block = block_of(index, place)
                if dc == 0:
                    keep_ref[plane, s] = block
                else:
                    give_ref[plane, s] = block.astype(bf16)


def mlp_pack(up_ref, down_ref, keep_ref, give_ref, mlp_s):
    mlp_s[:HIDDEN, :] = up_ref[...]
    mlp_s[HIDDEN:, :] = down_ref[...]

    def block_of(index, _):
        mlp = mlp_s[pl.ds(pl.multiple_of(index * MLP_ROWS, 8), MLP_ROWS), :]
        high = mlp[:, LANES:]
        return jnp.concatenate(
            [
                mlp[:, :LANES],
                jnp.concatenate([high[:8], high[8:16]], axis=1),
                jnp.concatenate([high[16:], jnp.zeros((8, HALF), f32)], axis=1),
            ],
            axis=0,
        )

    each_share(keep_ref, give_ref, block_of)


def grad_pack(feat_ref, item_ref, w7_ref, veca_ref, vecb_ref, keep_ref, give_ref, attn_s, vec_s):
    attn_s[: 4 * D, :] = feat_ref[...]
    attn_s[4 * D : 7 * D, :] = item_ref[...]
    attn_s[7 * D :, :] = w7_ref[...]
    vec = veca_ref[...] + vecb_ref[...]
    for j in range(4):
        part = vec[:, j * VEC_PART : (j + 1) * VEC_PART]
        vec_s[j] = jnp.concatenate([part, jnp.zeros((8, HALF - VEC_PART), f32)], axis=1)

    def block_of(index, place):
        z, y, c, r = place
        attn = attn_s[pl.ds(pl.multiple_of(index * ATTN_ROWS, 8), ATTN_ROWS), :]
        row = vec_s[c * 2 + r, pl.ds(z * 2 + y, 1), :]
        last = jnp.concatenate([row, jnp.zeros((15, HALF), f32)], axis=0)
        high = attn[:, LANES:]
        return jnp.concatenate(
            [
                attn[:, :LANES],
                jnp.concatenate([high[:16], high[16:32]], axis=1),
                jnp.concatenate([high[32:], last], axis=1),
            ],
            axis=0,
        )

    each_share(keep_ref, give_ref, block_of)


def grad_unpack(own_ref, *refs):
    total = own_ref[...]
    for ref in refs[: Z - 1]:
        total = total + ref[...].astype(f32)
    attn_ref, mlp_ref, vec_ref = refs[Z - 1 :]
    high = jnp.concatenate([total[48:64, :HALF], total[48:64, HALF:], total[64:80, :HALF]], axis=0)
    attn_ref[...] = jnp.concatenate([total[:48], high], axis=1)
    vec_ref[...] = total[64:65, HALF : HALF + VEC_PART]
    mlp = total[ATTN_PACK:]
    high = jnp.concatenate([mlp[24:32, :HALF], mlp[24:32, HALF:], mlp[32:, :HALF]], axis=0)
    mlp_ref[...] = jnp.concatenate([mlp[:24], high], axis=1)


VMEM = pl.BlockSpec(memory_space=pltpu.VMEM)
SMEM = pl.BlockSpec(memory_space=pltpu.SMEM)


def like(shape, kind=f32):
    return jax.ShapeDtypeStruct(shape, kind)


def swap(a, axis):
    return lax.ppermute(a, axis, [(0, 1), (1, 0)])


def exchange(a, axes):
    return lax.all_to_all(a, axes, 0, 0, tiled=True)


def along(axes, blocks):
    order = TASK_ORDER if axes == TASK_AXES else FAR_ORDER
    return blocks[:1] + [
        lax.ppermute(a, axes, [(i, i ^ x) for i in range(Z)]) for a, x in zip(blocks[1:], order[1:])
    ]


def gather_any(w_attn, w_mlp, vectors, table_ids, train_mask, feat_count, cells, cot, _):
    rows = table_ids.shape[1]
    fan, reps = lax.axis_size(FAN), lax.axis_size("rep")
    core = lax.axis_index("core")
    ra, rm, nv = w_attn.shape[0], w_mlp.shape[0], vectors.shape[0]
    code = (table_ids * 2 + (train_mask > 0)).astype(bf16)[0]
    last = jnp.pad(jnp.concatenate([vectors, code]), (0, D - nv - rows)).reshape(1, D)
    block = jnp.concatenate([w_attn, w_mlp, last], axis=0)
    rb = ra + rm + 1
    mine = exchange(jnp.broadcast_to(block[None], (fan, rb, D)), FAN)
    other = swap(mine, "core")
    both = jnp.stack([jnp.where(core == 0, mine, other), jnp.where(core == 0, other, mine)], axis=1)
    both = both.reshape(fan // reps, reps, 2, rb, D).transpose(0, 2, 1, 3, 4)
    attn = both[..., :ra, :].reshape(8 * D, D)
    mlp = both[..., ra : ra + rm, :].reshape(2 * HIDDEN, D)
    tail = both[..., ra + rm, :]
    vec = tail[..., :nv].reshape(8, D).astype(f32)
    codes = lax.dynamic_index_in_dim(tail[..., nv : nv + rows], lax.axis_index("rep"), 2, keepdims=False)
    hit = table_ids[0][:, None] == jnp.arange(TABLES)[None, :]
    counts = jnp.sum(jnp.where(hit, feat_count, 0), axis=1, keepdims=True).astype(f32)
    counts = jnp.broadcast_to(counts, (rows, D))
    return attn, mlp, vec, codes.reshape(-1, rows).astype(f32), counts, cells, cot


def gather_packed(w_attn, w_mlp, vectors, table_ids, train_mask, feat_count, cells, cot, limit):
    shares = (w_attn, w_mlp, vectors[None], table_ids, train_mask, feat_count)
    blocks = pl.pallas_call(
        share_pack,
        out_shape=(like((PACK, LANES), bf16),) * Z,
        in_specs=[pl.BlockSpec(memory_space=pl.ANY)] * 6,
        out_specs=(VMEM,) * Z,
        scratch_shapes=[pltpu.VMEM(a.shape, a.dtype) for a in shares] + [pltpu.SemaphoreType.DMA((6,))],
        compiler_params=pltpu.CompilerParams(vmem_limit_bytes=67000000),
        name="share_pack",
    )(*shares)
    *held, block_held = pl.pallas_call(
        hold,
        out_shape=(like(cells.shape, bf16), like(cells.shape, bf16), like((PACK, LANES), bf16)),
        in_specs=[VMEM] * 3,
        out_specs=(VMEM,) * 3,
        compiler_params=limit,
        name="hold",
    )(cells, cot, blocks[0])
    own = jnp.stack([block_held] + along(Z_AXES, list(blocks))[1:])
    own, held = lax.optimization_barrier((own, held))
    plane = along(PLANE_AXES, [own] * 4)
    *shares, counts = pl.pallas_call(
        share_unpack,
        out_shape=(
            like((8 * D, D), bf16),
            like((2 * HIDDEN, D), bf16),
            like((8, D)),
            like((4 * Z, table_ids.shape[1])),
            like((table_ids.shape[1], D)),
        ),
        in_specs=[VMEM] * 8,
        out_specs=(VMEM,) * 5,
        scratch_shapes=[pltpu.VMEM((2 * HIDDEN, D), f32), pltpu.VMEM((4, 8, HALF), f32)],
        compiler_params=limit,
        name="share_unpack",
    )(*plane, *[swap(a, "core") for a in plane])
    return *shares, counts, *held


def sum_any(grads, share, later, _):
    g_feat, g_item, g_w7, g_up, g_down, g_vec_a, g_vec_b = grads
    ra, rm, nv = share
    rb = ra + rm + 1
    fan, reps = lax.axis_size(FAN), lax.axis_size("rep")
    core = lax.axis_index("core")
    spread = (fan // reps, 2, reps)
    g_attn = jnp.concatenate([g_feat, g_item, g_w7], axis=0).reshape(spread + (ra, D))
    g_mlp = jnp.concatenate([g_up, g_down], axis=0).reshape(spread + (rm, D))
    g_vec = (g_vec_a + g_vec_b).reshape(spread + (1, nv))
    g_vec = jnp.pad(g_vec, ((0, 0),) * 4 + ((0, D - nv),))
    g_all = jnp.concatenate([g_attn, g_mlp, g_vec], axis=3)
    keep = lax.dynamic_index_in_dim(g_all, core, 1, keepdims=False)
    give = lax.dynamic_index_in_dim(g_all, 1 - core, 1, keepdims=False)
    chip = keep + swap(give.astype(bf16), "core").astype(f32)
    shares = exchange(chip.astype(bf16).reshape(fan, rb, D), FAN)
    total = jnp.sum(shares.astype(f32), axis=0)
    return total[:ra], total[ra : ra + rm], total[ra + rm, :nv], later


def over_plane(keep, got):
    sent = [keep[0]] + [(keep[i] + got[i]).astype(bf16) for i in range(1, 4)]
    return keep[0] + got[0], along(PLANE_AXES, sent)[1:]


def pack_call(kernel, grads, rows, scratch, limit, name):
    return pl.pallas_call(
        kernel,
        out_shape=(like((4, Z, rows, LANES)), like((4, Z, rows, LANES), bf16)),
        in_specs=[VMEM] * len(grads),
        out_specs=(VMEM,) * 2,
        scratch_shapes=scratch,
        compiler_params=limit,
        name=name,
    )(*grads)


def sum_packed(grads, mlp_total, share, later, limit):
    ra, rm, nv = share
    scratch = [pltpu.VMEM((8 * D, D), f32), pltpu.VMEM((4, 8, HALF), f32)]
    keep, give = pack_call(grad_pack, grads, ATTN_PACK, scratch, limit, "grad_pack")
    total, came = over_plane(keep, swap(give, "core").astype(f32))
    for a in came:
        total = total + a.astype(f32)
    total = jnp.concatenate([total, mlp_total], axis=1)
    steps = [total[0]] + [total[i].astype(bf16) for i in range(1, Z)]
    steps, later = lax.optimization_barrier((steps, later))
    attn, mlp, vec = pl.pallas_call(
        grad_unpack,
        out_shape=(like((ra, D)), like((rm, D)), like((1, nv))),
        in_specs=[VMEM] * Z,
        out_specs=(VMEM,) * 3,
        compiler_params=limit,
        name="grad_unpack",
    )(*along(Z_AXES, steps))
    return attn, mlp, vec.reshape(nv), later


def local(cell_values, table_ids, train_mask, feat_count, w_attn, w_mlp, vectors, cotangent):
    rows = cell_values.shape[1]
    cells_n = rows * FEAT
    h_n = lax.axis_size("zh")
    fast = h_n == 2
    all_rows = Z * h_n * 2 * rows
    q_rows = Z * rows
    small = pltpu.CompilerParams(vmem_limit_bytes=16 * 2**20)
    limit = small if fast else pltpu.CompilerParams(vmem_limit_bytes=63 * 2**20)

    cells = cell_values[0].transpose(1, 0, 2).reshape(cells_n, D)
    cot = cotangent[0].transpose(1, 0, 2).reshape(cells_n, D)

    shares = gather_packed if fast else gather_any
    attn, mlp, vec, codes, counts, cells, cot = shares(
        w_attn, w_mlp, vectors, table_ids, train_mask, feat_count, cells, cot, small
    )

    pair_block = like((rows, PAIR), bf16)
    half_rows = rows + rows // 2
    xhat1, rstd1, qkv, fo, probs, *x_out, cot_own = pl.pallas_call(
        functools.partial(feat_forward, rows),
        out_shape=(
            like((cells_n, D)),
            like((cells_n, D)),
            like((3, cells_n, D), bf16),
            like((cells_n, D), bf16),
            like((FEAT, FEAT, rows, D)),
            pair_block,
            like((2 * rows, PAIR), bf16),
            like((half_rows, PAIR), bf16),
            like((half_rows, PAIR), bf16),
            pair_block,
        ),
        in_specs=[VMEM] * 5,
        out_specs=(VMEM,) * 10,
        scratch_shapes=[
            pltpu.VMEM((Z, rows, PAIR), bf16),
            pltpu.VMEM((Z, rows, PAIR), bf16),
            pltpu.VMEM((Z, rows // 2, PAIR), bf16),
        ],
        compiler_params=small,
        name="feat_forward",
    )(cells, cot, counts, attn[: 4 * D], vec)

    def whole(*shape):
        return pl.BlockSpec(shape, lambda i: (0,) * len(shape))

    def by_slot(*shape):
        once = {"pipeline_mode": pl.Buffered(1)} if math.prod(shape) > 2**22 else {}
        return pl.BlockSpec(shape, lambda i: (i,) + (0,) * (len(shape) - 1), **once)

    def item_call(kernel, ins, outs, scratch, name):
        def specs(pairs):
            if fast:
                return [VMEM] * len(pairs)
            return [by_slot(a.shape[0] // SLOTS, *a.shape[1:]) if by else whole(*a.shape) for a, by in pairs]

        return pl.pallas_call(
            kernel,
            out_shape=[a for a, _ in outs],
            in_specs=specs(ins),
            out_specs=specs(outs),
            scratch_shapes=scratch,
            compiler_params=limit,
            cost_estimate=pl.CostEstimate(flops=10**8, bytes_accessed=0, transcendentals=0),
            name=name,
            **({} if fast else {"grid": (SLOTS,)}),
        )(*[a for a, _ in ins])

    def shared(*arrays):
        return [(a, False) for a in arrays]

    def tasked(*arrays):
        return [(a, True) for a in arrays]

    heads_block, pair_t = like((16, q_rows)), like((PAIR, q_rows))

    def forward_call(parts, bias, first, last, extra):
        keys = sum(a.shape[0] for a in parts)
        tasks = SLOTS if fast else 1
        outs = tasked(like((SLOTS * SLOT_HEADS, keys, q_rows), bf16)) + shared(heads_block)
        if first:
            outs += tasked(like((SLOTS, q_rows, LANES), bf16))
        if last:
            half_heads = like((q_rows // 2, SLOT_COLS), bf16)
            outs += shared(heads_block, heads_block, pair_t, like((q_rows, D), bf16), half_heads, half_heads)
        else:
            outs += shared(*([heads_block] * (1 if first else 2)), pair_t)
        scratch = [
            pltpu.VMEM((tasks, keys, LANES), bf16),
            pltpu.VMEM((tasks, LANES, keys), bf16),
            pltpu.VMEM((tasks * SLOT_HEADS, keys, q_rows), f32),
        ]
        kernel = functools.partial(item_forward, len(parts), 2, first, last, not fast)
        ins = shared(*parts) + tasked(kv_w, kv_wt) + shared(bias) + extra
        return item_call(kernel, ins, outs, scratch, "item_forward")

    def turn_call(groups, query):
        outs = tasked(like((SLOTS, LANES, q_rows), bf16))
        for parts in groups:
            keys = sum(a.shape[0] for a in parts)
            outs += shared(like((PAIR, keys), bf16))
            outs += tasked(like((SLOTS, keys, LANES), bf16), like((SLOTS, LANES, keys), bf16))
        kernel = functools.partial(item_turn, [len(g) for g in groups], not fast)
        ins = shared(*sum(groups, [])) + tasked(kv_w, kv_wt, query)
        query_t, *rest = item_call(kernel, ins, outs, [], "item_turn")
        return query_t, [tuple(rest[i : i + 3]) for i in range(0, len(rest), 3)]

    def backward_call(groups, parts, first, last, grads, extra):
        keys = sum(g[1].shape[1] for g in groups)
        tasks = SLOTS if fast else 1
        kv_shape, ds_shape = (tasks, 2 * LANES, keys), (tasks * SLOT_HEADS, keys, q_rows)
        scratch = [pltpu.VMEM(kv_shape, bf16), pltpu.VMEM(ds_shape, bf16)]
        if fast:
            outs = shared(*parts)
            outs += shared(like((3 * D, D))) if last else shared(pair_t, like(ds_shape, bf16), like(kv_shape, bf16))
            scratch = [pltpu.VMEM((PAIR, keys), f32)] + (scratch if last else [])
        else:
            outs = shared(like((3 * D, D)), *parts)
            scratch = [pltpu.VMEM((PAIR, q_rows), f32)] + scratch
        ins = []
        for xt, v, kt, p, top in groups:
            ins += shared(xt) + tasked(v, kt, p) + shared(top)
        ins += shared(*grads) + tasked(query_t) + shared(io_t, end, inv) + tasked(kv_w) + extra
        kernel = functools.partial(item_backward, len(groups), len(parts), first, last, not fast)
        return item_call(kernel, ins, outs, scratch, "item_backward")

    kv_w, kv_wt, q_w, key_bias, hot = pl.pallas_call(
        functools.partial(item_prepare, h_n),
        out_shape=(
            like((SLOTS, PAIR, 2 * LANES), bf16),
            like((SLOTS, 2 * LANES, PAIR), bf16),
            like((SLOTS, PAIR, LANES), bf16),
            like((all_rows, LANES), bf16),
            like((q_rows, LANES)),
        ),
        in_specs=[VMEM] * 2,
        out_specs=(VMEM,) * 5,
        compiler_params=limit,
        name="item_prepare",
    )(attn[4 * D : 7 * D], codes)

    def to_task(block, i):
        return lax.ppermute(block, TASK_AXES, [(j, j ^ TASK_ORDER[i]) for j in range(Z)])

    came = [to_task(x_out[i], i) for i in range(1, Z)]
    x_lo = jnp.concatenate([x_out[0], came[0][:rows]], axis=0)
    came[1:], _ = lax.optimization_barrier((came[1:], x_lo))
    x_hi = jnp.concatenate([a[:rows] for a in came[1:]], axis=0)
    cot_in = [cot_own] + [a[rows:] for a in came]
    if fast:
        h_lo, h_hi = swap(x_lo, "zh"), swap(x_hi, "zh")
        near = [x_lo, x_hi, swap(x_lo, "core"), swap(x_hi, "core")]
        ends = (0, 2 * q_rows, 3 * q_rows, 4 * q_rows)
        bias = [key_bias[a:b] for a, b in zip(ends, ends[1:])]
        near_p, near_top, query, total, mixed = forward_call(
            near, bias[0], True, False, tasked(q_w) + shared(hot)
        )
        h_lo, total = lax.optimization_barrier((h_lo, total))
        far_lo = [h_lo, swap(h_lo, "core")]
        lo_p, lo_top, end, total, mixed = forward_call(
            far_lo, bias[1], False, False, tasked(query) + shared(near_top, total, mixed)
        )
        h_hi, total = lax.optimization_barrier((h_hi, total))
        far_hi = [h_hi, swap(h_hi, "core")]
        hi_p, hi_top, end, inv, io_t, io_own, io_mine, io_give = forward_call(
            far_hi, bias[2], False, True, tasked(query) + shared(end, total, mixed)
        )
    else:
        x_q = jnp.concatenate([x_lo, x_hi], axis=0)
        parts = [lax.all_gather(x_q, ("zh", "core"), axis=0, tiled=True)]
        all_p, all_top, query, end, inv, io_t, io_own, io_mine, io_give = forward_call(
            parts, key_bias, True, True, tasked(q_w) + shared(hot, x_q)
        )

    def to_shared(block):
        return lax.ppermute(block, "y", [(0, 1), (1, 0)])

    io_came = to_shared(io_give)
    query, _ = lax.optimization_barrier((query, io_give))
    query_t, turned = turn_call([near, far_lo, far_hi] if fast else [parts], query)

    cells_low = like((cells_n, D), bf16)

    def middle_call(shared, ins, dio_shapes):
        count = q_rows // 2 if shared else q_rows
        low, full, hidden = like((count, D), bf16), like((count, D)), like((count, HIDDEN), bf16)
        dz2, *outs = pl.pallas_call(
            functools.partial(row_middle, shared),
            out_shape=[full] + [low] * 3 + [hidden] * 2 + [low] * 2 + [full] * 4 + dio_shapes,
            in_specs=[VMEM] * (3 + len(ins)),
            out_specs=[VMEM] * (12 + len(dio_shapes)),
            compiler_params=small,
            name="row_middle",
        )(attn[7 * D :], mlp, vec, *ins)
        return dz2, outs[:11], outs[11:]

    half_heads = like(io_mine.shape, bf16)
    dz2_own, kept, (dio_own,) = middle_call(False, [x_lo, x_hi, *cot_in, io_own], [like(io_own.shape, bf16)])
    io_came, dio_own = lax.optimization_barrier((io_came, dio_own))
    dz2_shared, kept_shared, (dio_mine, dio_give) = middle_call(
        True, [x_lo, *cot_in[:2], io_mine, io_came], [half_heads] * 2
    )
    dz2, kept = (dz2_own, dz2_shared), kept + kept_shared
    dio_in = [dio_own, dio_mine, to_shared(dio_give)]

    def rest_of_middle(kept):
        return pl.pallas_call(
            middle_grads,
            out_shape=(like((D, D)), like((HIDDEN, D)), like((HIDDEN, D)), like((8, D)))
            + (pair_block,) * 2
            + (like((rows // 2, PAIR), bf16),) * 2,
            in_specs=[VMEM] * 23,
            out_specs=(VMEM,) * (4 + Z),
            compiler_params=small,
            name="middle_grads",
        )(vec, *kept)

    if fast:
        half_f, half_b = like((2 * rows, PAIR)), like((2 * rows, PAIR), bf16)
        near, far_lo, far_hi = (t + s for t, s in zip(turned, ((near_p, near_top), (lo_p, lo_top), (hi_p, hi_top))))
        g_w7, g_up, g_down, g_vec_b, *out_blocks = rest_of_middle(kept)
        mlp_keep, mlp_give = pack_call(
            mlp_pack, (g_up, g_down), MLP_PACK, [pltpu.VMEM((2 * HIDDEN, D), f32)], small, "mlp_pack"
        )
        dio_in[2], mlp_give = lax.optimization_barrier((dio_in[2], mlp_give))
        lo_h, lo_hc, hi_h, hi_hc, dio_t, ds, dkv = backward_call(
            [far_lo, far_hi], (half_f, half_b) * 2, True, False, dio_in, []
        )
        dq_far, g_far = pl.pallas_call(
            item_far,
            out_shape=(like((SLOTS * SLOT_HEADS, HEAD_DIM, q_rows)), like((SLOTS, D, 2 * LANES))),
            in_specs=[VMEM] * 6,
            out_specs=(VMEM,) * 2,
            compiler_params=small,
            name="item_far",
        )(far_lo[0], far_lo[2], far_hi[0], far_hi[2], ds, dkv)
        from_c = [swap(a, "core") for a in (lo_hc, hi_hc)]
        from_c, dq_far = lax.optimization_barrier((from_c, dq_far))
        sent = [(a + b.astype(f32)).astype(bf16) for a, b in zip((lo_h, hi_h), from_c)]
        sent, dio_t, mlp_give = lax.optimization_barrier((sent, dio_t, mlp_give))
        from_h = [swap(a, "zh") for a in sent]
        mlp_got = swap(mlp_give, "core")
        *own, lo_c, hi_c, g_item = backward_call(
            [near],
            (half_f,) * 2 + (half_b,) * 2,
            False,
            True,
            [dio_t, *dz2],
            tasked(q_w) + shared(dq_far, g_far),
        )
        mlp_got, g_item = lax.optimization_barrier((mlp_got, g_item))
        mlp_total, mlp_came = over_plane(mlp_keep, mlp_got.astype(f32))
        from_h, to_c, out_blocks, mlp_came = lax.optimization_barrier((from_h, (lo_c, hi_c), out_blocks, mlp_came))
        for a in mlp_came:
            mlp_total = mlp_total + a.astype(f32)
        from_c = [swap(a, "core") for a in to_c]
        own = [(a + b.astype(f32) + c.astype(f32)).astype(bf16) for a, b, c in zip(own, from_c, from_h)]
    else:
        (xt, v, kt), = turned
        at_query = (lax.axis_index("zh") * 2 + lax.axis_index("core")) * q_rows
        xt_q = lax.dynamic_slice_in_dim(xt, at_query, q_rows, 1)
        g_item, dx_t, dxq_t = backward_call(
            [(xt, v, kt, all_p, all_top)],
            (like((PAIR, all_rows)), like((PAIR, q_rows))),
            True,
            True,
            dio_in,
            tasked(q_w) + shared(xt_q),
        )
        own = lax.psum_scatter(dx_t.T, ("zh", "core"), scatter_dimension=0, tiled=True) + dxq_t.T
        own = own + jnp.concatenate([dz2[0], jnp.pad(dz2[1], ((0, q_rows // 2), (0, 0)))], axis=1)
        own = jnp.split(own.astype(bf16), 2)
        g_w7, g_up, g_down, g_vec_b, *out_blocks = rest_of_middle(kept)
    dx_blocks = [own[s // 2][s % 2 * rows : (s % 2 + 1) * rows] for s in range(Z)]
    came = [to_task(jnp.concatenate([a, b], axis=0), i) for i, (a, b) in enumerate(zip(dx_blocks, out_blocks)) if i]
    dx_in = dx_blocks[:1] + [a[:rows] for a in came]
    out = pl.pallas_call(
        out_collect,
        out_shape=cells_low,
        in_specs=[VMEM] * Z,
        out_specs=VMEM,
        scratch_shapes=[pltpu.VMEM((FEAT, rows, D), bf16)],
        compiler_params=small,
        name="out_collect",
    )(out_blocks[0], *[a[rows:] for a in came])

    g_feat, g_vec_a, dz1, dqkv = pl.pallas_call(
        functools.partial(feat_backward, rows),
        out_shape=(like((4 * D, D)), like((8, D)), like((cells_n, D)), like((3, cells_n, D), bf16)),
        in_specs=[VMEM] * (8 + Z),
        out_specs=(VMEM,) * 4,
        scratch_shapes=[
            pltpu.VMEM((cells_n, D), f32),
            pltpu.VMEM((cells_n, D), f32),
            pltpu.VMEM((cells_n, D), f32),
            pltpu.VMEM((FEAT, rows, D), f32),
        ],
        compiler_params=small,
        name="feat_backward",
    )(xhat1, rstd1, cells, qkv, fo, probs, attn[: 4 * D], vec, *dx_in)

    share = (w_attn.shape[0], w_mlp.shape[0], vectors.shape[0])
    if fast:
        grads = (g_feat, g_item, g_w7, g_vec_a, g_vec_b)
        attn_share, mlp_share, vec_share, dz1 = sum_packed(grads, mlp_total, share, dz1, small)
    else:
        grads = (g_feat, g_item, g_w7, g_up, g_down, g_vec_a, g_vec_b)
        attn_share, mlp_share, vec_share, dz1 = sum_any(grads, share, dz1, small)

    dcell = pl.pallas_call(
        cell_out,
        out_shape=like((cells_n, D)),
        in_specs=[VMEM] * 3,
        out_specs=VMEM,
        compiler_params=small,
        name="cell_out",
    )(dz1, dqkv, attn[: 3 * D])

    def rows_first(a):
        return a.reshape(FEAT, rows, D).transpose(1, 0, 2)[None]

    return (
        rows_first(out),
        rows_first(dcell),
        attn_share,
        mlp_share,
        vec_share,
    )


def solution(mesh):
    blk_n, rep_n = mesh.devices.shape
    fine = Mesh(mesh.devices.reshape(blk_n // (2 * Z), 2, 2, 2, rep_n), BLK + ("rep",))
    every = BLK + ("rep",)
    in_specs = (
        P("rep", BLK, None, None),
        P("rep", BLK),
        P("rep", BLK),
        P("rep", None),
        P(every, None),
        P(every, None),
        P(every),
        P("rep", BLK, None, None),
    )
    out_specs = (
        P("rep", BLK, None, None),
        P("rep", BLK, None, None),
        P(every, None),
        P(every, None),
        P(every),
    )
    return jax.shard_map(local, mesh=fine, in_specs=in_specs, out_specs=out_specs, check_vma=False)
```

time: 918 us -> 99.6 us (0.11); the launches traced: 908 us -> 99.3 us
  blocking collectives: 268 us -> 0 us
  waiting for transfers between devices: 261 us -> 31 us
  other arithmetic: 110 us -> 0.44 us
  matrix products: 87.9 us -> 0 us
  local copies, waits for them, and re-layouts: 68.4 us -> 2.79 us
  starting transfers between devices: 94.3 us -> 38.1 us
  Pallas kernels: 0 us -> 26 us
  between operations: 16 us -> 0.99 us
    all_gather x2 -> x0, blocking collectives: 162 us -> none  [the longest x1 87.8 us: local(): lax.all_gather(w_mlp, ('blk', 'rep'), axis=0, tiled=True)]
    unnamed x3 -> x0, blocking collectives: 106 us -> none
    reduce_scatter x1 -> x0, waiting for transfers between devices: 102 us -> none  [local(): lax.psum_scatter(attn_grad, ('blk', 'rep'), scatter_dimension=0, tiled=True)]
    convert_element_type x121 -> x7, other arithmetic: 95.9 us -> 0.27 us  [the longest x2 0.09 us: over_plane(): sent = [keep[0]] + [(keep[i] + got[i]).astype(bf16) for i in range(1, 4)]]
    dot_general x122 -> x0, matrix products: 84.7 us -> none  [the longest x1 14.4 us: local(): jnp.einsum('fhrj,jfhe->fhre', powers.astype(bf16), lax.all_gather(item_va...]
    all_gather x2 -> x0, waiting for transfers between devices: 56.9 us -> none  [the longest x1 56.9 us: local(): lax.all_gather(item_value, 'blk', axis=0, tiled=True)]
    ppermute x97 -> x41, starting transfers between devices: 94 us -> 38.1 us  [the longest x15 20.9 us: along(): lax.ppermute(a, axes, [(i, i ^ x) for i in range(Z)])]
    ppermute x97 -> x41, waiting for transfers between devices: 80 us -> 31 us  [the longest x15 12.4 us: along(): lax.ppermute(a, axes, [(i, i ^ x) for i in range(Z)])]
  transfers between devices with their start and end apart: 101 -> 41, of which waited for: 20 -> 23; matrix products, arithmetic and copies ran while one was open for 22% -> 0% of each run, Pallas kernels for 0% -> 13%
where the time goes in v1:
time: 99.6 us; the launch traced here: 99.3 us
  starting transfers between devices  38.1 us (38%)
  waiting for transfers between devices  31 us (31%)
  Pallas kernels  26 us (26%)
  local copies, waits for them, and re-layouts  2.79 us (3%)
    ppermute x15, starting transfers between devices, along(): lax.ppermute(a, axes, [(i, i ^ x) for i in range(Z)])  20.9 us
    ppermute x15, waiting for transfers between devices, along(): lax.ppermute(a, axes, [(i, i ^ x) for i in range(Z)])  12.4 us
    pallas_call x6, Pallas kernels, item_call(): pl.pallas_call(kernel, out_shape=[a for a, _ in outs], in_specs=specs(ins...  11 us
    ppermute x18, waiting for transfers between devices, swap(): return lax.ppermute(a, axis, [(0, 1), (1, 0)])  9.84 us
    ppermute x18, starting transfers between devices, swap(): return lax.ppermute(a, axis, [(0, 1), (1, 0)])  8.58 us
    ppermute x6, starting transfers between devices, to_task(): lax.ppermute(block, TASK_AXES, [(j, j ^ TASK_ORDER[i]) for j in range(Z)])  7.23 us
    ppermute x6, waiting for transfers between devices, to_task(): lax.ppermute(block, TASK_AXES, [(j, j ^ TASK_ORDER[i]) for j in range(Z)])  5.81 us
    pallas_call x2, Pallas kernels, middle_call(): pl.pallas_call(functools.partial(row_middle, shared), out_shape=[full] +...  4.01 us
  transfers between devices with their start and end apart: 41, of which 23 were waited for; matrix products, arithmetic and copies ran while one was open for 0% of the time, Pallas kernels for 13%

profile of v1, /device:TPU:0, one launch (start us, length us, event | category | flops | bytes accessed | tf_op | source)
XLA Modules:
  0.0 99.3 jit_solution(4851876183544702751)
XLA Ops:
  0.6 1.5 %share_pack.1 = (bf16[112,128]{1,0:T(8,128)(2,1)}, bf16[112,128]{1,0:T(8,128)(2,1)}, bf16[112,128]{1,0:T(8,128)(2,1)}, bf16[112,128]{1,0:T(8,128)(2,1)}) custom-call(bf16[48,192]{1,0:T(8,128)(2,1)} %refs_0_.1, bf16[24,192]{1,0:T(8,128)(2,1)} %refs_1_.1, bf16[1,48]{1,0:T(2,128)(2,1)} %bitcast.70, s32[1,64]{1,0:T(1,128)} %refs_3_.1, s32[1,64]{1,0:T(1,128)} %refs_4_.1, ...), custom_call_target="tpu_custom_call" | custom-call | tf_op jit(solution)/shard_map/share_pack/pallas_call | solution.py:962
  2.1 5.1 %collective-permute-start = (bf16[112,128]{1,0:T(8,128)(2,1)}, bf16[112,128]{1,0:T(8,128)(2,1)S(1)}, u32[]{:S(2)}, u32[]{:S(2)}) collective-permute-start(bf16[112,128]{1,0:T(8,128)(2,1)} %get-tuple-element.161), channel_id=1, source_target_pairs={{0,24},{8,16},{16,8},{24,0},{1,25},{9,17},{17,9},{25,1},{2,26},{10... | collective-permute-start | bytes 86024 | tf_op jit(solution)/shard_map/ppermute | solution.py:932
  7.9 0.9 copy-done
  8.8 0.9 copy-done.1
  10.6 1.7 %collective-permute-done.1 = bf16[112,128]{1,0:T(8,128)(2,1)S(1)} collective-permute-done((bf16[112,128]{1,0:T(8,128)(2,1)}, bf16[112,128]{1,0:T(8,128)(2,1)S(1)}, u32[]{:S(2)}, u32[]{:S(2)}) %collective-permute-start.1) | collective-permute-done | bytes 28704 | tf_op jit(solution)/shard_map/ppermute | solution.py:932
  12.3 1.6 %collective-permute-start.5 = (bf16[4,112,128]{2,1,0:T(8,128)(2,1)S(1)}, bf16[4,112,128]{2,1,0:T(8,128)(2,1)S(1)}, u32[]{:S(2)}, u32[]{:S(2)}) collective-permute-start(bf16[4,112,128]{2,1,0:T(8,128)(2,1)S(1)} %pad_maximum_fusion.1.refs_0_), channel_id=1, source_target_pairs={{0,1},{1,0},{4,5},{5,4},{2,3},{3,2},{6,7},{7,6},{8,9},{9,8},{12,13... | collective-permute-start | bytes 344072 | tf_op jit(solution)/shard_map/ppermute | solution.py:932
  13.8 1.5 %collective-permute-start.4 = (bf16[4,112,128]{2,1,0:T(8,128)(2,1)S(1)}, bf16[4,112,128]{2,1,0:T(8,128)(2,1)S(1)}, u32[]{:S(2)}, u32[]{:S(2)}) collective-permute-start(bf16[4,112,128]{2,1,0:T(8,128)(2,1)S(1)} %pad_maximum_fusion.1.refs_0_), channel_id=1, source_target_pairs={{0,4},{1,5},{4,0},{5,1},{2,6},{3,7},{6,2},{7,3},{8,12},{9,13},{12,... | collective-permute-start | bytes 344072 | tf_op jit(solution)/shard_map/ppermute | solution.py:932
  15.8 2.4 %collective-permute-done.5.refs_3_ = bf16[4,112,128]{2,1,0:T(8,128)(2,1)S(1)} collective-permute-done((bf16[4,112,128]{2,1,0:T(8,128)(2,1)S(1)}, bf16[4,112,128]{2,1,0:T(8,128)(2,1)S(1)}, u32[]{:S(2)}, u32[]{:S(2)}) %collective-permute-start.5) | collective-permute-done | bytes 114720 | tf_op jit(solution)/shard_map/ppermute | solution.py:932
  18.2 1.2 %collective-permute-done.4.refs_2_ = bf16[4,112,128]{2,1,0:T(8,128)(2,1)S(1)} collective-permute-done((bf16[4,112,128]{2,1,0:T(8,128)(2,1)S(1)}, bf16[4,112,128]{2,1,0:T(8,128)(2,1)S(1)}, u32[]{:S(2)}, u32[]{:S(2)}) %collective-permute-start.4) | collective-permute-done | bytes 114720 | tf_op jit(solution)/shard_map/ppermute | solution.py:932
  19.4 1.6 %collective-permute-done.3.refs_1_ = bf16[4,112,128]{2,1,0:T(8,128)(2,1)S(1)} collective-permute-done((bf16[4,112,128]{2,1,0:T(8,128)(2,1)S(1)}, bf16[4,112,128]{2,1,0:T(8,128)(2,1)S(1)}, u32[]{:S(2)}, u32[]{:S(2)}) %collective-permute-start.3) | collective-permute-done | bytes 114720 | tf_op jit(solution)/shard_map/ppermute | solution.py:932
  21.1 1.3 %collective-permute-done.7.refs_5_ = bf16[4,112,128]{2,1,0:T(8,128)(2,1)S(1)} collective-permute-done((bf16[4,112,128]{2,1,0:T(8,128)(2,1)S(1)}, bf16[4,112,128]{2,1,0:T(8,128)(2,1)S(1)}, u32[]{:S(2)}, u32[]{:S(2)}) %collective-permute-start.7) | collective-permute-done | bytes 114720 | tf_op jit(solution)/shard_map/ppermute | solution.py:922
  22.8 1.9 %feat_forward.1 = (f32[384,192]{1,0:T(8,128)S(1)}, f32[384,192]{1,0:T(8,128)S(1)}, bf16[3,384,192]{2,1,0:T(8,128)(2,1)S(1)}, bf16[384,192]{1,0:T(8,128)(2,1)S(1)...) custom-call(bf16[384,192]{1,0:T(8,128)(2,1)S(1)} %get-tuple-element., ...), custom_call_target="tpu_custom_call" | custom-call | tf_op jit(solution)/shard_map/feat_forward/pallas_call | solution.py:1078
  24.8 1.1 %collective-permute-start.11 = (bf16[96,384]{1,0:T(8,128)(2,1)S(1)}, bf16[96,384]{1,0:T(8,128)(2,1)S(1)}, u32[]{:S(2)}, u32[]{:S(2)}) collective-permute-start(bf16[96,384]{1,0:T(8,128)(2,1)S(1)} %get-tuple-element.174), channel_id=1, source_target_pairs={{0,4},{4,0},{8,12},{12,8},{1,5},{5,1},{9,13},{13,9},{2,6},{6,2},{1... | collective-permute-start | bytes 221192 | tf_op jit(solution)/shard_map/ppermute | solution.py:1202
  25.9 2.4 %collective-permute-start.12 = (bf16[96,384]{1,0:T(8,128)(2,1)S(1)}, bf16[96,384]{1,0:T(8,128)(2,1)S(1)}, u32[]{:S(2)}, u32[]{:S(2)}) collective-permute-start(bf16[96,384]{1,0:T(8,128)(2,1)S(1)} %get-tuple-element.175), channel_id=1, source_target_pairs={{0,12},{4,8},{8,4},{12,0},{1,13},{5,9},{9,5},{13,1},{2,14},{6,10},... | collective-permute-start | bytes 221192 | tf_op jit(solution)/shard_map/ppermute | solution.py:1202
  28.3 2.2 %collective-permute-done.10 = bf16[128,384]{1,0:T(8,128)(2,1)S(1)} collective-permute-done((bf16[128,384]{1,0:T(8,128)(2,1)S(1)}, bf16[128,384]{1,0:T(8,128)(2,1)S(1)}, u32[]{:S(2)}, u32[]{:S(2)}) %collective-permute-start.10) | collective-permute-done | bytes 98336 | tf_op jit(solution)/shard_map/ppermute | solution.py:1202
  30.5 1.9 %collective-permute-start.15 = (bf16[128,384]{1,0:T(8,128)(2,1)S(1)}, bf16[128,384]{1,0:T(8,128)(2,1)S(1)}, u32[]{:S(2)}, u32[]{:S(2)}) collective-permute-start(bf16[128,384]{1,0:T(8,128)(2,1)S(1)} %pad_maximum_fusion.2.refs_0_), channel_id=1, source_target_pairs={{0,16},{16,0},{1,17},{17,1},{2,18},{18,2},{3,19},{19,3},{4,20},{20... | collective-permute-start | bytes 294920 | tf_op jit(solution)/shard_map/ppermute | solution.py:922
  33.8 1.3 %collective-permute-start.17 = (bf16[128,384]{1,0:T(8,128)(2,1)S(1)}, bf16[128,384]{1,0:T(8,128)(2,1)S(1)}, u32[]{:S(2)}, u32[]{:S(2)}) collective-permute-start(bf16[128,384]{1,0:T(8,128)(2,1)S(1)} %pad_maximum_fusion.3.refs_1_), channel_id=1, source_target_pairs={{0,16},{16,0},{1,17},{17,1},{2,18},{18,2},{3,19},{19,3},{4,20},{20... | collective-permute-start | bytes 294920 | tf_op jit(solution)/shard_map/ppermute | solution.py:922
  35.1 1.9 %item_forward.3 = (bf16[9,512,256]{2,1,0:T(8,128)(2,1)S(1)}, f32[16,256]{1,0:T(8,128)S(1)}, bf16[3,256,128]{2,1,0:T(8,128)(2,1)S(1)}, f32[16,256]{1,0:T(8,128)S(1)}, f32[384,256]{1,0:T(8,128)S(1)}) custom-call(bf16[128,384]{1,0:T(8,128)(2,1)S(1)} %pad_maximum_fusion.2.refs_0_, bf16[128,384]{1,0:T(8,128)(2,1)S(1)} %pad_maximum_fusion.3.refs_1_, ...), custom_call_target="tpu_custom_call" | custom-call | flops 100000000 | tf_op jit(solution)/shard_map/item_forward/pallas_call | solution.py:1116
  37.3 1.1 %collective-permute-done.16.refs_1_.refs_5_ = bf16[128,384]{1,0:T(8,128)(2,1)S(1)} collective-permute-done((bf16[128,384]{1,0:T(8,128)(2,1)S(1)}, bf16[128,384]{1,0:T(8,128)(2,1)S(1)}, u32[]{:S(2)}, u32[]{:S(2)}) %collective-permute-start.16) | collective-permute-done | bytes 98336 | tf_op jit(solution)/shard_map/ppermute | solution.py:922
  38.4 1.1 %item_forward.4 = (bf16[9,256,256]{2,1,0:T(8,128)(2,1)S(1)}, f32[16,256]{1,0:T(8,128)S(1)}, f32[16,256]{1,0:T(8,128)S(1)}, f32[16,256]{1,0:T(8,128)S(1)}, f32[384,256]{1,0:T(8,128)S(1)}) custom-call(bf16[128,384]{1,0:T(8,128)(2,1)S(1)} %collective-permute-done.15.refs_0_.refs_4_, bf16[128,384]{1,0:T(8,128)(2,1)S(1)} %collective-permute-done.16.refs_1_.refs_5_, ...), custom_call_target="tpu_custom_call" | custom-call | flops 100000000 | tf_op jit(solution)/shard_map/item_forward/pallas_call | solution.py:1116
  39.4 2.0 %collective-permute-done.17.refs_0_.refs_6_ = bf16[128,384]{1,0:T(8,128)(2,1)S(1)} collective-permute-done((bf16[128,384]{1,0:T(8,128)(2,1)S(1)}, bf16[128,384]{1,0:T(8,128)(2,1)S(1)}, u32[]{:S(2)}, u32[]{:S(2)}) %collective-permute-start.17) | collective-permute-done | bytes 98336 | tf_op jit(solution)/shard_map/ppermute | solution.py:922
  41.4 1.3 %collective-permute-done.18.refs_1_.refs_7_ = bf16[128,384]{1,0:T(8,128)(2,1)S(1)} collective-permute-done((bf16[128,384]{1,0:T(8,128)(2,1)S(1)}, bf16[128,384]{1,0:T(8,128)(2,1)S(1)}, u32[]{:S(2)}, u32[]{:S(2)}) %collective-permute-start.18) | collective-permute-done | bytes 98336 | tf_op jit(solution)/shard_map/ppermute | solution.py:922
  42.7 1.1 %item_forward.5 = (bf16[9,256,256]{2,1,0:T(8,128)(2,1)S(1)}, f32[16,256]{1,0:T(8,128)S(1)}, f32[16,256]{1,0:T(8,128)S(1)}, f32[16,256]{1,0:T(8,128)S(1)}, f32[38...) custom-call(bf16[128,384]{1,0:T(8,128)(2,1)S(1)} %collective-permute, ...), custom_call_target="tpu_custom_call" | custom-call | flops 100000000 | tf_op jit(solution)/shard_map/item_forward/pallas_call | solution.py:1116
  44.6 1.6 %row_middle.2 = (f32[256,192]{1,0:T(8,128)S(1)}, bf16[256,192]{1,0:T(8,128)(2,1)S(1)}, bf16[256,192]{1,0:T(8,128)(2,1)S(1)}, bf16[256,192]{1,0:T(8,128)(2,1)S(1)...) custom-call(bf16[192,192]{1,0:T(8,128)(2,1)S(1)} %slice.142.w_ref, ...), custom_call_target="tpu_custom_call" | custom-call | tf_op jit(solution)/shard_map/row_middle/pallas_call | solution.py:1246
  46.2 1.7 %collective-permute-done.19.refs_4_ = bf16[128,96]{1,0:T(8,128)(2,1)S(1)} collective-permute-done((bf16[128,96]{1,0:T(8,128)(2,1)S(1)}, bf16[128,96]{1,0:T(8,128)(2,1)S(1)}, u32[]{:S(2)}, u32[]{:S(2)}) %collective-permute-start.19) | collective-permute-done | bytes 24608 | tf_op jit(solution)/shard_map/ppermute | solution.py:1235
  47.8 2.4 %row_middle.3 = (f32[128,192]{1,0:T(8,128)S(1)}, bf16[128,192]{1,0:T(8,128)(2,1)S(1)}, bf16[128,192]{1,0:T(8,128)(2,1)S(1)}, bf16[128,192]{1,0:T(8,128)(2,1)S(1)...) custom-call(bf16[192,192]{1,0:T(8,128)(2,1)S(1)} %slice.142.w_ref, ...), custom_call_target="tpu_custom_call" | custom-call | tf_op jit(solution)/shard_map/row_middle/pallas_call | solution.py:1246
  50.9 1.2 %item_turn.1 = (bf16[3,128,256]{2,1,0:T(8,128)(2,1)S(1)}, bf16[384,512]{1,0:T(8,128)(2,1)S(1)}, bf16[3,512,128]{2,1,0:T(8,128)(2,1)S(1)}, bf16[3,128,512]{2,1,0:...) custom-call(bf16[128,384]{1,0:T(8,128)(2,1)S(1)} %pad_maximum_fusion, ...), custom_call_target="tpu_custom_call" | custom-call | flops 100000000 | tf_op jit(solution)/shard_map/item_turn/pallas_call | solution.py:1116
  52.9 1.3 %collective-permute-done.20.refs_12_ = bf16[128,96]{1,0:T(8,128)(2,1)S(1)} collective-permute-done((bf16[128,96]{1,0:T(8,128)(2,1)S(1)}, bf16[128,96]{1,0:T(8,128)(2,1)S(1)}, u32[]{:S(2)}, u32[]{:S(2)}) %collective-permute-start.20) | collective-permute-done | bytes 24608 | tf_op jit(solution)/shard_map/ppermute | solution.py:1235
  54.2 2.4 %item_backward.2 = (f32[128,384]{1,0:T(8,128)S(1)}, bf16[128,384]{1,0:T(8,128)(2,1)S(1)}, f32[128,384]{1,0:T(8,128)S(1)}, bf16[128,384]{1,0:T(8,128)(2,1)S(1)}, ...) custom-call(bf16[384,256]{1,0:T(8,128)(2,1)S(1)} %get-tuple-element.197.refs_0_, ...), custom_call_target="tpu_custom_call" | custom-call | flops 100000000 | tf_op jit(solution)/shard_map/item_backward/pallas_call | solution.py:1116
  58.6 2.9 %collective-permute-start.24 = (bf16[128,384]{1,0:T(8,128)(2,1)S(1)}, bf16[128,384]{1,0:T(8,128)(2,1)S(1)}, u32[]{:S(2)}, u32[]{:S(2)}) collective-permute-start(bf16[128,384]{1,0:T(8,128)(2,1)S(1)} %get-tuple-element.258), channel_id=1, source_target_pairs={{0,16},{16,0},{1,17},{17,1},{2,18},{18,2},{3,19},{19,3},{4,20},{20... | collective-permute-start | bytes 294920 | tf_op jit(solution)/shard_map/ppermute | solution.py:922
  61.5 3.3 %item_backward.3 = (f32[128,384]{1,0:T(8,128)S(1)}, f32[128,384]{1,0:T(8,128)S(1)}, bf16[128,384]{1,0:T(8,128)(2,1)S(1)}, bf16[128,384]{1,0:T(8,128)(2,1)S(1)}, f32[576,192]{1,0:T(8,128)S(1)}) custom-call(bf16[384,512]{1,0:T(8,128)(2,1)S(1)} %get-tuple-element.259.refs_0_, bf16[3,512,128]{2,1,0:T(8,128)(2,1)S(1)} %get-tuple-element.260.refs_1_, ...), custom_call_target="tpu_custom_call" | custom-call | flops 100000000 | tf_op jit(solution)/shard_map/item_backward/pallas_call | solution.py:1116
  65.9 2.5 %collective-permute-start.26 = (bf16[4,40,128]{2,1,0:T(8,128)(2,1)S(1)}, bf16[4,40,128]{2,1,0:T(8,128)(2,1)S(1)}, u32[]{:S(2)}, u32[]{:S(2)}) collective-permute-start(bf16[4,40,128]{2,1,0:T(8,128)(2,1)S(1)} %get-tuple-element.320), channel_id=1, source_target_pairs={{0,5},{1,4},{4,1},{5,0},{2,7},{3,6},{6,3},{7,2},{8,13},{9,12},{12,... | collective-permute-start | bytes 122888 | tf_op jit(solution)/shard_map/ppermute | solution.py:932
  68.5 1.5 %collective-permute-done.24 = bf16[128,384]{1,0:T(8,128)(2,1)S(1)} collective-permute-done((bf16[128,384]{1,0:T(8,128)(2,1)S(1)}, bf16[128,384]{1,0:T(8,128)(2,1)S(1)}, u32[]{:S(2)}, u32[]{:S(2)}) %collective-permute-start.24) | collective-permute-done | bytes 98336 | tf_op jit(solution)/shard_map/ppermute | solution.py:922
  70.0 0.9 collective-permute-done.26
  72.9 1.1 %collective-permute-start.32 = (bf16[96,384]{1,0:T(8,128)(2,1)S(1)}, bf16[96,384]{1,0:T(8,128)(2,1)S(1)}, u32[]{:S(2)}, u32[]{:S(2)}) collective-permute-start(bf16[96,384]{1,0:T(8,128)(2,1)S(1)} %pad_maximum_fusion.5), channel_id=1, source_target_pairs={{0,4},{4,0},{8,12},{12,8},{1,5},{5,1},{9,13},{13,9},{2,6},{6,2},{1... | collective-permute-start | bytes 221192 | tf_op jit(solution)/shard_map/ppermute | solution.py:1202
  74.0 2.0 %collective-permute-start.33 = (bf16[96,384]{1,0:T(8,128)(2,1)S(1)}, bf16[96,384]{1,0:T(8,128)(2,1)S(1)}, u32[]{:S(2)}, u32[]{:S(2)}) collective-permute-start(bf16[96,384]{1,0:T(8,128)(2,1)S(1)} %pad_maximum_fusion.6), channel_id=1, source_target_pairs={{0,12},{4,8},{8,4},{12,0},{1,13},{5,9},{9,5},{13,1},{2,14},{6,10},... | collective-permute-start | bytes 221192 | tf_op jit(solution)/shard_map/ppermute | solution.py:1202
  76.0 1.3 %collective-permute-done.32 = bf16[96,384]{1,0:T(8,128)(2,1)S(1)} collective-permute-done((bf16[96,384]{1,0:T(8,128)(2,1)S(1)}, bf16[96,384]{1,0:T(8,128)(2,1)S(1)}, u32[]{:S(2)}, u32[]{:S(2)}) %collective-permute-start.32) | collective-permute-done | bytes 73760 | tf_op jit(solution)/shard_map/ppermute | solution.py:1202
  77.3 2.3 %collective-permute-done.33 = bf16[96,384]{1,0:T(8,128)(2,1)S(1)} collective-permute-done((bf16[96,384]{1,0:T(8,128)(2,1)S(1)}, bf16[96,384]{1,0:T(8,128)(2,1)S(1)}, u32[]{:S(2)}, u32[]{:S(2)}) %collective-permute-start.33) | collective-permute-done | bytes 73760 | tf_op jit(solution)/shard_map/ppermute | solution.py:1202
  79.7 2.2 %feat_backward.1 = (f32[768,192]{1,0:T(8,128)S(1)}, f32[8,192]{1,0:T(8,128)S(1)}, f32[384,192]{1,0:T(8,128)S(1)}, bf16[3,384,192]{2,1,0:T(8,128)(2,1)S(1)}) custom-call(f32[384,192]{1,0:T(8,128)S(1)} %get-tuple-element.288.xhat1_ref, f32[384,192]{1,0:T(8,128)S(1)} %get-tuple-element.289.rstd1_ref, bf16[384,192]{1,0:T(8,128)(2,1)S(1)} %get-tuple-element.166.cells_ref, ...), custom_call_target="tpu_custom_call" | custom-call | tf_op jit(solution)/shard_map/feat_backward/pallas_call | solution.py:1346
  82.2 1.6 %collective-permute-done.34 = bf16[4,4,80,128]{3,2,1,0:T(8,128)(2,1)S(1)} collective-permute-done((bf16[4,4,80,128]{3,2,1,0:T(8,128)(2,1)S(1)}, bf16[4,4,80,128]{3,2,1,0:T(8,128)(2,1)S(1)}, u32[]{:S(2)}, u32[]{:S(2)}) %collective-permute-start.34) | collective-permute-done | bytes 327712 | tf_op jit(solution)/shard_map/ppermute | solution.py:922
  84.0 1.7 %collective-permute-start.35 = (bf16[4,80,128]{2,1,0:T(8,128)(2,1)S(1)}, bf16[4,80,128]{2,1,0:T(8,128)(2,1)S(1)}, u32[]{:S(2)}, u32[]{:S(2)}) collective-permute-start(bf16[4,80,128]{2,1,0:T(8,128)(2,1)S(1)} %get-tuple-element.313), channel_id=1, source_target_pairs={{0,5},{1,4},{4,1},{5,0},{2,7},{3,6},{6,3},{7,2},{8,13},{9,12},{12,... | collective-permute-start | bytes 245768 | tf_op jit(solution)/shard_map/ppermute | solution.py:932
  86.1 1.4 %collective-permute-start.36 = (bf16[4,80,128]{2,1,0:T(8,128)(2,1)S(1)}, bf16[4,80,128]{2,1,0:T(8,128)(2,1)S(1)}, u32[]{:S(2)}, u32[]{:S(2)}) collective-permute-start(bf16[4,80,128]{2,1,0:T(8,128)(2,1)S(1)} %get-tuple-element.315), channel_id=1, source_target_pairs={{0,4},{1,5},{4,0},{5,1},{2,6},{3,7},{6,2},{7,3},{8,12},{9,13},{12,... | collective-permute-start | bytes 245768 | tf_op jit(solution)/shard_map/ppermute | solution.py:932
  87.5 2.4 %collective-permute-done.35 = bf16[4,80,128]{2,1,0:T(8,128)(2,1)S(1)} collective-permute-done((bf16[4,80,128]{2,1,0:T(8,128)(2,1)S(1)}, bf16[4,80,128]{2,1,0:T(8,128)(2,1)S(1)}, u32[]{:S(2)}, u32[]{:S(2)}) %collective-permute-start.35) | collective-permute-done | bytes 81952 | tf_op jit(solution)/shard_map/ppermute | solution.py:932
  91.3 2.2 %collective-permute-start.38 = (bf16[120,128]{1,0:T(8,128)(2,1)S(1)}, bf16[120,128]{1,0:T(8,128)(2,1)S(1)}, u32[]{:S(2)}, u32[]{:S(2)}) collective-permute-start(bf16[120,128]{1,0:T(8,128)(2,1)S(1)} %get-tuple-element.307), channel_id=1, source_target_pairs={{0,24},{8,16},{16,8},{24,0},{1,25},{9,17},{17,9},{25,1},{2,26},{10... | collective-permute-start | bytes 92168 | tf_op jit(solution)/shard_map/ppermute | solution.py:932
  93.5 0.9 collective-permute-start.39
  94.4 1.3 %collective-permute-start.40 = (bf16[120,128]{1,0:T(8,128)(2,1)S(1)}, bf16[120,128]{1,0:T(8,128)(2,1)S(1)}, u32[]{:S(2)}, u32[]{:S(2)}) collective-permute-start(bf16[120,128]{1,0:T(8,128)(2,1)S(1)} %get-tuple-element.309), channel_id=1, source_target_pairs={{0,8},{8,0},{16,24},{24,16},{1,9},{9,1},{17,25},{25,17},{2,10},{10... | collective-permute-start | bytes 92168 | tf_op jit(solution)/shard_map/ppermute | solution.py:932
  96.5 1.1 %cell_out.1 = f32[384,192]{1,0:T(8,128)} custom-call(f32[384,192]{1,0:T(8,128)S(1)} %get-tuple-element.304.dz1_ref, bf16[3,384,192]{2,1,0:T(8,128)(2,1)S(1)} %get-tuple-element.305.dqkv_ref, bf16[576,192]{1,0:T(8,128)(2,1)S(1)} %get-tuple-element.316.w_ref), custom_call_target="tpu_custom_call" | custom-call | tf_op jit(solution)/shard_map/cell_out/pallas_call | solution.py:1369
  97.6 1.0 collective-permute-done.39.refs_1_
  (96 shorter events, 15.3 us)
Async XLA Ops:
  2.1 8.4 %collective-permute-start = (bf16[112,128]{1,0:T(8,128)(2,1)}, bf16[112,128]{1,0:T(8,128)(2,1)S(1)}, u32[]{:S(2)}, u32[]{:S(2)}) collective-permute-start(bf16[112,128]{1,0:T(8,128)(2,1)} %get-tuple-element.161), channel_id=1, source_target_pairs={{0,24},{8,16},{16,8},{24,0},{1,25},{9,17},{17,9},{25,1},{2,26},{10... | collective-permute-start | bytes 86024 | tf_op jit(solution)/shard_map/ppermute | solution.py:932
  7.3 5.0 %collective-permute-start.1 = (bf16[112,128]{1,0:T(8,128)(2,1)}, bf16[112,128]{1,0:T(8,128)(2,1)S(1)}, u32[]{:S(2)}, u32[]{:S(2)}) collective-permute-start(bf16[112,128]{1,0:T(8,128)(2,1)} %get-tuple-element.162), channel_id=1, source_target_pairs={{0,16},{8,24},{16,0},{24,8},{1,17},{9,25},{17,1},{25,9},{2,18},{10... | collective-permute-start | bytes 86024 | tf_op jit(solution)/shard_map/ppermute | solution.py:932
  7.3 5.0 %collective-permute-start.2 = (bf16[112,128]{1,0:T(8,128)(2,1)}, bf16[112,128]{1,0:T(8,128)(2,1)S(1)}, u32[]{:S(2)}, u32[]{:S(2)}) collective-permute-start(bf16[112,128]{1,0:T(8,128)(2,1)} %get-tuple-element.163), channel_id=1, source_target_pairs={{0,8},{8,0},{16,24},{24,16},{1,9},{9,1},{17,25},{25,17},{2,10},{10... | collective-permute-start | bytes 86024 | tf_op jit(solution)/shard_map/ppermute | solution.py:932
  7.9 0.9 copy-start
  8.8 0.9 copy-start.1
  9.8 0.7 copy-start.2
  12.3 5.9 %collective-permute-start.5 = (bf16[4,112,128]{2,1,0:T(8,128)(2,1)S(1)}, bf16[4,112,128]{2,1,0:T(8,128)(2,1)S(1)}, u32[]{:S(2)}, u32[]{:S(2)}) collective-permute-start(bf16[4,112,128]{2,1,0:T(8,128)(2,1)S(1)} %pad_maximum_fusion.1.refs_0_), channel_id=1, source_target_pairs={{0,1},{1,0},{4,5},{5,4},{2,3},{3,2},{6,7},{7,6},{8,9},{9,8},{12,13... | collective-permute-start | bytes 344072 | tf_op jit(solution)/shard_map/ppermute | solution.py:932
  13.8 5.6 %collective-permute-start.4 = (bf16[4,112,128]{2,1,0:T(8,128)(2,1)S(1)}, bf16[4,112,128]{2,1,0:T(8,128)(2,1)S(1)}, u32[]{:S(2)}, u32[]{:S(2)}) collective-permute-start(bf16[4,112,128]{2,1,0:T(8,128)(2,1)S(1)} %pad_maximum_fusion.1.refs_0_), channel_id=1, source_target_pairs={{0,4},{1,5},{4,0},{5,1},{2,6},{3,7},{6,2},{7,3},{8,12},{9,13},{12,... | collective-permute-start | bytes 344072 | tf_op jit(solution)/shard_map/ppermute | solution.py:932
  15.3 5.7 %collective-permute-start.3 = (bf16[4,112,128]{2,1,0:T(8,128)(2,1)S(1)}, bf16[4,112,128]{2,1,0:T(8,128)(2,1)S(1)}, u32[]{:S(2)}, u32[]{:S(2)}) collective-permute-start(bf16[4,112,128]{2,1,0:T(8,128)(2,1)S(1)} %pad_maximum_fusion.1.refs_0_), channel_id=1, source_target_pairs={{0,5},{1,4},{4,1},{5,0},{2,7},{3,6},{6,3},{7,2},{8,13},{9,12},{12,... | collective-permute-start | bytes 344072 | tf_op jit(solution)/shard_map/ppermute | solution.py:932
  15.8 5.2 %collective-permute-start.6 = (bf16[4,112,128]{2,1,0:T(8,128)(2,1)S(1)}, bf16[4,112,128]{2,1,0:T(8,128)(2,1)S(1)}, u32[]{:S(2)}, u32[]{:S(2)}) collective-permute-start(bf16[4,112,128]{2,1,0:T(8,128)(2,1)S(1)} %pad_maximum_fusion.1.refs_0_), channel_id=1, source_target_pairs={{0,2},{2,0},{1,3},{3,1},{4,6},{6,4},{5,7},{7,5},{8,10},{10,8},{9,1... | collective-permute-start | bytes 344072 | tf_op jit(solution)/shard_map/ppermute | solution.py:922
  18.2 2.9 %collective-permute-start.9 = (bf16[4,112,128]{2,1,0:T(8,128)(2,1)S(1)}, bf16[4,112,128]{2,1,0:T(8,128)(2,1)S(1)}, u32[]{:S(2)}, u32[]{:S(2)}) collective-permute-start(bf16[4,112,128]{2,1,0:T(8,128)(2,1)S(1)} %collective-permute-done.5.refs_3_), channel_id=1, source_target_pairs={{0,2},{2,0},{1,3},{3,1},{4,6},{6,4},{5,7},{7,5},{8,10},{10,8},{9,1... | collective-permute-start | bytes 344072 | tf_op jit(solution)/shard_map/ppermute | solution.py:922
  19.4 1.6 %collective-permute-start.8 = (bf16[4,112,128]{2,1,0:T(8,128)(2,1)S(1)}, bf16[4,112,128]{2,1,0:T(8,128)(2,1)S(1)}, u32[]{:S(2)}, u32[]{:S(2)}) collective-permute-start(bf16[4,112,128]{2,1,0:T(8,128)(2,1)S(1)} %collective-permute-done.4.refs_2_), channel_id=1, source_target_pairs={{0,2},{2,0},{1,3},{3,1},{4,6},{6,4},{5,7},{7,5},{8,10},{10,8},{9,1... | collective-permute-start | bytes 344072 | tf_op jit(solution)/shard_map/ppermute | solution.py:922
  21.0 1.3 %collective-permute-start.7 = (bf16[4,112,128]{2,1,0:T(8,128)(2,1)S(1)}, bf16[4,112,128]{2,1,0:T(8,128)(2,1)S(1)}, u32[]{:S(2)}, u32[]{:S(2)}) collective-permute-start(bf16[4,112,128]{2,1,0:T(8,128)(2,1)S(1)} %collective-permute-done.3.refs_1_), channel_id=1, source_target_pairs={{0,2},{2,0},{1,3},{3,1},{4,6},{6,4},{5,7},{7,5},{8,10},{10,8},{9,1... | collective-permute-start | bytes 344072 | tf_op jit(solution)/shard_map/ppermute | solution.py:922
  24.7 5.7 %collective-permute-start.10 = (bf16[128,384]{1,0:T(8,128)(2,1)S(1)}, bf16[128,384]{1,0:T(8,128)(2,1)S(1)}, u32[]{:S(2)}, u32[]{:S(2)}) collective-permute-start(bf16[128,384]{1,0:T(8,128)(2,1)S(1)} %get-tuple-element.173), channel_id=1, source_target_pairs={{0,8},{4,12},{8,0},{12,4},{1,9},{5,13},{9,1},{13,5},{2,10},{6,14},... | collective-permute-start | bytes 294920 | tf_op jit(solution)/shard_map/ppermute | solution.py:1202
  24.8 7.6 %collective-permute-start.11 = (bf16[96,384]{1,0:T(8,128)(2,1)S(1)}, bf16[96,384]{1,0:T(8,128)(2,1)S(1)}, u32[]{:S(2)}, u32[]{:S(2)}) collective-permute-start(bf16[96,384]{1,0:T(8,128)(2,1)S(1)} %get-tuple-element.174), channel_id=1, source_target_pairs={{0,4},{4,0},{8,12},{12,8},{1,5},{5,1},{9,13},{13,9},{2,6},{6,2},{1... | collective-permute-start | bytes 221192 | tf_op jit(solution)/shard_map/ppermute | solution.py:1202
  25.9 6.5 %collective-permute-start.12 = (bf16[96,384]{1,0:T(8,128)(2,1)S(1)}, bf16[96,384]{1,0:T(8,128)(2,1)S(1)}, u32[]{:S(2)}, u32[]{:S(2)}) collective-permute-start(bf16[96,384]{1,0:T(8,128)(2,1)S(1)} %get-tuple-element.175), channel_id=1, source_target_pairs={{0,12},{4,8},{8,4},{12,0},{1,13},{5,9},{9,5},{13,1},{2,14},{6,10},... | collective-permute-start | bytes 221192 | tf_op jit(solution)/shard_map/ppermute | solution.py:1202
  30.5 6.6 %collective-permute-start.15 = (bf16[128,384]{1,0:T(8,128)(2,1)S(1)}, bf16[128,384]{1,0:T(8,128)(2,1)S(1)}, u32[]{:S(2)}, u32[]{:S(2)}) collective-permute-start(bf16[128,384]{1,0:T(8,128)(2,1)S(1)} %pad_maximum_fusion.2.refs_0_), channel_id=1, source_target_pairs={{0,16},{16,0},{1,17},{17,1},{2,18},{18,2},{3,19},{19,3},{4,20},{20... | collective-permute-start | bytes 294920 | tf_op jit(solution)/shard_map/ppermute | solution.py:922
  32.4 2.7 %collective-permute-start.13 = (bf16[128,384]{1,0:T(8,128)(2,1)S(1)}, bf16[128,384]{1,0:T(8,128)(2,1)S(1)}, u32[]{:S(2)}, u32[]{:S(2)}) collective-permute-start(bf16[128,384]{1,0:T(8,128)(2,1)S(1)} %pad_maximum_fusion.2.refs_0_), channel_id=1, source_target_pairs={{0,2},{2,0},{1,3},{3,1},{4,6},{6,4},{5,7},{7,5},{8,10},{10,8},{9,1... | collective-permute-start | bytes 294920 | tf_op jit(solution)/shard_map/ppermute | solution.py:922
  32.4 2.6 %collective-permute-start.14 = (bf16[128,384]{1,0:T(8,128)(2,1)S(1)}, bf16[128,384]{1,0:T(8,128)(2,1)S(1)}, u32[]{:S(2)}, u32[]{:S(2)}) collective-permute-start(bf16[128,384]{1,0:T(8,128)(2,1)S(1)} %pad_maximum_fusion.3.refs_1_), channel_id=1, source_target_pairs={{0,2},{2,0},{1,3},{3,1},{4,6},{6,4},{5,7},{7,5},{8,10},{10,8},{9,1... | collective-permute-start | bytes 294920 | tf_op jit(solution)/shard_map/ppermute | solution.py:922
  33.8 7.6 %collective-permute-start.17 = (bf16[128,384]{1,0:T(8,128)(2,1)S(1)}, bf16[128,384]{1,0:T(8,128)(2,1)S(1)}, u32[]{:S(2)}, u32[]{:S(2)}) collective-permute-start(bf16[128,384]{1,0:T(8,128)(2,1)S(1)} %pad_maximum_fusion.3.refs_1_), channel_id=1, source_target_pairs={{0,16},{16,0},{1,17},{17,1},{2,18},{18,2},{3,19},{19,3},{4,20},{20... | collective-permute-start | bytes 294920 | tf_op jit(solution)/shard_map/ppermute | solution.py:922
  37.0 1.3 %collective-permute-start.16 = (bf16[128,384]{1,0:T(8,128)(2,1)S(1)}, bf16[128,384]{1,0:T(8,128)(2,1)S(1)}, u32[]{:S(2)}, u32[]{:S(2)}) collective-permute-start(bf16[128,384]{1,0:T(8,128)(2,1)S(1)} %collective-permute-done.15.refs_0_.refs_4_), channel_id=1, source_target_pairs={{0,2},{2,0},{1,3},{3,1},{4,6},{6,4},{5,7},{7,5},{8,10},{10,8},{9,1... | collective-permute-start | bytes 294920 | tf_op jit(solution)/shard_map/ppermute | solution.py:922
  41.4 1.3 %collective-permute-start.18 = (bf16[128,384]{1,0:T(8,128)(2,1)S(1)}, bf16[128,384]{1,0:T(8,128)(2,1)S(1)}, u32[]{:S(2)}, u32[]{:S(2)}) collective-permute-start(bf16[128,384]{1,0:T(8,128)(2,1)S(1)} %collective-permute-done.17.refs_0_.refs_6_), channel_id=1, source_target_pairs={{0,2},{2,0},{1,3},{3,1},{4,6},{6,4},{5,7},{7,5},{8,10},{10,8},{9,1... | collective-permute-start | bytes 294920 | tf_op jit(solution)/shard_map/ppermute | solution.py:922
  43.9 4.0 %collective-permute-start.19 = (bf16[128,96]{1,0:T(8,128)(2,1)S(1)}, bf16[128,96]{1,0:T(8,128)(2,1)S(1)}, u32[]{:S(2)}, u32[]{:S(2)}) collective-permute-start(bf16[128,96]{1,0:T(8,128)(2,1)S(1)} %get-tuple-element.195), channel_id=1, source_target_pairs={{0,4},{4,0},{1,5},{5,1},{2,6},{6,2},{3,7},{7,3},{8,12},{12,8},{9,1... | collective-permute-start | bytes 73736 | tf_op jit(solution)/shard_map/ppermute | solution.py:1235
  50.3 4.0 %collective-permute-start.20 = (bf16[128,96]{1,0:T(8,128)(2,1)S(1)}, bf16[128,96]{1,0:T(8,128)(2,1)S(1)}, u32[]{:S(2)}, u32[]{:S(2)}) collective-permute-start(bf16[128,96]{1,0:T(8,128)(2,1)S(1)} %get-tuple-element.215), channel_id=1, source_target_pairs={{0,4},{4,0},{1,5},{5,1},{2,6},{6,2},{3,7},{7,3},{8,12},{12,8},{9,1... | collective-permute-start | bytes 73736 | tf_op jit(solution)/shard_map/ppermute | solution.py:1235
  56.6 1.4 %collective-permute-start.21 = (bf16[128,384]{1,0:T(8,128)(2,1)S(1)}, bf16[128,384]{1,0:T(8,128)(2,1)S(1)}, u32[]{:S(2)}, u32[]{:S(2)}) collective-permute-start(bf16[128,384]{1,0:T(8,128)(2,1)S(1)} %get-tuple-element.247), channel_id=1, source_target_pairs={{0,2},{2,0},{1,3},{3,1},{4,6},{6,4},{5,7},{7,5},{8,10},{10,8},{9,1... | collective-permute-start | bytes 294920 | tf_op jit(solution)/shard_map/ppermute | solution.py:922
  56.7 1.4 %collective-permute-start.22 = (bf16[128,384]{1,0:T(8,128)(2,1)S(1)}, bf16[128,384]{1,0:T(8,128)(2,1)S(1)}, u32[]{:S(2)}, u32[]{:S(2)}) collective-permute-start(bf16[128,384]{1,0:T(8,128)(2,1)S(1)} %get-tuple-element.248), channel_id=1, source_target_pairs={{0,2},{2,0},{1,3},{3,1},{4,6},{6,4},{5,7},{7,5},{8,10},{10,8},{9,1... | collective-permute-start | bytes 294920 | tf_op jit(solution)/shard_map/ppermute | solution.py:922
  58.2 6.6 %collective-permute-start.25 = (bf16[4,4,40,128]{3,2,1,0:T(8,128)(2,1)S(1)}, bf16[4,4,40,128]{3,2,1,0:T(8,128)(2,1)S(1)}, u32[]{:S(2)}, u32[]{:S(2)}) collective-permute-start(bf16[4,4,40,128]{3,2,1,0:T(8,128)(2,1)S(1)} %get-tuple-element.275), channel_id=1, source_target_pairs={{0,2},{2,0},{1,3},{3,1},{4,6},{6,4},{5,7},{7,5},{8,10},{10,8},{9,1... | collective-permute-start | bytes 491528 | tf_op jit(solution)/shard_map/ppermute | solution.py:922
  58.6 9.8 %collective-permute-start.23 = (bf16[128,384]{1,0:T(8,128)(2,1)S(1)}, bf16[128,384]{1,0:T(8,128)(2,1)S(1)}, u32[]{:S(2)}, u32[]{:S(2)}) collective-permute-start(bf16[128,384]{1,0:T(8,128)(2,1)S(1)} %get-tuple-element.257), channel_id=1, source_target_pairs={{0,16},{16,0},{1,17},{17,1},{2,18},{18,2},{3,19},{19,3},{4,20},{20... | collective-permute-start | bytes 294920 | tf_op jit(solution)/shard_map/ppermute | solution.py:922
  58.6 11.4 %collective-permute-start.24 = (bf16[128,384]{1,0:T(8,128)(2,1)S(1)}, bf16[128,384]{1,0:T(8,128)(2,1)S(1)}, u32[]{:S(2)}, u32[]{:S(2)}) collective-permute-start(bf16[128,384]{1,0:T(8,128)(2,1)S(1)} %get-tuple-element.258), channel_id=1, source_target_pairs={{0,16},{16,0},{1,17},{17,1},{2,18},{18,2},{3,19},{19,3},{4,20},{20... | collective-permute-start | bytes 294920 | tf_op jit(solution)/shard_map/ppermute | solution.py:922
  64.9 5.1 %collective-permute-start.28 = (bf16[4,40,128]{2,1,0:T(8,128)(2,1)S(1)}, bf16[4,40,128]{2,1,0:T(8,128)(2,1)S(1)}, u32[]{:S(2)}, u32[]{:S(2)}) collective-permute-start(bf16[4,40,128]{2,1,0:T(8,128)(2,1)S(1)} %get-tuple-element.318), channel_id=1, source_target_pairs={{0,1},{1,0},{4,5},{5,4},{2,3},{3,2},{6,7},{7,6},{8,9},{9,8},{12,13... | collective-permute-start | bytes 122888 | tf_op jit(solution)/shard_map/ppermute | solution.py:932
  65.4 4.6 %collective-permute-start.27 = (bf16[4,40,128]{2,1,0:T(8,128)(2,1)S(1)}, bf16[4,40,128]{2,1,0:T(8,128)(2,1)S(1)}, u32[]{:S(2)}, u32[]{:S(2)}) collective-permute-start(bf16[4,40,128]{2,1,0:T(8,128)(2,1)S(1)} %get-tuple-element.319), channel_id=1, source_target_pairs={{0,4},{1,5},{4,0},{5,1},{2,6},{3,7},{6,2},{7,3},{8,12},{9,13},{12,... | collective-permute-start | bytes 122888 | tf_op jit(solution)/shard_map/ppermute | solution.py:932
  65.9 4.9 %collective-permute-start.26 = (bf16[4,40,128]{2,1,0:T(8,128)(2,1)S(1)}, bf16[4,40,128]{2,1,0:T(8,128)(2,1)S(1)}, u32[]{:S(2)}, u32[]{:S(2)}) collective-permute-start(bf16[4,40,128]{2,1,0:T(8,128)(2,1)S(1)} %get-tuple-element.320), channel_id=1, source_target_pairs={{0,5},{1,4},{4,1},{5,0},{2,7},{3,6},{6,3},{7,2},{8,13},{9,12},{12,... | collective-permute-start | bytes 122888 | tf_op jit(solution)/shard_map/ppermute | solution.py:932
  70.9 1.3 %collective-permute-start.29 = (bf16[128,384]{1,0:T(8,128)(2,1)S(1)}, bf16[128,384]{1,0:T(8,128)(2,1)S(1)}, u32[]{:S(2)}, u32[]{:S(2)}) collective-permute-start(bf16[128,384]{1,0:T(8,128)(2,1)S(1)} %get-tuple-element.280), channel_id=1, source_target_pairs={{0,2},{2,0},{1,3},{3,1},{4,6},{6,4},{5,7},{7,5},{8,10},{10,8},{9,1... | collective-permute-start | bytes 294920 | tf_op jit(solution)/shard_map/ppermute | solution.py:922
  70.9 2.0 %collective-permute-start.31 = (bf16[128,384]{1,0:T(8,128)(2,1)S(1)}, bf16[128,384]{1,0:T(8,128)(2,1)S(1)}, u32[]{:S(2)}, u32[]{:S(2)}) collective-permute-start(bf16[128,384]{1,0:T(8,128)(2,1)S(1)} %get-tuple-element.284), channel_id=1, source_target_pairs={{0,2},{2,0},{1,3},{3,1},{4,6},{6,4},{5,7},{7,5},{8,10},{10,8},{9,1... | collective-permute-start | bytes 294920 | tf_op jit(solution)/shard_map/ppermute | solution.py:922
  72.2 7.4 %collective-permute-start.30 = (bf16[128,384]{1,0:T(8,128)(2,1)S(1)}, bf16[128,384]{1,0:T(8,128)(2,1)S(1)}, u32[]{:S(2)}, u32[]{:S(2)}) collective-permute-start(bf16[128,384]{1,0:T(8,128)(2,1)S(1)} %pad_maximum_fusion.4), channel_id=1, source_target_pairs={{0,8},{4,12},{8,0},{12,4},{1,9},{5,13},{9,1},{13,5},{2,10},{6,14},... | collective-permute-start | bytes 294920 | tf_op jit(solution)/shard_map/ppermute | solution.py:1202
  72.9 4.4 %collective-permute-start.32 = (bf16[96,384]{1,0:T(8,128)(2,1)S(1)}, bf16[96,384]{1,0:T(8,128)(2,1)S(1)}, u32[]{:S(2)}, u32[]{:S(2)}) collective-permute-start(bf16[96,384]{1,0:T(8,128)(2,1)S(1)} %pad_maximum_fusion.5), channel_id=1, source_target_pairs={{0,4},{4,0},{8,12},{12,8},{1,5},{5,1},{9,13},{13,9},{2,6},{6,2},{1... | collective-permute-start | bytes 221192 | tf_op jit(solution)/shard_map/ppermute | solution.py:1202
  74.0 5.7 %collective-permute-start.33 = (bf16[96,384]{1,0:T(8,128)(2,1)S(1)}, bf16[96,384]{1,0:T(8,128)(2,1)S(1)}, u32[]{:S(2)}, u32[]{:S(2)}) collective-permute-start(bf16[96,384]{1,0:T(8,128)(2,1)S(1)} %pad_maximum_fusion.6), channel_id=1, source_target_pairs={{0,12},{4,8},{8,4},{12,0},{1,13},{5,9},{9,5},{13,1},{2,14},{6,10},... | collective-permute-start | bytes 221192 | tf_op jit(solution)/shard_map/ppermute | solution.py:1202
  82.1 1.7 %collective-permute-start.34 = (bf16[4,4,80,128]{3,2,1,0:T(8,128)(2,1)S(1)}, bf16[4,4,80,128]{3,2,1,0:T(8,128)(2,1)S(1)}, u32[]{:S(2)}, u32[]{:S(2)}) collective-permute-start(bf16[4,4,80,128]{3,2,1,0:T(8,128)(2,1)S(1)} %get-tuple-element.299), channel_id=1, source_target_pairs={{0,2},{2,0},{1,3},{3,1},{4,6},{6,4},{5,7},{7,5},{8,10},{10,8},{9,1... | collective-permute-start | bytes 983048 | tf_op jit(solution)/shard_map/ppermute | solution.py:922
  84.0 6.0 %collective-permute-start.35 = (bf16[4,80,128]{2,1,0:T(8,128)(2,1)S(1)}, bf16[4,80,128]{2,1,0:T(8,128)(2,1)S(1)}, u32[]{:S(2)}, u32[]{:S(2)}) collective-permute-start(bf16[4,80,128]{2,1,0:T(8,128)(2,1)S(1)} %get-tuple-element.313), channel_id=1, source_target_pairs={{0,5},{1,4},{4,1},{5,0},{2,7},{3,6},{6,3},{7,2},{8,13},{9,12},{12,... | collective-permute-start | bytes 245768 | tf_op jit(solution)/shard_map/ppermute | solution.py:932
  85.7 4.7 %collective-permute-start.37 = (bf16[4,80,128]{2,1,0:T(8,128)(2,1)S(1)}, bf16[4,80,128]{2,1,0:T(8,128)(2,1)S(1)}, u32[]{:S(2)}, u32[]{:S(2)}) collective-permute-start(bf16[4,80,128]{2,1,0:T(8,128)(2,1)S(1)} %get-tuple-element.314), channel_id=1, source_target_pairs={{0,1},{1,0},{4,5},{5,4},{2,3},{3,2},{6,7},{7,6},{8,9},{9,8},{12,13... | collective-permute-start | bytes 245768 | tf_op jit(solution)/shard_map/ppermute | solution.py:932
  86.1 5.0 %collective-permute-start.36 = (bf16[4,80,128]{2,1,0:T(8,128)(2,1)S(1)}, bf16[4,80,128]{2,1,0:T(8,128)(2,1)S(1)}, u32[]{:S(2)}, u32[]{:S(2)}) collective-permute-start(bf16[4,80,128]{2,1,0:T(8,128)(2,1)S(1)} %get-tuple-element.315), channel_id=1, source_target_pairs={{0,4},{1,5},{4,0},{5,1},{2,6},{3,7},{6,2},{7,3},{8,12},{9,13},{12,... | collective-permute-start | bytes 245768 | tf_op jit(solution)/shard_map/ppermute | solution.py:932
  91.3 6.4 %collective-permute-start.38 = (bf16[120,128]{1,0:T(8,128)(2,1)S(1)}, bf16[120,128]{1,0:T(8,128)(2,1)S(1)}, u32[]{:S(2)}, u32[]{:S(2)}) collective-permute-start(bf16[120,128]{1,0:T(8,128)(2,1)S(1)} %get-tuple-element.307), channel_id=1, source_target_pairs={{0,24},{8,16},{16,8},{24,0},{1,25},{9,17},{17,9},{25,1},{2,26},{10... | collective-permute-start | bytes 92168 | tf_op jit(solution)/shard_map/ppermute | solution.py:932
  93.5 5.1 %collective-permute-start.39 = (bf16[120,128]{1,0:T(8,128)(2,1)S(1)}, bf16[120,128]{1,0:T(8,128)(2,1)S(1)}, u32[]{:S(2)}, u32[]{:S(2)}) collective-permute-start(bf16[120,128]{1,0:T(8,128)(2,1)S(1)} %get-tuple-element.308), channel_id=1, source_target_pairs={{0,16},{8,24},{16,0},{24,8},{1,17},{9,25},{17,1},{25,9},{2,18},{10... | collective-permute-start | bytes 92168 | tf_op jit(solution)/shard_map/ppermute | solution.py:932
  94.4 4.2 %collective-permute-start.40 = (bf16[120,128]{1,0:T(8,128)(2,1)S(1)}, bf16[120,128]{1,0:T(8,128)(2,1)S(1)}, u32[]{:S(2)}, u32[]{:S(2)}) collective-permute-start(bf16[120,128]{1,0:T(8,128)(2,1)S(1)} %get-tuple-element.309), channel_id=1, source_target_pairs={{0,8},{8,0},{16,24},{24,16},{1,9},{9,1},{17,25},{25,17},{2,10},{10... | collective-permute-start | bytes 92168 | tf_op jit(solution)/shard_map/ppermute | solution.py:932

commit v2 on v1

--- a/solution.py
+++ b/solution.py
@@ -438,26 +438,31 @@
 
 
 def row_middle(shared, w_ref, m_ref, vec_ref, *refs):
-    w7 = w_ref[...]
     if shared:
-        (lo_ref, *cot_refs, mine_ref, came_ref), refs = refs[:5], refs[5:]
-        x1 = lo_ref[...].astype(f32)[:, D:]
-        cot = [ref[...].astype(f32)[:, D:] for ref in cot_refs]
-        io = jnp.concatenate([mine_ref[...].astype(f32), came_ref[...].astype(f32)], axis=1).astype(bf16)
-        w7 = swap_halves(w7)
+        (x1_ref, cot_in, mine_ref, came_ref), refs = refs[:4], refs[4:]
+        x1, cot = x1_ref[...], cot_in[...]
+        halves = ((mine_ref[...], w_ref[:SLOT_COLS, :]), (came_ref[...], w_ref[SLOT_COLS:, :]))
     else:
         (lo_ref, hi_ref, *cot_refs, own_ref), refs = refs[: 3 + Z], refs[3 + Z :]
-        x1 = jnp.concatenate([lo_ref[:, :D], hi_ref[:, :D]], axis=0).astype(f32)
+        ready_refs, refs = refs[:3], refs[3:]
+        lo = lo_ref[...].astype(f32)
+        x1 = jnp.concatenate([lo[:, :D], hi_ref[:, :D].astype(f32)], axis=0)
+        near = [ref[...].astype(f32) for ref in cot_refs[:2]]
         wide = [ref[...].astype(f32) for ref in cot_refs[2:]]
-        cot = [ref[:, :D].astype(f32) for ref in cot_refs[:2]] + [b for a in wide for b in (a[:, :D], a[:, D:])]
-        io = own_ref[...]
-    dz2_ref, low_refs, full_refs, dio_refs = refs[0], refs[1:8], refs[8:12], refs[12:]
-    io_ref, dt2_ref, x2_ref, du_ref, hid_ref, dm_ref, cot_ref = low_refs
+        cot = [a[:, :D] for a in near] + [b for a in wide for b in (a[:, :D], a[:, D:])]
+        cot = jnp.concatenate(cot, axis=0)
+        ready_refs[0][...] = lo[:, D:]
+        ready_refs[1][...] = jnp.concatenate([a[:, D:] for a in near], axis=0)
+        ready_refs[2][...] = swap_halves(w_ref[...])
+        halves = ((own_ref[...], w_ref[...]),)
+    dz2_ref, low_refs, full_refs, dio_refs = refs[0], refs[1:7], refs[7:11], refs[11:]
+    dt2_ref, x2_ref, du_ref, hid_ref, dm_ref, cot_ref = low_refs
     xhat3_ref, dz3_ref, xhat2_ref, dx2_ref = full_refs
-    cot = jnp.concatenate(cot, axis=0)
     cot_ref[...] = cot.astype(bf16)
-    io_ref[...] = io
-    xhat2, rstd2 = normed(x1 + dot(io, w7))
+    z2 = x1
+    for io, w7 in halves:
+        z2 = z2 + dot(io, w7)
+    xhat2, rstd2 = normed(z2)
     xhat2_ref[...] = xhat2
     x2 = xhat2 * vec_ref[1:2, :] + vec_ref[4:5, :]
     x2_low = x2.astype(bf16)
@@ -488,12 +493,8 @@
     dz2_ref[...] = dz2
     dt2 = dz2.astype(bf16)
     dt2_ref[...] = dt2
-    dio = dot_t(dt2, w7).astype(bf16)
-    if shared:
-        dio_refs[0][...] = dio[:, :SLOT_COLS]
-        dio_refs[1][...] = dio[:, SLOT_COLS:]
-    else:
-        dio_refs[0][...] = dio
+    for ref, (_, w7) in zip(dio_refs, halves):
+        ref[...] = dot_t(dt2, w7).astype(bf16)
 
 
 def item_backward(n_groups, n_outs, first, last, grid, *refs):
@@ -705,14 +706,17 @@
 
 
 def middle_grads(vec_ref, *refs):
-    sets, refs = (refs[:11], refs[11:22]), refs[22:]
+    (own_ref, mine_ref, came_ref), sets, refs = refs[:3], (refs[3:13], refs[13:23]), refs[23:]
     (gw_ref, gu_ref, gv_ref, gvec_ref), out_refs = refs[:4], refs[4:]
     outs = []
-    for i, (io_ref, dt2_ref, x2_ref, du_ref, hid_ref, dm_ref, cot_ref, *full_refs) in enumerate(sets):
+    for i, (dt2_ref, x2_ref, du_ref, hid_ref, dm_ref, cot_ref, *full_refs) in enumerate(sets):
         xhat3, dz3, xhat2, dx2 = [ref[...] for ref in full_refs]
         cot = cot_ref[...].astype(f32)
         outs.append(xhat3 * vec_ref[2:3, :] + vec_ref[5:6, :])
-        gw = t_dot(io_ref[...], dt2_ref[...])
+        if i == 0:
+            gw = t_dot(own_ref[...], dt2_ref[...])
+        else:
+            gw = jnp.concatenate([t_dot(mine_ref[...], dt2_ref[...]), t_dot(came_ref[...], dt2_ref[...])], axis=0)
         gu = t_dot(du_ref[...], x2_ref[...])
         gv = t_dot(hid_ref[...], dm_ref[...])
         rows = {1: dx2 * xhat2, 2: cot * xhat3, 4: dx2, 5: cot, 7: dz3}
@@ -1240,25 +1244,30 @@
 
     cells_low = like((cells_n, D), bf16)
 
-    def middle_call(shared, ins, dio_shapes):
+    def middle_call(shared, w7, ins, ready, dio_shapes):
         count = q_rows // 2 if shared else q_rows
         low, full, hidden = like((count, D), bf16), like((count, D)), like((count, HIDDEN), bf16)
-        dz2, *outs = pl.pallas_call(
+        outs = pl.pallas_call(
             functools.partial(row_middle, shared),
-            out_shape=[full] + [low] * 3 + [hidden] * 2 + [low] * 2 + [full] * 4 + dio_shapes,
+            out_shape=ready + [full] + [low] * 2 + [hidden] * 2 + [low] * 2 + [full] * 4 + dio_shapes,
             in_specs=[VMEM] * (3 + len(ins)),
-            out_specs=[VMEM] * (12 + len(dio_shapes)),
+            out_specs=[VMEM] * (len(ready) + 11 + len(dio_shapes)),
             compiler_params=small,
             name="row_middle",
-        )(attn[7 * D :], mlp, vec, *ins)
-        return dz2, outs[:11], outs[11:]
+        )(w7, mlp, vec, *ins)
+        ready, (dz2, *outs) = outs[: len(ready)], outs[len(ready) :]
+        return ready, dz2, outs[:10], outs[10:]
 
     half_heads = like(io_mine.shape, bf16)
-    dz2_own, kept, (dio_own,) = middle_call(False, [x_lo, x_hi, *cot_in, io_own], [like(io_own.shape, bf16)])
+    ready = [like((q_rows // 2, D)), like((q_rows // 2, D)), like((D, D), bf16)]
+    (x1_shared, cot_shared, w7_shared), dz2_own, kept, (dio_own,) = middle_call(
+        False, attn[7 * D :], [x_lo, x_hi, *cot_in, io_own], ready, [like(io_own.shape, bf16)]
+    )
     io_came, dio_own = lax.optimization_barrier((io_came, dio_own))
-    dz2_shared, kept_shared, (dio_mine, dio_give) = middle_call(
-        True, [x_lo, *cot_in[:2], io_mine, io_came], [half_heads] * 2
+    _, dz2_shared, kept_shared, (dio_mine, dio_give) = middle_call(
+        True, w7_shared, [x1_shared, cot_shared, io_mine, io_came], [], [half_heads] * 2
     )
+    kept = [io_own, io_mine, io_came] + kept
     dz2, kept = (dz2_own, dz2_shared), kept + kept_shared
     dio_in = [dio_own, dio_mine, to_shared(dio_give)]
 
@@ -1268,7 +1277,7 @@
             out_shape=(like((D, D)), like((HIDDEN, D)), like((HIDDEN, D)), like((8, D)))
             + (pair_block,) * 2
             + (like((rows // 2, PAIR), bf16),) * 2,
-            in_specs=[VMEM] * 23,
+            in_specs=[VMEM] * 24,
             out_specs=(VMEM,) * (4 + Z),
             compiler_params=small,
             name="middle_grads",

time: 99.6 us -> 98.6 us (0.990)
  no operation moved by 1% of the time
where the time goes in v2:
time: 98.6 us; the launch traced here: 98.4 us
  starting transfers between devices  38.1 us (39%)
  waiting for transfers between devices  31 us (31%)
  Pallas kernels  25.1 us (25%)
  local copies, waits for them, and re-layouts  2.79 us (3%)
  between operations  1 us (1%)
    ppermute x15, starting transfers between devices, along(): lax.ppermute(a, axes, [(i, i ^ x) for i in range(Z)])  20.9 us
    ppermute x15, waiting for transfers between devices, along(): lax.ppermute(a, axes, [(i, i ^ x) for i in range(Z)])  12.3 us
    pallas_call x6, Pallas kernels, item_call(): pl.pallas_call(kernel, out_shape=[a for a, _ in outs], in_specs=specs(ins...  10.8 us
    ppermute x18, waiting for transfers between devices, swap(): return lax.ppermute(a, axis, [(0, 1), (1, 0)])  9.84 us
    ppermute x18, starting transfers between devices, swap(): return lax.ppermute(a, axis, [(0, 1), (1, 0)])  8.58 us
    ppermute x6, starting transfers between devices, to_task(): lax.ppermute(block, TASK_AXES, [(j, j ^ TASK_ORDER[i]) for j in range(Z)])  7.23 us
    ppermute x6, waiting for transfers between devices, to_task(): lax.ppermute(block, TASK_AXES, [(j, j ^ TASK_ORDER[i]) for j in range(Z)])  5.82 us
    pallas_call x2, Pallas kernels, middle_call(): pl.pallas_call(functools.partial(row_middle, shared), out_shape=ready + [...  3.05 us
  transfers between devices with their start and end apart: 41, of which 23 were waited for; matrix products, arithmetic and copies ran while one was open for 0% of the time, Pallas kernels for 13%

profile of v2, /device:TPU:0, one launch (start us, length us, event | category | flops | bytes accessed | tf_op | source)
XLA Modules:
  0.0 98.4 jit_solution(15584075541408716565)
XLA Ops:
  0.6 1.5 %share_pack.1 = (bf16[112,128]{1,0:T(8,128)(2,1)}, bf16[112,128]{1,0:T(8,128)(2,1)}, bf16[112,128]{1,0:T(8,128)(2,1)}, bf16[112,128]{1,0:T(8,128)(2,1)}) custom-call(bf16[48,192]{1,0:T(8,128)(2,1)} %refs_0_.1, bf16[24,192]{1,0:T(8,128)(2,1)} %refs_1_.1, bf16[1,48]{1,0:T(2,128)(2,1)} %bitcast.70, s32[1,64]{1,0:T(1,128)} %refs_3_.1, s32[1,64]{1,0:T(1,128)} %refs_4_.1, ...), custom_call_target="tpu_custom_call" | custom-call | tf_op jit(solution)/shard_map/share_pack/pallas_call | solution.py:966
  2.1 5.1 %collective-permute-start = (bf16[112,128]{1,0:T(8,128)(2,1)}, bf16[112,128]{1,0:T(8,128)(2,1)S(1)}, u32[]{:S(2)}, u32[]{:S(2)}) collective-permute-start(bf16[112,128]{1,0:T(8,128)(2,1)} %get-tuple-element.162), channel_id=1, source_target_pairs={{0,24},{8,16},{16,8},{24,0},{1,25},{9,17},{17,9},{25,1},{2,26},{10... | collective-permute-start | bytes 86024 | tf_op jit(solution)/shard_map/ppermute | solution.py:936
  7.9 0.9 copy-done
  8.8 0.9 copy-done.1
  10.6 1.7 %collective-permute-done.1 = bf16[112,128]{1,0:T(8,128)(2,1)S(1)} collective-permute-done((bf16[112,128]{1,0:T(8,128)(2,1)}, bf16[112,128]{1,0:T(8,128)(2,1)S(1)}, u32[]{:S(2)}, u32[]{:S(2)}) %collective-permute-start.1) | collective-permute-done | bytes 28704 | tf_op jit(solution)/shard_map/ppermute | solution.py:936
  12.3 1.6 %collective-permute-start.5 = (bf16[4,112,128]{2,1,0:T(8,128)(2,1)S(1)}, bf16[4,112,128]{2,1,0:T(8,128)(2,1)S(1)}, u32[]{:S(2)}, u32[]{:S(2)}) collective-permute-start(bf16[4,112,128]{2,1,0:T(8,128)(2,1)S(1)} %pad_maximum_fusion.1.refs_0_), channel_id=1, source_target_pairs={{0,1},{1,0},{4,5},{5,4},{2,3},{3,2},{6,7},{7,6},{8,9},{9,8},{12,13... | collective-permute-start | bytes 344072 | tf_op jit(solution)/shard_map/ppermute | solution.py:936
  13.8 1.5 %collective-permute-start.4 = (bf16[4,112,128]{2,1,0:T(8,128)(2,1)S(1)}, bf16[4,112,128]{2,1,0:T(8,128)(2,1)S(1)}, u32[]{:S(2)}, u32[]{:S(2)}) collective-permute-start(bf16[4,112,128]{2,1,0:T(8,128)(2,1)S(1)} %pad_maximum_fusion.1.refs_0_), channel_id=1, source_target_pairs={{0,4},{1,5},{4,0},{5,1},{2,6},{3,7},{6,2},{7,3},{8,12},{9,13},{12,... | collective-permute-start | bytes 344072 | tf_op jit(solution)/shard_map/ppermute | solution.py:936
  15.8 2.4 %collective-permute-done.5.refs_3_ = bf16[4,112,128]{2,1,0:T(8,128)(2,1)S(1)} collective-permute-done((bf16[4,112,128]{2,1,0:T(8,128)(2,1)S(1)}, bf16[4,112,128]{2,1,0:T(8,128)(2,1)S(1)}, u32[]{:S(2)}, u32[]{:S(2)}) %collective-permute-start.5) | collective-permute-done | bytes 114720 | tf_op jit(solution)/shard_map/ppermute | solution.py:936
  18.2 1.2 %collective-permute-done.4.refs_2_ = bf16[4,112,128]{2,1,0:T(8,128)(2,1)S(1)} collective-permute-done((bf16[4,112,128]{2,1,0:T(8,128)(2,1)S(1)}, bf16[4,112,128]{2,1,0:T(8,128)(2,1)S(1)}, u32[]{:S(2)}, u32[]{:S(2)}) %collective-permute-start.4) | collective-permute-done | bytes 114720 | tf_op jit(solution)/shard_map/ppermute | solution.py:936
  19.4 1.6 %collective-permute-done.3.refs_1_ = bf16[4,112,128]{2,1,0:T(8,128)(2,1)S(1)} collective-permute-done((bf16[4,112,128]{2,1,0:T(8,128)(2,1)S(1)}, bf16[4,112,128]{2,1,0:T(8,128)(2,1)S(1)}, u32[]{:S(2)}, u32[]{:S(2)}) %collective-permute-start.3) | collective-permute-done | bytes 114720 | tf_op jit(solution)/shard_map/ppermute | solution.py:936
  21.1 1.3 %collective-permute-done.7.refs_5_ = bf16[4,112,128]{2,1,0:T(8,128)(2,1)S(1)} collective-permute-done((bf16[4,112,128]{2,1,0:T(8,128)(2,1)S(1)}, bf16[4,112,128]{2,1,0:T(8,128)(2,1)S(1)}, u32[]{:S(2)}, u32[]{:S(2)}) %collective-permute-start.7) | collective-permute-done | bytes 114720 | tf_op jit(solution)/shard_map/ppermute | solution.py:926
  22.8 1.9 %feat_forward.1 = (f32[384,192]{1,0:T(8,128)S(1)}, f32[384,192]{1,0:T(8,128)S(1)}, bf16[3,384,192]{2,1,0:T(8,128)(2,1)S(1)}, bf16[384,192]{1,0:T(8,128)(2,1)S(1)...) custom-call(bf16[384,192]{1,0:T(8,128)(2,1)S(1)} %get-tuple-element., ...), custom_call_target="tpu_custom_call" | custom-call | tf_op jit(solution)/shard_map/feat_forward/pallas_call | solution.py:1082
  24.8 1.1 %collective-permute-start.11 = (bf16[96,384]{1,0:T(8,128)(2,1)S(1)}, bf16[96,384]{1,0:T(8,128)(2,1)S(1)}, u32[]{:S(2)}, u32[]{:S(2)}) collective-permute-start(bf16[96,384]{1,0:T(8,128)(2,1)S(1)} %get-tuple-element.175), channel_id=1, source_target_pairs={{0,4},{4,0},{8,12},{12,8},{1,5},{5,1},{9,13},{13,9},{2,6},{6,2},{1... | collective-permute-start | bytes 221192 | tf_op jit(solution)/shard_map/ppermute | solution.py:1206
  25.9 2.4 %collective-permute-start.12 = (bf16[96,384]{1,0:T(8,128)(2,1)S(1)}, bf16[96,384]{1,0:T(8,128)(2,1)S(1)}, u32[]{:S(2)}, u32[]{:S(2)}) collective-permute-start(bf16[96,384]{1,0:T(8,128)(2,1)S(1)} %get-tuple-element.176), channel_id=1, source_target_pairs={{0,12},{4,8},{8,4},{12,0},{1,13},{5,9},{9,5},{13,1},{2,14},{6,10},... | collective-permute-start | bytes 221192 | tf_op jit(solution)/shard_map/ppermute | solution.py:1206
  28.3 2.2 %collective-permute-done.10 = bf16[128,384]{1,0:T(8,128)(2,1)S(1)} collective-permute-done((bf16[128,384]{1,0:T(8,128)(2,1)S(1)}, bf16[128,384]{1,0:T(8,128)(2,1)S(1)}, u32[]{:S(2)}, u32[]{:S(2)}) %collective-permute-start.10) | collective-permute-done | bytes 98336 | tf_op jit(solution)/shard_map/ppermute | solution.py:1206
  30.5 1.9 %collective-permute-start.15 = (bf16[128,384]{1,0:T(8,128)(2,1)S(1)}, bf16[128,384]{1,0:T(8,128)(2,1)S(1)}, u32[]{:S(2)}, u32[]{:S(2)}) collective-permute-start(bf16[128,384]{1,0:T(8,128)(2,1)S(1)} %pad_maximum_fusion.2.refs_0_), channel_id=1, source_target_pairs={{0,16},{16,0},{1,17},{17,1},{2,18},{18,2},{3,19},{19,3},{4,20},{20... | collective-permute-start | bytes 294920 | tf_op jit(solution)/shard_map/ppermute | solution.py:926
  33.8 1.3 %collective-permute-start.17 = (bf16[128,384]{1,0:T(8,128)(2,1)S(1)}, bf16[128,384]{1,0:T(8,128)(2,1)S(1)}, u32[]{:S(2)}, u32[]{:S(2)}) collective-permute-start(bf16[128,384]{1,0:T(8,128)(2,1)S(1)} %pad_maximum_fusion.3.refs_1_), channel_id=1, source_target_pairs={{0,16},{16,0},{1,17},{17,1},{2,18},{18,2},{3,19},{19,3},{4,20},{20... | collective-permute-start | bytes 294920 | tf_op jit(solution)/shard_map/ppermute | solution.py:926
  35.1 1.9 %item_forward.3 = (bf16[9,512,256]{2,1,0:T(8,128)(2,1)S(1)}, f32[16,256]{1,0:T(8,128)S(1)}, bf16[3,256,128]{2,1,0:T(8,128)(2,1)S(1)}, f32[16,256]{1,0:T(8,128)S(1)}, f32[384,256]{1,0:T(8,128)S(1)}) custom-call(bf16[128,384]{1,0:T(8,128)(2,1)S(1)} %pad_maximum_fusion.2.refs_0_, bf16[128,384]{1,0:T(8,128)(2,1)S(1)} %pad_maximum_fusion.3.refs_1_, ...), custom_call_target="tpu_custom_call" | custom-call | flops 100000000 | tf_op jit(solution)/shard_map/item_forward/pallas_call | solution.py:1120
  37.3 1.1 %collective-permute-done.16.refs_1_.refs_5_ = bf16[128,384]{1,0:T(8,128)(2,1)S(1)} collective-permute-done((bf16[128,384]{1,0:T(8,128)(2,1)S(1)}, bf16[128,384]{1,0:T(8,128)(2,1)S(1)}, u32[]{:S(2)}, u32[]{:S(2)}) %collective-permute-start.16) | collective-permute-done | bytes 98336 | tf_op jit(solution)/shard_map/ppermute | solution.py:926
  38.4 1.1 %item_forward.4 = (bf16[9,256,256]{2,1,0:T(8,128)(2,1)S(1)}, f32[16,256]{1,0:T(8,128)S(1)}, f32[16,256]{1,0:T(8,128)S(1)}, f32[16,256]{1,0:T(8,128)S(1)}, f32[384,256]{1,0:T(8,128)S(1)}) custom-call(bf16[128,384]{1,0:T(8,128)(2,1)S(1)} %collective-permute-done.15.refs_0_.refs_4_, bf16[128,384]{1,0:T(8,128)(2,1)S(1)} %collective-permute-done.16.refs_1_.refs_5_, ...), custom_call_target="tpu_custom_call" | custom-call | flops 100000000 | tf_op jit(solution)/shard_map/item_forward/pallas_call | solution.py:1120
  39.4 2.0 %collective-permute-done.17.refs_0_.refs_6_ = bf16[128,384]{1,0:T(8,128)(2,1)S(1)} collective-permute-done((bf16[128,384]{1,0:T(8,128)(2,1)S(1)}, bf16[128,384]{1,0:T(8,128)(2,1)S(1)}, u32[]{:S(2)}, u32[]{:S(2)}) %collective-permute-start.17) | collective-permute-done | bytes 98336 | tf_op jit(solution)/shard_map/ppermute | solution.py:926
  41.4 1.3 %collective-permute-done.18.refs_1_.refs_7_ = bf16[128,384]{1,0:T(8,128)(2,1)S(1)} collective-permute-done((bf16[128,384]{1,0:T(8,128)(2,1)S(1)}, bf16[128,384]{1,0:T(8,128)(2,1)S(1)}, u32[]{:S(2)}, u32[]{:S(2)}) %collective-permute-start.18) | collective-permute-done | bytes 98336 | tf_op jit(solution)/shard_map/ppermute | solution.py:926
  42.7 1.1 %item_forward.5 = (bf16[9,256,256]{2,1,0:T(8,128)(2,1)S(1)}, f32[16,256]{1,0:T(8,128)S(1)}, f32[16,256]{1,0:T(8,128)S(1)}, f32[16,256]{1,0:T(8,128)S(1)}, f32[38...) custom-call(bf16[128,384]{1,0:T(8,128)(2,1)S(1)} %collective-permute, ...), custom_call_target="tpu_custom_call" | custom-call | flops 100000000 | tf_op jit(solution)/shard_map/item_forward/pallas_call | solution.py:1120
  44.6 1.6 %row_middle.2 = (f32[128,192]{1,0:T(8,128)S(1)}, f32[128,192]{1,0:T(8,128)S(1)}, bf16[192,192]{1,0:T(8,128)(2,1)S(1)}, f32[256,192]{1,0:T(8,128)S(1)}, bf16[256,...) custom-call(bf16[192,192]{1,0:T(8,128)(2,1)S(1)} %slice.141.w_ref, ...), custom_call_target="tpu_custom_call" | custom-call | tf_op jit(solution)/shard_map/row_middle/pallas_call | solution.py:1250
  46.2 1.7 %collective-permute-done.19.refs_3_.refs_2_ = bf16[128,96]{1,0:T(8,128)(2,1)S(1)} collective-permute-done((bf16[128,96]{1,0:T(8,128)(2,1)S(1)}, bf16[128,96]{1,0:T(8,128)(2,1)S(1)}, u32[]{:S(2)}, u32[]{:S(2)}) %collective-permute-start.19) | collective-permute-done | bytes 24608 | tf_op jit(solution)/shard_map/ppermute | solution.py:1239
  47.8 1.5 %row_middle.3 = (f32[128,192]{1,0:T(8,128)S(1)}, bf16[128,192]{1,0:T(8,128)(2,1)S(1)}, bf16[128,192]{1,0:T(8,128)(2,1)S(1)}, bf16[128,384]{1,0:T(8,128)(2,1)S(1)...) custom-call(bf16[192,192]{1,0:T(8,128)(2,1)S(1)} %get-tuple-element., ...), custom_call_target="tpu_custom_call" | custom-call | tf_op jit(solution)/shard_map/row_middle/pallas_call | solution.py:1250
  50.0 1.0 item_turn.1
  52.0 1.3 %collective-permute-done.20.refs_12_ = bf16[128,96]{1,0:T(8,128)(2,1)S(1)} collective-permute-done((bf16[128,96]{1,0:T(8,128)(2,1)S(1)}, bf16[128,96]{1,0:T(8,128)(2,1)S(1)}, u32[]{:S(2)}, u32[]{:S(2)}) %collective-permute-start.20) | collective-permute-done | bytes 24608 | tf_op jit(solution)/shard_map/ppermute | solution.py:1239
  53.3 2.4 %item_backward.2 = (f32[128,384]{1,0:T(8,128)S(1)}, bf16[128,384]{1,0:T(8,128)(2,1)S(1)}, f32[128,384]{1,0:T(8,128)S(1)}, bf16[128,384]{1,0:T(8,128)(2,1)S(1)}, ...) custom-call(bf16[384,256]{1,0:T(8,128)(2,1)S(1)} %get-tuple-element.198.refs_0_, ...), custom_call_target="tpu_custom_call" | custom-call | flops 100000000 | tf_op jit(solution)/shard_map/item_backward/pallas_call | solution.py:1120
  57.7 2.9 %collective-permute-start.24 = (bf16[128,384]{1,0:T(8,128)(2,1)S(1)}, bf16[128,384]{1,0:T(8,128)(2,1)S(1)}, u32[]{:S(2)}, u32[]{:S(2)}) collective-permute-start(bf16[128,384]{1,0:T(8,128)(2,1)S(1)} %get-tuple-element.260), channel_id=1, source_target_pairs={{0,16},{16,0},{1,17},{17,1},{2,18},{18,2},{3,19},{19,3},{4,20},{20... | collective-permute-start | bytes 294920 | tf_op jit(solution)/shard_map/ppermute | solution.py:926
  60.6 3.3 %item_backward.3 = (f32[128,384]{1,0:T(8,128)S(1)}, f32[128,384]{1,0:T(8,128)S(1)}, bf16[128,384]{1,0:T(8,128)(2,1)S(1)}, bf16[128,384]{1,0:T(8,128)(2,1)S(1)}, f32[576,192]{1,0:T(8,128)S(1)}) custom-call(bf16[384,512]{1,0:T(8,128)(2,1)S(1)} %get-tuple-element.261.refs_0_, bf16[3,512,128]{2,1,0:T(8,128)(2,1)S(1)} %get-tuple-element.262.refs_1_, ...), custom_call_target="tpu_custom_call" | custom-call | flops 100000000 | tf_op jit(solution)/shard_map/item_backward/pallas_call | solution.py:1120
  65.0 2.5 %collective-permute-start.26 = (bf16[4,40,128]{2,1,0:T(8,128)(2,1)S(1)}, bf16[4,40,128]{2,1,0:T(8,128)(2,1)S(1)}, u32[]{:S(2)}, u32[]{:S(2)}) collective-permute-start(bf16[4,40,128]{2,1,0:T(8,128)(2,1)S(1)} %get-tuple-element.322), channel_id=1, source_target_pairs={{0,5},{1,4},{4,1},{5,0},{2,7},{3,6},{6,3},{7,2},{8,13},{9,12},{12,... | collective-permute-start | bytes 122888 | tf_op jit(solution)/shard_map/ppermute | solution.py:936
  67.5 1.5 %collective-permute-done.24 = bf16[128,384]{1,0:T(8,128)(2,1)S(1)} collective-permute-done((bf16[128,384]{1,0:T(8,128)(2,1)S(1)}, bf16[128,384]{1,0:T(8,128)(2,1)S(1)}, u32[]{:S(2)}, u32[]{:S(2)}) %collective-permute-start.24) | collective-permute-done | bytes 98336 | tf_op jit(solution)/shard_map/ppermute | solution.py:926
  69.1 0.9 collective-permute-done.26
  71.9 1.1 %collective-permute-start.32 = (bf16[96,384]{1,0:T(8,128)(2,1)S(1)}, bf16[96,384]{1,0:T(8,128)(2,1)S(1)}, u32[]{:S(2)}, u32[]{:S(2)}) collective-permute-start(bf16[96,384]{1,0:T(8,128)(2,1)S(1)} %pad_maximum_fusion.5), channel_id=1, source_target_pairs={{0,4},{4,0},{8,12},{12,8},{1,5},{5,1},{9,13},{13,9},{2,6},{6,2},{1... | collective-permute-start | bytes 221192 | tf_op jit(solution)/shard_map/ppermute | solution.py:1206
  73.0 2.0 %collective-permute-start.33 = (bf16[96,384]{1,0:T(8,128)(2,1)S(1)}, bf16[96,384]{1,0:T(8,128)(2,1)S(1)}, u32[]{:S(2)}, u32[]{:S(2)}) collective-permute-start(bf16[96,384]{1,0:T(8,128)(2,1)S(1)} %pad_maximum_fusion.6), channel_id=1, source_target_pairs={{0,12},{4,8},{8,4},{12,0},{1,13},{5,9},{9,5},{13,1},{2,14},{6,10},... | collective-permute-start | bytes 221192 | tf_op jit(solution)/shard_map/ppermute | solution.py:1206
  75.1 1.3 %collective-permute-done.32 = bf16[96,384]{1,0:T(8,128)(2,1)S(1)} collective-permute-done((bf16[96,384]{1,0:T(8,128)(2,1)S(1)}, bf16[96,384]{1,0:T(8,128)(2,1)S(1)}, u32[]{:S(2)}, u32[]{:S(2)}) %collective-permute-start.32) | collective-permute-done | bytes 73760 | tf_op jit(solution)/shard_map/ppermute | solution.py:1206
  76.4 2.4 %collective-permute-done.33 = bf16[96,384]{1,0:T(8,128)(2,1)S(1)} collective-permute-done((bf16[96,384]{1,0:T(8,128)(2,1)S(1)}, bf16[96,384]{1,0:T(8,128)(2,1)S(1)}, u32[]{:S(2)}, u32[]{:S(2)}) %collective-permute-start.33) | collective-permute-done | bytes 73760 | tf_op jit(solution)/shard_map/ppermute | solution.py:1206
  78.8 2.2 %feat_backward.1 = (f32[768,192]{1,0:T(8,128)S(1)}, f32[8,192]{1,0:T(8,128)S(1)}, f32[384,192]{1,0:T(8,128)S(1)}, bf16[3,384,192]{2,1,0:T(8,128)(2,1)S(1)}) custom-call(f32[384,192]{1,0:T(8,128)S(1)} %get-tuple-element.290.xhat1_ref, f32[384,192]{1,0:T(8,128)S(1)} %get-tuple-element.291.rstd1_ref, bf16[384,192]{1,0:T(8,128)(2,1)S(1)} %get-tuple-element.167.cells_ref, ...), custom_call_target="tpu_custom_call" | custom-call | tf_op jit(solution)/shard_map/feat_backward/pallas_call | solution.py:1355
  81.3 1.6 %collective-permute-done.34 = bf16[4,4,80,128]{3,2,1,0:T(8,128)(2,1)S(1)} collective-permute-done((bf16[4,4,80,128]{3,2,1,0:T(8,128)(2,1)S(1)}, bf16[4,4,80,128]{3,2,1,0:T(8,128)(2,1)S(1)}, u32[]{:S(2)}, u32[]{:S(2)}) %collective-permute-start.34) | collective-permute-done | bytes 327712 | tf_op jit(solution)/shard_map/ppermute | solution.py:926
  83.0 1.7 %collective-permute-start.35 = (bf16[4,80,128]{2,1,0:T(8,128)(2,1)S(1)}, bf16[4,80,128]{2,1,0:T(8,128)(2,1)S(1)}, u32[]{:S(2)}, u32[]{:S(2)}) collective-permute-start(bf16[4,80,128]{2,1,0:T(8,128)(2,1)S(1)} %get-tuple-element.315), channel_id=1, source_target_pairs={{0,5},{1,4},{4,1},{5,0},{2,7},{3,6},{6,3},{7,2},{8,13},{9,12},{12,... | collective-permute-start | bytes 245768 | tf_op jit(solution)/shard_map/ppermute | solution.py:936
  85.2 1.4 %collective-permute-start.36 = (bf16[4,80,128]{2,1,0:T(8,128)(2,1)S(1)}, bf16[4,80,128]{2,1,0:T(8,128)(2,1)S(1)}, u32[]{:S(2)}, u32[]{:S(2)}) collective-permute-start(bf16[4,80,128]{2,1,0:T(8,128)(2,1)S(1)} %get-tuple-element.317), channel_id=1, source_target_pairs={{0,4},{1,5},{4,0},{5,1},{2,6},{3,7},{6,2},{7,3},{8,12},{9,13},{12,... | collective-permute-start | bytes 245768 | tf_op jit(solution)/shard_map/ppermute | solution.py:936
  86.6 2.4 %collective-permute-done.35 = bf16[4,80,128]{2,1,0:T(8,128)(2,1)S(1)} collective-permute-done((bf16[4,80,128]{2,1,0:T(8,128)(2,1)S(1)}, bf16[4,80,128]{2,1,0:T(8,128)(2,1)S(1)}, u32[]{:S(2)}, u32[]{:S(2)}) %collective-permute-start.35) | collective-permute-done | bytes 81952 | tf_op jit(solution)/shard_map/ppermute | solution.py:936
  90.3 2.2 %collective-permute-start.38 = (bf16[120,128]{1,0:T(8,128)(2,1)S(1)}, bf16[120,128]{1,0:T(8,128)(2,1)S(1)}, u32[]{:S(2)}, u32[]{:S(2)}) collective-permute-start(bf16[120,128]{1,0:T(8,128)(2,1)S(1)} %get-tuple-element.309), channel_id=1, source_target_pairs={{0,24},{8,16},{16,8},{24,0},{1,25},{9,17},{17,9},{25,1},{2,26},{10... | collective-permute-start | bytes 92168 | tf_op jit(solution)/shard_map/ppermute | solution.py:936
  92.5 1.0 collective-permute-start.39
  93.5 1.3 %collective-permute-start.40 = (bf16[120,128]{1,0:T(8,128)(2,1)S(1)}, bf16[120,128]{1,0:T(8,128)(2,1)S(1)}, u32[]{:S(2)}, u32[]{:S(2)}) collective-permute-start(bf16[120,128]{1,0:T(8,128)(2,1)S(1)} %get-tuple-element.311), channel_id=1, source_target_pairs={{0,8},{8,0},{16,24},{24,16},{1,9},{9,1},{17,25},{25,17},{2,10},{10... | collective-permute-start | bytes 92168 | tf_op jit(solution)/shard_map/ppermute | solution.py:936
  95.6 1.1 %cell_out.1 = f32[384,192]{1,0:T(8,128)} custom-call(f32[384,192]{1,0:T(8,128)S(1)} %get-tuple-element.306.dz1_ref, bf16[3,384,192]{2,1,0:T(8,128)(2,1)S(1)} %get-tuple-element.307.dqkv_ref, bf16[576,192]{1,0:T(8,128)(2,1)S(1)} %get-tuple-element.318.w_ref), custom_call_target="tpu_custom_call" | custom-call | tf_op jit(solution)/shard_map/cell_out/pallas_call | solution.py:1378
  96.7 1.0 collective-permute-done.39.refs_1_
  (96 shorter events, 15.4 us)
Async XLA Ops:
  2.1 8.4 %collective-permute-start = (bf16[112,128]{1,0:T(8,128)(2,1)}, bf16[112,128]{1,0:T(8,128)(2,1)S(1)}, u32[]{:S(2)}, u32[]{:S(2)}) collective-permute-start(bf16[112,128]{1,0:T(8,128)(2,1)} %get-tuple-element.162), channel_id=1, source_target_pairs={{0,24},{8,16},{16,8},{24,0},{1,25},{9,17},{17,9},{25,1},{2,26},{10... | collective-permute-start | bytes 86024 | tf_op jit(solution)/shard_map/ppermute | solution.py:936
  7.3 5.0 %collective-permute-start.1 = (bf16[112,128]{1,0:T(8,128)(2,1)}, bf16[112,128]{1,0:T(8,128)(2,1)S(1)}, u32[]{:S(2)}, u32[]{:S(2)}) collective-permute-start(bf16[112,128]{1,0:T(8,128)(2,1)} %get-tuple-element.163), channel_id=1, source_target_pairs={{0,16},{8,24},{16,0},{24,8},{1,17},{9,25},{17,1},{25,9},{2,18},{10... | collective-permute-start | bytes 86024 | tf_op jit(solution)/shard_map/ppermute | solution.py:936
  7.3 5.0 %collective-permute-start.2 = (bf16[112,128]{1,0:T(8,128)(2,1)}, bf16[112,128]{1,0:T(8,128)(2,1)S(1)}, u32[]{:S(2)}, u32[]{:S(2)}) collective-permute-start(bf16[112,128]{1,0:T(8,128)(2,1)} %get-tuple-element.164), channel_id=1, source_target_pairs={{0,8},{8,0},{16,24},{24,16},{1,9},{9,1},{17,25},{25,17},{2,10},{10... | collective-permute-start | bytes 86024 | tf_op jit(solution)/shard_map/ppermute | solution.py:936
  7.9 0.9 copy-start
  8.8 0.9 copy-start.1
  9.8 0.7 copy-start.2
  12.3 5.9 %collective-permute-start.5 = (bf16[4,112,128]{2,1,0:T(8,128)(2,1)S(1)}, bf16[4,112,128]{2,1,0:T(8,128)(2,1)S(1)}, u32[]{:S(2)}, u32[]{:S(2)}) collective-permute-start(bf16[4,112,128]{2,1,0:T(8,128)(2,1)S(1)} %pad_maximum_fusion.1.refs_0_), channel_id=1, source_target_pairs={{0,1},{1,0},{4,5},{5,4},{2,3},{3,2},{6,7},{7,6},{8,9},{9,8},{12,13... | collective-permute-start | bytes 344072 | tf_op jit(solution)/shard_map/ppermute | solution.py:936
  13.8 5.6 %collective-permute-start.4 = (bf16[4,112,128]{2,1,0:T(8,128)(2,1)S(1)}, bf16[4,112,128]{2,1,0:T(8,128)(2,1)S(1)}, u32[]{:S(2)}, u32[]{:S(2)}) collective-permute-start(bf16[4,112,128]{2,1,0:T(8,128)(2,1)S(1)} %pad_maximum_fusion.1.refs_0_), channel_id=1, source_target_pairs={{0,4},{1,5},{4,0},{5,1},{2,6},{3,7},{6,2},{7,3},{8,12},{9,13},{12,... | collective-permute-start | bytes 344072 | tf_op jit(solution)/shard_map/ppermute | solution.py:936
  15.3 5.7 %collective-permute-start.3 = (bf16[4,112,128]{2,1,0:T(8,128)(2,1)S(1)}, bf16[4,112,128]{2,1,0:T(8,128)(2,1)S(1)}, u32[]{:S(2)}, u32[]{:S(2)}) collective-permute-start(bf16[4,112,128]{2,1,0:T(8,128)(2,1)S(1)} %pad_maximum_fusion.1.refs_0_), channel_id=1, source_target_pairs={{0,5},{1,4},{4,1},{5,0},{2,7},{3,6},{6,3},{7,2},{8,13},{9,12},{12,... | collective-permute-start | bytes 344072 | tf_op jit(solution)/shard_map/ppermute | solution.py:936
  15.8 5.2 %collective-permute-start.6 = (bf16[4,112,128]{2,1,0:T(8,128)(2,1)S(1)}, bf16[4,112,128]{2,1,0:T(8,128)(2,1)S(1)}, u32[]{:S(2)}, u32[]{:S(2)}) collective-permute-start(bf16[4,112,128]{2,1,0:T(8,128)(2,1)S(1)} %pad_maximum_fusion.1.refs_0_), channel_id=1, source_target_pairs={{0,2},{2,0},{1,3},{3,1},{4,6},{6,4},{5,7},{7,5},{8,10},{10,8},{9,1... | collective-permute-start | bytes 344072 | tf_op jit(solution)/shard_map/ppermute | solution.py:926
  18.2 2.9 %collective-permute-start.9 = (bf16[4,112,128]{2,1,0:T(8,128)(2,1)S(1)}, bf16[4,112,128]{2,1,0:T(8,128)(2,1)S(1)}, u32[]{:S(2)}, u32[]{:S(2)}) collective-permute-start(bf16[4,112,128]{2,1,0:T(8,128)(2,1)S(1)} %collective-permute-done.5.refs_3_), channel_id=1, source_target_pairs={{0,2},{2,0},{1,3},{3,1},{4,6},{6,4},{5,7},{7,5},{8,10},{10,8},{9,1... | collective-permute-start | bytes 344072 | tf_op jit(solution)/shard_map/ppermute | solution.py:926
  19.4 1.6 %collective-permute-start.8 = (bf16[4,112,128]{2,1,0:T(8,128)(2,1)S(1)}, bf16[4,112,128]{2,1,0:T(8,128)(2,1)S(1)}, u32[]{:S(2)}, u32[]{:S(2)}) collective-permute-start(bf16[4,112,128]{2,1,0:T(8,128)(2,1)S(1)} %collective-permute-done.4.refs_2_), channel_id=1, source_target_pairs={{0,2},{2,0},{1,3},{3,1},{4,6},{6,4},{5,7},{7,5},{8,10},{10,8},{9,1... | collective-permute-start | bytes 344072 | tf_op jit(solution)/shard_map/ppermute | solution.py:926
  21.0 1.3 %collective-permute-start.7 = (bf16[4,112,128]{2,1,0:T(8,128)(2,1)S(1)}, bf16[4,112,128]{2,1,0:T(8,128)(2,1)S(1)}, u32[]{:S(2)}, u32[]{:S(2)}) collective-permute-start(bf16[4,112,128]{2,1,0:T(8,128)(2,1)S(1)} %collective-permute-done.3.refs_1_), channel_id=1, source_target_pairs={{0,2},{2,0},{1,3},{3,1},{4,6},{6,4},{5,7},{7,5},{8,10},{10,8},{9,1... | collective-permute-start | bytes 344072 | tf_op jit(solution)/shard_map/ppermute | solution.py:926
  24.7 5.7 %collective-permute-start.10 = (bf16[128,384]{1,0:T(8,128)(2,1)S(1)}, bf16[128,384]{1,0:T(8,128)(2,1)S(1)}, u32[]{:S(2)}, u32[]{:S(2)}) collective-permute-start(bf16[128,384]{1,0:T(8,128)(2,1)S(1)} %get-tuple-element.174), channel_id=1, source_target_pairs={{0,8},{4,12},{8,0},{12,4},{1,9},{5,13},{9,1},{13,5},{2,10},{6,14},... | collective-permute-start | bytes 294920 | tf_op jit(solution)/shard_map/ppermute | solution.py:1206
  24.8 7.6 %collective-permute-start.11 = (bf16[96,384]{1,0:T(8,128)(2,1)S(1)}, bf16[96,384]{1,0:T(8,128)(2,1)S(1)}, u32[]{:S(2)}, u32[]{:S(2)}) collective-permute-start(bf16[96,384]{1,0:T(8,128)(2,1)S(1)} %get-tuple-element.175), channel_id=1, source_target_pairs={{0,4},{4,0},{8,12},{12,8},{1,5},{5,1},{9,13},{13,9},{2,6},{6,2},{1... | collective-permute-start | bytes 221192 | tf_op jit(solution)/shard_map/ppermute | solution.py:1206
  25.9 6.5 %collective-permute-start.12 = (bf16[96,384]{1,0:T(8,128)(2,1)S(1)}, bf16[96,384]{1,0:T(8,128)(2,1)S(1)}, u32[]{:S(2)}, u32[]{:S(2)}) collective-permute-start(bf16[96,384]{1,0:T(8,128)(2,1)S(1)} %get-tuple-element.176), channel_id=1, source_target_pairs={{0,12},{4,8},{8,4},{12,0},{1,13},{5,9},{9,5},{13,1},{2,14},{6,10},... | collective-permute-start | bytes 221192 | tf_op jit(solution)/shard_map/ppermute | solution.py:1206
  30.5 6.5 %collective-permute-start.15 = (bf16[128,384]{1,0:T(8,128)(2,1)S(1)}, bf16[128,384]{1,0:T(8,128)(2,1)S(1)}, u32[]{:S(2)}, u32[]{:S(2)}) collective-permute-start(bf16[128,384]{1,0:T(8,128)(2,1)S(1)} %pad_maximum_fusion.2.refs_0_), channel_id=1, source_target_pairs={{0,16},{16,0},{1,17},{17,1},{2,18},{18,2},{3,19},{19,3},{4,20},{20... | collective-permute-start | bytes 294920 | tf_op jit(solution)/shard_map/ppermute | solution.py:926
  32.4 2.7 %collective-permute-start.13 = (bf16[128,384]{1,0:T(8,128)(2,1)S(1)}, bf16[128,384]{1,0:T(8,128)(2,1)S(1)}, u32[]{:S(2)}, u32[]{:S(2)}) collective-permute-start(bf16[128,384]{1,0:T(8,128)(2,1)S(1)} %pad_maximum_fusion.2.refs_0_), channel_id=1, source_target_pairs={{0,2},{2,0},{1,3},{3,1},{4,6},{6,4},{5,7},{7,5},{8,10},{10,8},{9,1... | collective-permute-start | bytes 294920 | tf_op jit(solution)/shard_map/ppermute | solution.py:926
  32.4 2.6 %collective-permute-start.14 = (bf16[128,384]{1,0:T(8,128)(2,1)S(1)}, bf16[128,384]{1,0:T(8,128)(2,1)S(1)}, u32[]{:S(2)}, u32[]{:S(2)}) collective-permute-start(bf16[128,384]{1,0:T(8,128)(2,1)S(1)} %pad_maximum_fusion.3.refs_1_), channel_id=1, source_target_pairs={{0,2},{2,0},{1,3},{3,1},{4,6},{6,4},{5,7},{7,5},{8,10},{10,8},{9,1... | collective-permute-start | bytes 294920 | tf_op jit(solution)/shard_map/ppermute | solution.py:926
  33.8 7.6 %collective-permute-start.17 = (bf16[128,384]{1,0:T(8,128)(2,1)S(1)}, bf16[128,384]{1,0:T(8,128)(2,1)S(1)}, u32[]{:S(2)}, u32[]{:S(2)}) collective-permute-start(bf16[128,384]{1,0:T(8,128)(2,1)S(1)} %pad_maximum_fusion.3.refs_1_), channel_id=1, source_target_pairs={{0,16},{16,0},{1,17},{17,1},{2,18},{18,2},{3,19},{19,3},{4,20},{20... | collective-permute-start | bytes 294920 | tf_op jit(solution)/shard_map/ppermute | solution.py:926
  37.0 1.3 %collective-permute-start.16 = (bf16[128,384]{1,0:T(8,128)(2,1)S(1)}, bf16[128,384]{1,0:T(8,128)(2,1)S(1)}, u32[]{:S(2)}, u32[]{:S(2)}) collective-permute-start(bf16[128,384]{1,0:T(8,128)(2,1)S(1)} %collective-permute-done.15.refs_0_.refs_4_), channel_id=1, source_target_pairs={{0,2},{2,0},{1,3},{3,1},{4,6},{6,4},{5,7},{7,5},{8,10},{10,8},{9,1... | collective-permute-start | bytes 294920 | tf_op jit(solution)/shard_map/ppermute | solution.py:926
  41.4 1.3 %collective-permute-start.18 = (bf16[128,384]{1,0:T(8,128)(2,1)S(1)}, bf16[128,384]{1,0:T(8,128)(2,1)S(1)}, u32[]{:S(2)}, u32[]{:S(2)}) collective-permute-start(bf16[128,384]{1,0:T(8,128)(2,1)S(1)} %collective-permute-done.17.refs_0_.refs_6_), channel_id=1, source_target_pairs={{0,2},{2,0},{1,3},{3,1},{4,6},{6,4},{5,7},{7,5},{8,10},{10,8},{9,1... | collective-permute-start | bytes 294920 | tf_op jit(solution)/shard_map/ppermute | solution.py:926
  43.9 4.0 %collective-permute-start.19 = (bf16[128,96]{1,0:T(8,128)(2,1)S(1)}, bf16[128,96]{1,0:T(8,128)(2,1)S(1)}, u32[]{:S(2)}, u32[]{:S(2)}) collective-permute-start(bf16[128,96]{1,0:T(8,128)(2,1)S(1)} %get-tuple-element.196), channel_id=1, source_target_pairs={{0,4},{4,0},{1,5},{5,1},{2,6},{6,2},{3,7},{7,3},{8,12},{12,8},{9,1... | collective-permute-start | bytes 73736 | tf_op jit(solution)/shard_map/ppermute | solution.py:1239
  49.3 4.0 %collective-permute-start.20 = (bf16[128,96]{1,0:T(8,128)(2,1)S(1)}, bf16[128,96]{1,0:T(8,128)(2,1)S(1)}, u32[]{:S(2)}, u32[]{:S(2)}) collective-permute-start(bf16[128,96]{1,0:T(8,128)(2,1)S(1)} %get-tuple-element.219), channel_id=1, source_target_pairs={{0,4},{4,0},{1,5},{5,1},{2,6},{6,2},{3,7},{7,3},{8,12},{12,8},{9,1... | collective-permute-start | bytes 73736 | tf_op jit(solution)/shard_map/ppermute | solution.py:1239
  55.7 1.4 %collective-permute-start.21 = (bf16[128,384]{1,0:T(8,128)(2,1)S(1)}, bf16[128,384]{1,0:T(8,128)(2,1)S(1)}, u32[]{:S(2)}, u32[]{:S(2)}) collective-permute-start(bf16[128,384]{1,0:T(8,128)(2,1)S(1)} %get-tuple-element.249), channel_id=1, source_target_pairs={{0,2},{2,0},{1,3},{3,1},{4,6},{6,4},{5,7},{7,5},{8,10},{10,8},{9,1... | collective-permute-start | bytes 294920 | tf_op jit(solution)/shard_map/ppermute | solution.py:926
  55.8 1.4 %collective-permute-start.22 = (bf16[128,384]{1,0:T(8,128)(2,1)S(1)}, bf16[128,384]{1,0:T(8,128)(2,1)S(1)}, u32[]{:S(2)}, u32[]{:S(2)}) collective-permute-start(bf16[128,384]{1,0:T(8,128)(2,1)S(1)} %get-tuple-element.250), channel_id=1, source_target_pairs={{0,2},{2,0},{1,3},{3,1},{4,6},{6,4},{5,7},{7,5},{8,10},{10,8},{9,1... | collective-permute-start | bytes 294920 | tf_op jit(solution)/shard_map/ppermute | solution.py:926
  57.3 6.6 %collective-permute-start.25 = (bf16[4,4,40,128]{3,2,1,0:T(8,128)(2,1)S(1)}, bf16[4,4,40,128]{3,2,1,0:T(8,128)(2,1)S(1)}, u32[]{:S(2)}, u32[]{:S(2)}) collective-permute-start(bf16[4,4,40,128]{3,2,1,0:T(8,128)(2,1)S(1)} %get-tuple-element.277), channel_id=1, source_target_pairs={{0,2},{2,0},{1,3},{3,1},{4,6},{6,4},{5,7},{7,5},{8,10},{10,8},{9,1... | collective-permute-start | bytes 491528 | tf_op jit(solution)/shard_map/ppermute | solution.py:926
  57.7 9.8 %collective-permute-start.23 = (bf16[128,384]{1,0:T(8,128)(2,1)S(1)}, bf16[128,384]{1,0:T(8,128)(2,1)S(1)}, u32[]{:S(2)}, u32[]{:S(2)}) collective-permute-start(bf16[128,384]{1,0:T(8,128)(2,1)S(1)} %get-tuple-element.259), channel_id=1, source_target_pairs={{0,16},{16,0},{1,17},{17,1},{2,18},{18,2},{3,19},{19,3},{4,20},{20... | collective-permute-start | bytes 294920 | tf_op jit(solution)/shard_map/ppermute | solution.py:926
  57.7 11.4 %collective-permute-start.24 = (bf16[128,384]{1,0:T(8,128)(2,1)S(1)}, bf16[128,384]{1,0:T(8,128)(2,1)S(1)}, u32[]{:S(2)}, u32[]{:S(2)}) collective-permute-start(bf16[128,384]{1,0:T(8,128)(2,1)S(1)} %get-tuple-element.260), channel_id=1, source_target_pairs={{0,16},{16,0},{1,17},{17,1},{2,18},{18,2},{3,19},{19,3},{4,20},{20... | collective-permute-start | bytes 294920 | tf_op jit(solution)/shard_map/ppermute | solution.py:926
  64.0 5.1 %collective-permute-start.28 = (bf16[4,40,128]{2,1,0:T(8,128)(2,1)S(1)}, bf16[4,40,128]{2,1,0:T(8,128)(2,1)S(1)}, u32[]{:S(2)}, u32[]{:S(2)}) collective-permute-start(bf16[4,40,128]{2,1,0:T(8,128)(2,1)S(1)} %get-tuple-element.320), channel_id=1, source_target_pairs={{0,1},{1,0},{4,5},{5,4},{2,3},{3,2},{6,7},{7,6},{8,9},{9,8},{12,13... | collective-permute-start | bytes 122888 | tf_op jit(solution)/shard_map/ppermute | solution.py:936
  64.5 4.6 %collective-permute-start.27 = (bf16[4,40,128]{2,1,0:T(8,128)(2,1)S(1)}, bf16[4,40,128]{2,1,0:T(8,128)(2,1)S(1)}, u32[]{:S(2)}, u32[]{:S(2)}) collective-permute-start(bf16[4,40,128]{2,1,0:T(8,128)(2,1)S(1)} %get-tuple-element.321), channel_id=1, source_target_pairs={{0,4},{1,5},{4,0},{5,1},{2,6},{3,7},{6,2},{7,3},{8,12},{9,13},{12,... | collective-permute-start | bytes 122888 | tf_op jit(solution)/shard_map/ppermute | solution.py:936
  65.0 4.9 %collective-permute-start.26 = (bf16[4,40,128]{2,1,0:T(8,128)(2,1)S(1)}, bf16[4,40,128]{2,1,0:T(8,128)(2,1)S(1)}, u32[]{:S(2)}, u32[]{:S(2)}) collective-permute-start(bf16[4,40,128]{2,1,0:T(8,128)(2,1)S(1)} %get-tuple-element.322), channel_id=1, source_target_pairs={{0,5},{1,4},{4,1},{5,0},{2,7},{3,6},{6,3},{7,2},{8,13},{9,12},{12,... | collective-permute-start | bytes 122888 | tf_op jit(solution)/shard_map/ppermute | solution.py:936
  69.9 1.3 %collective-permute-start.29 = (bf16[128,384]{1,0:T(8,128)(2,1)S(1)}, bf16[128,384]{1,0:T(8,128)(2,1)S(1)}, u32[]{:S(2)}, u32[]{:S(2)}) collective-permute-start(bf16[128,384]{1,0:T(8,128)(2,1)S(1)} %get-tuple-element.282), channel_id=1, source_target_pairs={{0,2},{2,0},{1,3},{3,1},{4,6},{6,4},{5,7},{7,5},{8,10},{10,8},{9,1... | collective-permute-start | bytes 294920 | tf_op jit(solution)/shard_map/ppermute | solution.py:926
  69.9 2.0 %collective-permute-start.31 = (bf16[128,384]{1,0:T(8,128)(2,1)S(1)}, bf16[128,384]{1,0:T(8,128)(2,1)S(1)}, u32[]{:S(2)}, u32[]{:S(2)}) collective-permute-start(bf16[128,384]{1,0:T(8,128)(2,1)S(1)} %get-tuple-element.286), channel_id=1, source_target_pairs={{0,2},{2,0},{1,3},{3,1},{4,6},{6,4},{5,7},{7,5},{8,10},{10,8},{9,1... | collective-permute-start | bytes 294920 | tf_op jit(solution)/shard_map/ppermute | solution.py:926
  71.3 7.5 %collective-permute-start.30 = (bf16[128,384]{1,0:T(8,128)(2,1)S(1)}, bf16[128,384]{1,0:T(8,128)(2,1)S(1)}, u32[]{:S(2)}, u32[]{:S(2)}) collective-permute-start(bf16[128,384]{1,0:T(8,128)(2,1)S(1)} %pad_maximum_fusion.4), channel_id=1, source_target_pairs={{0,8},{4,12},{8,0},{12,4},{1,9},{5,13},{9,1},{13,5},{2,10},{6,14},... | collective-permute-start | bytes 294920 | tf_op jit(solution)/shard_map/ppermute | solution.py:1206
  71.9 4.4 %collective-permute-start.32 = (bf16[96,384]{1,0:T(8,128)(2,1)S(1)}, bf16[96,384]{1,0:T(8,128)(2,1)S(1)}, u32[]{:S(2)}, u32[]{:S(2)}) collective-permute-start(bf16[96,384]{1,0:T(8,128)(2,1)S(1)} %pad_maximum_fusion.5), channel_id=1, source_target_pairs={{0,4},{4,0},{8,12},{12,8},{1,5},{5,1},{9,13},{13,9},{2,6},{6,2},{1... | collective-permute-start | bytes 221192 | tf_op jit(solution)/shard_map/ppermute | solution.py:1206
  73.0 5.7 %collective-permute-start.33 = (bf16[96,384]{1,0:T(8,128)(2,1)S(1)}, bf16[96,384]{1,0:T(8,128)(2,1)S(1)}, u32[]{:S(2)}, u32[]{:S(2)}) collective-permute-start(bf16[96,384]{1,0:T(8,128)(2,1)S(1)} %pad_maximum_fusion.6), channel_id=1, source_target_pairs={{0,12},{4,8},{8,4},{12,0},{1,13},{5,9},{9,5},{13,1},{2,14},{6,10},... | collective-permute-start | bytes 221192 | tf_op jit(solution)/shard_map/ppermute | solution.py:1206
  81.2 1.7 %collective-permute-start.34 = (bf16[4,4,80,128]{3,2,1,0:T(8,128)(2,1)S(1)}, bf16[4,4,80,128]{3,2,1,0:T(8,128)(2,1)S(1)}, u32[]{:S(2)}, u32[]{:S(2)}) collective-permute-start(bf16[4,4,80,128]{3,2,1,0:T(8,128)(2,1)S(1)} %get-tuple-element.301), channel_id=1, source_target_pairs={{0,2},{2,0},{1,3},{3,1},{4,6},{6,4},{5,7},{7,5},{8,10},{10,8},{9,1... | collective-permute-start | bytes 983048 | tf_op jit(solution)/shard_map/ppermute | solution.py:926
  83.0 6.0 %collective-permute-start.35 = (bf16[4,80,128]{2,1,0:T(8,128)(2,1)S(1)}, bf16[4,80,128]{2,1,0:T(8,128)(2,1)S(1)}, u32[]{:S(2)}, u32[]{:S(2)}) collective-permute-start(bf16[4,80,128]{2,1,0:T(8,128)(2,1)S(1)} %get-tuple-element.315), channel_id=1, source_target_pairs={{0,5},{1,4},{4,1},{5,0},{2,7},{3,6},{6,3},{7,2},{8,13},{9,12},{12,... | collective-permute-start | bytes 245768 | tf_op jit(solution)/shard_map/ppermute | solution.py:936
  84.7 4.7 %collective-permute-start.37 = (bf16[4,80,128]{2,1,0:T(8,128)(2,1)S(1)}, bf16[4,80,128]{2,1,0:T(8,128)(2,1)S(1)}, u32[]{:S(2)}, u32[]{:S(2)}) collective-permute-start(bf16[4,80,128]{2,1,0:T(8,128)(2,1)S(1)} %get-tuple-element.316), channel_id=1, source_target_pairs={{0,1},{1,0},{4,5},{5,4},{2,3},{3,2},{6,7},{7,6},{8,9},{9,8},{12,13... | collective-permute-start | bytes 245768 | tf_op jit(solution)/shard_map/ppermute | solution.py:936
  85.2 5.0 %collective-permute-start.36 = (bf16[4,80,128]{2,1,0:T(8,128)(2,1)S(1)}, bf16[4,80,128]{2,1,0:T(8,128)(2,1)S(1)}, u32[]{:S(2)}, u32[]{:S(2)}) collective-permute-start(bf16[4,80,128]{2,1,0:T(8,128)(2,1)S(1)} %get-tuple-element.317), channel_id=1, source_target_pairs={{0,4},{1,5},{4,0},{5,1},{2,6},{3,7},{6,2},{7,3},{8,12},{9,13},{12,... | collective-permute-start | bytes 245768 | tf_op jit(solution)/shard_map/ppermute | solution.py:936
  90.3 6.4 %collective-permute-start.38 = (bf16[120,128]{1,0:T(8,128)(2,1)S(1)}, bf16[120,128]{1,0:T(8,128)(2,1)S(1)}, u32[]{:S(2)}, u32[]{:S(2)}) collective-permute-start(bf16[120,128]{1,0:T(8,128)(2,1)S(1)} %get-tuple-element.309), channel_id=1, source_target_pairs={{0,24},{8,16},{16,8},{24,0},{1,25},{9,17},{17,9},{25,1},{2,26},{10... | collective-permute-start | bytes 92168 | tf_op jit(solution)/shard_map/ppermute | solution.py:936
  92.5 5.1 %collective-permute-start.39 = (bf16[120,128]{1,0:T(8,128)(2,1)S(1)}, bf16[120,128]{1,0:T(8,128)(2,1)S(1)}, u32[]{:S(2)}, u32[]{:S(2)}) collective-permute-start(bf16[120,128]{1,0:T(8,128)(2,1)S(1)} %get-tuple-element.310), channel_id=1, source_target_pairs={{0,16},{8,24},{16,0},{24,8},{1,17},{9,25},{17,1},{25,9},{2,18},{10... | collective-permute-start | bytes 92168 | tf_op jit(solution)/shard_map/ppermute | solution.py:936
  93.5 4.2 %collective-permute-start.40 = (bf16[120,128]{1,0:T(8,128)(2,1)S(1)}, bf16[120,128]{1,0:T(8,128)(2,1)S(1)}, u32[]{:S(2)}, u32[]{:S(2)}) collective-permute-start(bf16[120,128]{1,0:T(8,128)(2,1)S(1)} %get-tuple-element.311), channel_id=1, source_target_pairs={{0,8},{8,0},{16,24},{24,16},{1,9},{9,1},{17,25},{25,17},{2,10},{10... | collective-permute-start | bytes 92168 | tf_op jit(solution)/shard_map/ppermute | solution.py:936

commit v3 on v2

--- a/solution.py
+++ b/solution.py
@@ -201,7 +201,7 @@
             q_w_ref[p, at, :] = jnp.concatenate([mats[0][p][side], lane_pad], axis=1)
             kv_w_ref[p, at, :LANES] = jnp.concatenate([mats[1][p][side], lane_pad], axis=1)
             kv_w_ref[p, at, LANES:] = jnp.concatenate([mats[2][p][side], lane_pad], axis=1)
-        kv_wt_ref[p] = kv_w_ref[p].astype(f32).T.astype(bf16)
+        kv_wt_ref[p] = kv_w_ref[p].T
 
     rows = code_ref.shape[1]
     per = LANES // rows
@@ -982,7 +982,7 @@
     )(cells, cot, blocks[0])
     own = jnp.stack([block_held] + along(Z_AXES, list(blocks))[1:])
     own, held = lax.optimization_barrier((own, held))
-    plane = along(PLANE_AXES, [own] * 4)
+    plane = along(PLANE_AXES, list(lax.optimization_barrier((own,) * 4)))
     *shares, counts = pl.pallas_call(
         share_unpack,
         out_shape=(
@@ -1318,7 +1318,9 @@
         )
         mlp_got, g_item = lax.optimization_barrier((mlp_got, g_item))
         mlp_total, mlp_came = over_plane(mlp_keep, mlp_got.astype(f32))
-        from_h, to_c, out_blocks, mlp_came = lax.optimization_barrier((from_h, (lo_c, hi_c), out_blocks, mlp_came))
+        from_h, to_c, out_blocks, mlp_came = lax.optimization_barrier(
+            (from_h, (lo_c, hi_c), out_blocks, mlp_came[::-1])
+        )
         for a in mlp_came:
             mlp_total = mlp_total + a.astype(f32)
         from_c = [swap(a, "core") for a in to_c]

time: 98.6 us -> 98.2 us (level)
  waiting for transfers between devices: 31 us -> 28.9 us
  starting transfers between devices: 38.1 us -> 39.5 us
    ppermute x15, waiting for transfers between devices: 12.3 us -> 11.2 us  [along(): lax.ppermute(a, axes, [(i, i ^ x) for i in range(Z)])]
  transfers between devices with their start and end apart: 41 -> 41, of which waited for: 23 -> 23; matrix products, arithmetic and copies ran while one was open for 0% -> 0% of each run, Pallas kernels for 13% -> 14%
where the time goes in v3:
time: 98.2 us; the launch traced here: 97.9 us
  starting transfers between devices  39.5 us (40%)
  waiting for transfers between devices  28.9 us (29%)
  Pallas kernels  25.3 us (26%)
  local copies, waits for them, and re-layouts  2.79 us (3%)
  between operations  0.99 us (1%)
    ppermute x15, starting transfers between devices, along(): lax.ppermute(a, axes, [(i, i ^ x) for i in range(Z)])  20.9 us
    ppermute x15, waiting for transfers between devices, along(): lax.ppermute(a, axes, [(i, i ^ x) for i in range(Z)])  11.2 us
    pallas_call x6, Pallas kernels, item_call(): pl.pallas_call(kernel, out_shape=[a for a, _ in outs], in_specs=specs(ins...  10.8 us
    ppermute x18, waiting for transfers between devices, swap(): return lax.ppermute(a, axis, [(0, 1), (1, 0)])  10.1 us
    ppermute x18, starting transfers between devices, swap(): return lax.ppermute(a, axis, [(0, 1), (1, 0)])  9.14 us
    ppermute x6, starting transfers between devices, to_task(): lax.ppermute(block, TASK_AXES, [(j, j ^ TASK_ORDER[i]) for j in range(Z)])  7.23 us
    ppermute x6, waiting for transfers between devices, to_task(): lax.ppermute(block, TASK_AXES, [(j, j ^ TASK_ORDER[i]) for j in range(Z)])  5.38 us
    pallas_call x2, Pallas kernels, middle_call(): pl.pallas_call(functools.partial(row_middle, shared), out_shape=ready + [...  3.05 us
  transfers between devices with their start and end apart: 41, of which 23 were waited for; matrix products, arithmetic and copies ran while one was open for 0% of the time, Pallas kernels for 14%

profile of v3, /device:TPU:0, one launch (start us, length us, event | category | flops | bytes accessed | tf_op | source)
XLA Modules:
  0.0 97.9 jit_solution(282928147707987697)
XLA Ops:
  0.6 1.5 %share_pack.1 = (bf16[112,128]{1,0:T(8,128)(2,1)}, bf16[112,128]{1,0:T(8,128)(2,1)}, bf16[112,128]{1,0:T(8,128)(2,1)}, bf16[112,128]{1,0:T(8,128)(2,1)}) custom-call(bf16[48,192]{1,0:T(8,128)(2,1)} %refs_0_.1, bf16[24,192]{1,0:T(8,128)(2,1)} %refs_1_.1, bf16[1,48]{1,0:T(2,128)(2,1)} %bitcast.70, s32[1,64]{1,0:T(1,128)} %refs_3_.1, s32[1,64]{1,0:T(1,128)} %refs_4_.1, ...), custom_call_target="tpu_custom_call" | custom-call | tf_op jit(solution)/shard_map/share_pack/pallas_call | solution.py:966
  2.1 5.1 %collective-permute-start = (bf16[112,128]{1,0:T(8,128)(2,1)}, bf16[112,128]{1,0:T(8,128)(2,1)S(1)}, u32[]{:S(2)}, u32[]{:S(2)}) collective-permute-start(bf16[112,128]{1,0:T(8,128)(2,1)} %get-tuple-element.166), channel_id=1, source_target_pairs={{0,24},{8,16},{16,8},{24,0},{1,25},{9,17},{17,9},{25,1},{2,26},{10... | collective-permute-start | bytes 86024 | tf_op jit(solution)/shard_map/ppermute | solution.py:936
  7.9 0.9 copy-done
  8.8 0.9 copy-done.1
  10.6 1.7 %collective-permute-done.1 = bf16[112,128]{1,0:T(8,128)(2,1)S(1)} collective-permute-done((bf16[112,128]{1,0:T(8,128)(2,1)}, bf16[112,128]{1,0:T(8,128)(2,1)S(1)}, u32[]{:S(2)}, u32[]{:S(2)}) %collective-permute-start.1) | collective-permute-done | bytes 28704 | tf_op jit(solution)/shard_map/ppermute | solution.py:936
  12.3 2.5 %collective-permute-start.3 = (bf16[4,112,128]{2,1,0:T(8,128)(2,1)S(1)}, bf16[4,112,128]{2,1,0:T(8,128)(2,1)S(1)}, u32[]{:S(2)}, u32[]{:S(2)}) collective-permute-start(bf16[4,112,128]{2,1,0:T(8,128)(2,1)S(1)} %pad_maximum_fusion.1.refs_0_), channel_id=1, source_target_pairs={{0,5},{1,4},{4,1},{5,0},{2,7},{3,6},{6,3},{7,2},{8,13},{9,12},{12,... | collective-permute-start | bytes 344072 | tf_op jit(solution)/shard_map/ppermute | solution.py:936
  15.8 3.4 %collective-permute-done.3.refs_1_ = bf16[4,112,128]{2,1,0:T(8,128)(2,1)S(1)} collective-permute-done((bf16[4,112,128]{2,1,0:T(8,128)(2,1)S(1)}, bf16[4,112,128]{2,1,0:T(8,128)(2,1)S(1)}, u32[]{:S(2)}, u32[]{:S(2)}) %collective-permute-start.3) | collective-permute-done | bytes 114720 | tf_op jit(solution)/shard_map/ppermute | solution.py:936
  22.0 1.9 %feat_forward.1 = (f32[384,192]{1,0:T(8,128)S(1)}, f32[384,192]{1,0:T(8,128)S(1)}, bf16[3,384,192]{2,1,0:T(8,128)(2,1)S(1)}, bf16[384,192]{1,0:T(8,128)(2,1)S(1)...) custom-call(bf16[384,192]{1,0:T(8,128)(2,1)S(1)} %get-tuple-element., ...), custom_call_target="tpu_custom_call" | custom-call | tf_op jit(solution)/shard_map/feat_forward/pallas_call | solution.py:1082
  23.9 1.5 %collective-permute-start.11 = (bf16[96,384]{1,0:T(8,128)(2,1)S(1)}, bf16[96,384]{1,0:T(8,128)(2,1)S(1)}, u32[]{:S(2)}, u32[]{:S(2)}) collective-permute-start(bf16[96,384]{1,0:T(8,128)(2,1)S(1)} %get-tuple-element.183), channel_id=1, source_target_pairs={{0,4},{4,0},{8,12},{12,8},{1,5},{5,1},{9,13},{13,9},{2,6},{6,2},{1... | collective-permute-start | bytes 221192 | tf_op jit(solution)/shard_map/ppermute | solution.py:1206
  25.4 2.0 %collective-permute-start.12 = (bf16[96,384]{1,0:T(8,128)(2,1)S(1)}, bf16[96,384]{1,0:T(8,128)(2,1)S(1)}, u32[]{:S(2)}, u32[]{:S(2)}) collective-permute-start(bf16[96,384]{1,0:T(8,128)(2,1)S(1)} %get-tuple-element.184), channel_id=1, source_target_pairs={{0,12},{4,8},{8,4},{12,0},{1,13},{5,9},{9,5},{13,1},{2,14},{6,10},... | collective-permute-start | bytes 221192 | tf_op jit(solution)/shard_map/ppermute | solution.py:1206
  27.4 2.1 %collective-permute-done.10 = bf16[128,384]{1,0:T(8,128)(2,1)S(1)} collective-permute-done((bf16[128,384]{1,0:T(8,128)(2,1)S(1)}, bf16[128,384]{1,0:T(8,128)(2,1)S(1)}, u32[]{:S(2)}, u32[]{:S(2)}) %collective-permute-start.10) | collective-permute-done | bytes 98336 | tf_op jit(solution)/shard_map/ppermute | solution.py:1206
  29.6 2.1 %collective-permute-start.15 = (bf16[128,384]{1,0:T(8,128)(2,1)S(1)}, bf16[128,384]{1,0:T(8,128)(2,1)S(1)}, u32[]{:S(2)}, u32[]{:S(2)}) collective-permute-start(bf16[128,384]{1,0:T(8,128)(2,1)S(1)} %pad_maximum_fusion.2.refs_0_), channel_id=1, source_target_pairs={{0,16},{16,0},{1,17},{17,1},{2,18},{18,2},{3,19},{19,3},{4,20},{20... | collective-permute-start | bytes 294920 | tf_op jit(solution)/shard_map/ppermute | solution.py:926
  32.3 0.9 item_prepare.1
  33.3 1.3 %collective-permute-start.17 = (bf16[128,384]{1,0:T(8,128)(2,1)S(1)}, bf16[128,384]{1,0:T(8,128)(2,1)S(1)}, u32[]{:S(2)}, u32[]{:S(2)}) collective-permute-start(bf16[128,384]{1,0:T(8,128)(2,1)S(1)} %pad_maximum_fusion.3.refs_1_), channel_id=1, source_target_pairs={{0,16},{16,0},{1,17},{17,1},{2,18},{18,2},{3,19},{19,3},{4,20},{20... | collective-permute-start | bytes 294920 | tf_op jit(solution)/shard_map/ppermute | solution.py:926
  34.5 1.9 %item_forward.3 = (bf16[9,512,256]{2,1,0:T(8,128)(2,1)S(1)}, f32[16,256]{1,0:T(8,128)S(1)}, bf16[3,256,128]{2,1,0:T(8,128)(2,1)S(1)}, f32[16,256]{1,0:T(8,128)S(1)}, f32[384,256]{1,0:T(8,128)S(1)}) custom-call(bf16[128,384]{1,0:T(8,128)(2,1)S(1)} %pad_maximum_fusion.2.refs_0_, bf16[128,384]{1,0:T(8,128)(2,1)S(1)} %pad_maximum_fusion.3.refs_1_, ...), custom_call_target="tpu_custom_call" | custom-call | flops 100000000 | tf_op jit(solution)/shard_map/item_forward/pallas_call | solution.py:1120
  36.7 1.1 %collective-permute-done.16.refs_1_.refs_5_ = bf16[128,384]{1,0:T(8,128)(2,1)S(1)} collective-permute-done((bf16[128,384]{1,0:T(8,128)(2,1)S(1)}, bf16[128,384]{1,0:T(8,128)(2,1)S(1)}, u32[]{:S(2)}, u32[]{:S(2)}) %collective-permute-start.16) | collective-permute-done | bytes 98336 | tf_op jit(solution)/shard_map/ppermute | solution.py:926
  37.8 1.1 %item_forward.4 = (bf16[9,256,256]{2,1,0:T(8,128)(2,1)S(1)}, f32[16,256]{1,0:T(8,128)S(1)}, f32[16,256]{1,0:T(8,128)S(1)}, f32[16,256]{1,0:T(8,128)S(1)}, f32[384,256]{1,0:T(8,128)S(1)}) custom-call(bf16[128,384]{1,0:T(8,128)(2,1)S(1)} %collective-permute-done.15.refs_0_.refs_4_, bf16[128,384]{1,0:T(8,128)(2,1)S(1)} %collective-permute-done.16.refs_1_.refs_5_, ...), custom_call_target="tpu_custom_call" | custom-call | flops 100000000 | tf_op jit(solution)/shard_map/item_forward/pallas_call | solution.py:1120
  38.9 2.2 %collective-permute-done.17.refs_0_.refs_6_ = bf16[128,384]{1,0:T(8,128)(2,1)S(1)} collective-permute-done((bf16[128,384]{1,0:T(8,128)(2,1)S(1)}, bf16[128,384]{1,0:T(8,128)(2,1)S(1)}, u32[]{:S(2)}, u32[]{:S(2)}) %collective-permute-start.17) | collective-permute-done | bytes 98336 | tf_op jit(solution)/shard_map/ppermute | solution.py:926
  41.1 1.3 %collective-permute-done.18.refs_1_.refs_7_ = bf16[128,384]{1,0:T(8,128)(2,1)S(1)} collective-permute-done((bf16[128,384]{1,0:T(8,128)(2,1)S(1)}, bf16[128,384]{1,0:T(8,128)(2,1)S(1)}, u32[]{:S(2)}, u32[]{:S(2)}) %collective-permute-start.18) | collective-permute-done | bytes 98336 | tf_op jit(solution)/shard_map/ppermute | solution.py:926
  42.4 1.1 %item_forward.5 = (bf16[9,256,256]{2,1,0:T(8,128)(2,1)S(1)}, f32[16,256]{1,0:T(8,128)S(1)}, f32[16,256]{1,0:T(8,128)S(1)}, f32[16,256]{1,0:T(8,128)S(1)}, f32[38...) custom-call(bf16[128,384]{1,0:T(8,128)(2,1)S(1)} %collective-permute, ...), custom_call_target="tpu_custom_call" | custom-call | flops 100000000 | tf_op jit(solution)/shard_map/item_forward/pallas_call | solution.py:1120
  43.5 1.1 %collective-permute-start.19 = (bf16[128,96]{1,0:T(8,128)(2,1)S(1)}, bf16[128,96]{1,0:T(8,128)(2,1)S(1)}, u32[]{:S(2)}, u32[]{:S(2)}) collective-permute-start(bf16[128,96]{1,0:T(8,128)(2,1)S(1)} %get-tuple-element.204), channel_id=1, source_target_pairs={{0,4},{4,0},{1,5},{5,1},{2,6},{6,2},{3,7},{7,3},{8,12},{12,8},{9,1... | collective-permute-start | bytes 73736 | tf_op jit(solution)/shard_map/ppermute | solution.py:1239
  44.6 1.6 %row_middle.2 = (f32[128,192]{1,0:T(8,128)S(1)}, f32[128,192]{1,0:T(8,128)S(1)}, bf16[192,192]{1,0:T(8,128)(2,1)S(1)}, f32[256,192]{1,0:T(8,128)S(1)}, bf16[256,...) custom-call(bf16[192,192]{1,0:T(8,128)(2,1)S(1)} %slice.141.w_ref, ...), custom_call_target="tpu_custom_call" | custom-call | tf_op jit(solution)/shard_map/row_middle/pallas_call | solution.py:1250
  46.2 1.2 %collective-permute-done.19.refs_3_.refs_2_ = bf16[128,96]{1,0:T(8,128)(2,1)S(1)} collective-permute-done((bf16[128,96]{1,0:T(8,128)(2,1)S(1)}, bf16[128,96]{1,0:T(8,128)(2,1)S(1)}, u32[]{:S(2)}, u32[]{:S(2)}) %collective-permute-start.19) | collective-permute-done | bytes 24608 | tf_op jit(solution)/shard_map/ppermute | solution.py:1239
  47.5 1.5 %row_middle.3 = (f32[128,192]{1,0:T(8,128)S(1)}, bf16[128,192]{1,0:T(8,128)(2,1)S(1)}, bf16[128,192]{1,0:T(8,128)(2,1)S(1)}, bf16[128,384]{1,0:T(8,128)(2,1)S(1)...) custom-call(bf16[192,192]{1,0:T(8,128)(2,1)S(1)} %get-tuple-element., ...), custom_call_target="tpu_custom_call" | custom-call | tf_op jit(solution)/shard_map/row_middle/pallas_call | solution.py:1250
  49.0 1.1 %collective-permute-start.20 = (bf16[128,96]{1,0:T(8,128)(2,1)S(1)}, bf16[128,96]{1,0:T(8,128)(2,1)S(1)}, u32[]{:S(2)}, u32[]{:S(2)}) collective-permute-start(bf16[128,96]{1,0:T(8,128)(2,1)S(1)} %get-tuple-element.227), channel_id=1, source_target_pairs={{0,4},{4,0},{1,5},{5,1},{2,6},{6,2},{3,7},{7,3},{8,12},{12,8},{9,1... | collective-permute-start | bytes 73736 | tf_op jit(solution)/shard_map/ppermute | solution.py:1239
  50.1 1.0 item_turn.1
  52.0 0.9 collective-permute-done.20.refs_12_
  52.9 2.4 %item_backward.2 = (f32[128,384]{1,0:T(8,128)S(1)}, bf16[128,384]{1,0:T(8,128)(2,1)S(1)}, f32[128,384]{1,0:T(8,128)S(1)}, bf16[128,384]{1,0:T(8,128)(2,1)S(1)}, ...) custom-call(bf16[384,256]{1,0:T(8,128)(2,1)S(1)} %get-tuple-element.206.refs_0_, ...), custom_call_target="tpu_custom_call" | custom-call | flops 100000000 | tf_op jit(solution)/shard_map/item_backward/pallas_call | solution.py:1120
  57.3 2.9 %collective-permute-start.24 = (bf16[128,384]{1,0:T(8,128)(2,1)S(1)}, bf16[128,384]{1,0:T(8,128)(2,1)S(1)}, u32[]{:S(2)}, u32[]{:S(2)}) collective-permute-start(bf16[128,384]{1,0:T(8,128)(2,1)S(1)} %get-tuple-element.268), channel_id=1, source_target_pairs={{0,16},{16,0},{1,17},{17,1},{2,18},{18,2},{3,19},{19,3},{4,20},{20... | collective-permute-start | bytes 294920 | tf_op jit(solution)/shard_map/ppermute | solution.py:926
  60.3 3.3 %item_backward.3 = (f32[128,384]{1,0:T(8,128)S(1)}, f32[128,384]{1,0:T(8,128)S(1)}, bf16[128,384]{1,0:T(8,128)(2,1)S(1)}, bf16[128,384]{1,0:T(8,128)(2,1)S(1)}, f32[576,192]{1,0:T(8,128)S(1)}) custom-call(bf16[384,512]{1,0:T(8,128)(2,1)S(1)} %get-tuple-element.269.refs_0_, bf16[3,512,128]{2,1,0:T(8,128)(2,1)S(1)} %get-tuple-element.270.refs_1_, ...), custom_call_target="tpu_custom_call" | custom-call | flops 100000000 | tf_op jit(solution)/shard_map/item_backward/pallas_call | solution.py:1120
  63.6 1.1 %collective-permute-start.28 = (bf16[4,40,128]{2,1,0:T(8,128)(2,1)S(1)}, bf16[4,40,128]{2,1,0:T(8,128)(2,1)S(1)}, u32[]{:S(2)}, u32[]{:S(2)}) collective-permute-start(bf16[4,40,128]{2,1,0:T(8,128)(2,1)S(1)} %get-tuple-element.328), channel_id=1, source_target_pairs={{0,5},{1,4},{4,1},{5,0},{2,7},{3,6},{6,3},{7,2},{8,13},{9,12},{12,... | collective-permute-start | bytes 122888 | tf_op jit(solution)/shard_map/ppermute | solution.py:936
  64.7 0.9 collective-permute-start.27
  65.7 1.5 %collective-permute-start.26 = (bf16[4,40,128]{2,1,0:T(8,128)(2,1)S(1)}, bf16[4,40,128]{2,1,0:T(8,128)(2,1)S(1)}, u32[]{:S(2)}, u32[]{:S(2)}) collective-permute-start(bf16[4,40,128]{2,1,0:T(8,128)(2,1)S(1)} %get-tuple-element.330), channel_id=1, source_target_pairs={{0,1},{1,0},{4,5},{5,4},{2,3},{3,2},{6,7},{7,6},{8,9},{9,8},{12,13... | collective-permute-start | bytes 122888 | tf_op jit(solution)/shard_map/ppermute | solution.py:936
  67.2 2.0 %collective-permute-done.24 = bf16[128,384]{1,0:T(8,128)(2,1)S(1)} collective-permute-done((bf16[128,384]{1,0:T(8,128)(2,1)S(1)}, bf16[128,384]{1,0:T(8,128)(2,1)S(1)}, u32[]{:S(2)}, u32[]{:S(2)}) %collective-permute-start.24) | collective-permute-done | bytes 98336 | tf_op jit(solution)/shard_map/ppermute | solution.py:926
  71.3 1.1 %collective-permute-start.32 = (bf16[96,384]{1,0:T(8,128)(2,1)S(1)}, bf16[96,384]{1,0:T(8,128)(2,1)S(1)}, u32[]{:S(2)}, u32[]{:S(2)}) collective-permute-start(bf16[96,384]{1,0:T(8,128)(2,1)S(1)} %pad_maximum_fusion.5), channel_id=1, source_target_pairs={{0,4},{4,0},{8,12},{12,8},{1,5},{5,1},{9,13},{13,9},{2,6},{6,2},{1... | collective-permute-start | bytes 221192 | tf_op jit(solution)/shard_map/ppermute | solution.py:1206
  72.4 2.4 %collective-permute-start.33 = (bf16[96,384]{1,0:T(8,128)(2,1)S(1)}, bf16[96,384]{1,0:T(8,128)(2,1)S(1)}, u32[]{:S(2)}, u32[]{:S(2)}) collective-permute-start(bf16[96,384]{1,0:T(8,128)(2,1)S(1)} %pad_maximum_fusion.6), channel_id=1, source_target_pairs={{0,12},{4,8},{8,4},{12,0},{1,13},{5,9},{9,5},{13,1},{2,14},{6,10},... | collective-permute-start | bytes 221192 | tf_op jit(solution)/shard_map/ppermute | solution.py:1206
  74.8 1.0 collective-permute-done.32
  75.8 2.3 %collective-permute-done.33 = bf16[96,384]{1,0:T(8,128)(2,1)S(1)} collective-permute-done((bf16[96,384]{1,0:T(8,128)(2,1)S(1)}, bf16[96,384]{1,0:T(8,128)(2,1)S(1)}, u32[]{:S(2)}, u32[]{:S(2)}) %collective-permute-start.33) | collective-permute-done | bytes 73760 | tf_op jit(solution)/shard_map/ppermute | solution.py:1206
  78.1 2.2 %feat_backward.1 = (f32[768,192]{1,0:T(8,128)S(1)}, f32[8,192]{1,0:T(8,128)S(1)}, f32[384,192]{1,0:T(8,128)S(1)}, bf16[3,384,192]{2,1,0:T(8,128)(2,1)S(1)}) custom-call(f32[384,192]{1,0:T(8,128)S(1)} %get-tuple-element.298.xhat1_ref, f32[384,192]{1,0:T(8,128)S(1)} %get-tuple-element.299.rstd1_ref, bf16[384,192]{1,0:T(8,128)(2,1)S(1)} %get-tuple-element.171.cells_ref, ...), custom_call_target="tpu_custom_call" | custom-call | tf_op jit(solution)/shard_map/feat_backward/pallas_call | solution.py:1357
  80.7 1.6 %collective-permute-done.34 = bf16[4,4,80,128]{3,2,1,0:T(8,128)(2,1)S(1)} collective-permute-done((bf16[4,4,80,128]{3,2,1,0:T(8,128)(2,1)S(1)}, bf16[4,4,80,128]{3,2,1,0:T(8,128)(2,1)S(1)}, u32[]{:S(2)}, u32[]{:S(2)}) %collective-permute-start.34) | collective-permute-done | bytes 327712 | tf_op jit(solution)/shard_map/ppermute | solution.py:926
  82.4 1.9 %collective-permute-start.35 = (bf16[4,80,128]{2,1,0:T(8,128)(2,1)S(1)}, bf16[4,80,128]{2,1,0:T(8,128)(2,1)S(1)}, u32[]{:S(2)}, u32[]{:S(2)}) collective-permute-start(bf16[4,80,128]{2,1,0:T(8,128)(2,1)S(1)} %get-tuple-element.323), channel_id=1, source_target_pairs={{0,5},{1,4},{4,1},{5,0},{2,7},{3,6},{6,3},{7,2},{8,13},{9,12},{12,... | collective-permute-start | bytes 245768 | tf_op jit(solution)/shard_map/ppermute | solution.py:936
  84.8 1.1 %collective-permute-start.36 = (bf16[4,80,128]{2,1,0:T(8,128)(2,1)S(1)}, bf16[4,80,128]{2,1,0:T(8,128)(2,1)S(1)}, u32[]{:S(2)}, u32[]{:S(2)}) collective-permute-start(bf16[4,80,128]{2,1,0:T(8,128)(2,1)S(1)} %get-tuple-element.325), channel_id=1, source_target_pairs={{0,4},{1,5},{4,0},{5,1},{2,6},{3,7},{6,2},{7,3},{8,12},{9,13},{12,... | collective-permute-start | bytes 245768 | tf_op jit(solution)/shard_map/ppermute | solution.py:936
  86.0 2.5 %collective-permute-done.35 = bf16[4,80,128]{2,1,0:T(8,128)(2,1)S(1)} collective-permute-done((bf16[4,80,128]{2,1,0:T(8,128)(2,1)S(1)}, bf16[4,80,128]{2,1,0:T(8,128)(2,1)S(1)}, u32[]{:S(2)}, u32[]{:S(2)}) %collective-permute-start.35) | collective-permute-done | bytes 81952 | tf_op jit(solution)/shard_map/ppermute | solution.py:936
  89.7 2.4 %collective-permute-start.38 = (bf16[120,128]{1,0:T(8,128)(2,1)S(1)}, bf16[120,128]{1,0:T(8,128)(2,1)S(1)}, u32[]{:S(2)}, u32[]{:S(2)}) collective-permute-start(bf16[120,128]{1,0:T(8,128)(2,1)S(1)} %get-tuple-element.317), channel_id=1, source_target_pairs={{0,24},{8,16},{16,8},{24,0},{1,25},{9,17},{17,9},{25,1},{2,26},{10... | collective-permute-start | bytes 92168 | tf_op jit(solution)/shard_map/ppermute | solution.py:936
  92.9 1.3 %collective-permute-start.40 = (bf16[120,128]{1,0:T(8,128)(2,1)S(1)}, bf16[120,128]{1,0:T(8,128)(2,1)S(1)}, u32[]{:S(2)}, u32[]{:S(2)}) collective-permute-start(bf16[120,128]{1,0:T(8,128)(2,1)S(1)} %get-tuple-element.319), channel_id=1, source_target_pairs={{0,8},{8,0},{16,24},{24,16},{1,9},{9,1},{17,25},{25,17},{2,10},{10... | collective-permute-start | bytes 92168 | tf_op jit(solution)/shard_map/ppermute | solution.py:936
  94.2 0.8 out_collect.1
  95.0 1.1 %cell_out.1 = f32[384,192]{1,0:T(8,128)} custom-call(f32[384,192]{1,0:T(8,128)S(1)} %get-tuple-element.314.dz1_ref, bf16[3,384,192]{2,1,0:T(8,128)(2,1)S(1)} %get-tuple-element.315.dqkv_ref, bf16[576,192]{1,0:T(8,128)(2,1)S(1)} %get-tuple-element.326.w_ref), custom_call_target="tpu_custom_call" | custom-call | tf_op jit(solution)/shard_map/cell_out/pallas_call | solution.py:1380
  96.0 1.1 %collective-permute-done.39.refs_1_ = bf16[120,128]{1,0:T(8,128)(2,1)S(1)} collective-permute-done((bf16[120,128]{1,0:T(8,128)(2,1)S(1)}, bf16[120,128]{1,0:T(8,128)(2,1)S(1)}, u32[]{:S(2)}, u32[]{:S(2)}) %collective-permute-start.39) | collective-permute-done | bytes 30752 | tf_op jit(solution)/shard_map/ppermute | solution.py:936
  (96 shorter events, 15.1 us)
Async XLA Ops:
  2.1 8.4 %collective-permute-start = (bf16[112,128]{1,0:T(8,128)(2,1)}, bf16[112,128]{1,0:T(8,128)(2,1)S(1)}, u32[]{:S(2)}, u32[]{:S(2)}) collective-permute-start(bf16[112,128]{1,0:T(8,128)(2,1)} %get-tuple-element.166), channel_id=1, source_target_pairs={{0,24},{8,16},{16,8},{24,0},{1,25},{9,17},{17,9},{25,1},{2,26},{10... | collective-permute-start | bytes 86024 | tf_op jit(solution)/shard_map/ppermute | solution.py:936
  7.3 5.0 %collective-permute-start.1 = (bf16[112,128]{1,0:T(8,128)(2,1)}, bf16[112,128]{1,0:T(8,128)(2,1)S(1)}, u32[]{:S(2)}, u32[]{:S(2)}) collective-permute-start(bf16[112,128]{1,0:T(8,128)(2,1)} %get-tuple-element.167), channel_id=1, source_target_pairs={{0,16},{8,24},{16,0},{24,8},{1,17},{9,25},{17,1},{25,9},{2,18},{10... | collective-permute-start | bytes 86024 | tf_op jit(solution)/shard_map/ppermute | solution.py:936
  7.3 5.0 %collective-permute-start.2 = (bf16[112,128]{1,0:T(8,128)(2,1)}, bf16[112,128]{1,0:T(8,128)(2,1)S(1)}, u32[]{:S(2)}, u32[]{:S(2)}) collective-permute-start(bf16[112,128]{1,0:T(8,128)(2,1)} %get-tuple-element.168), channel_id=1, source_target_pairs={{0,8},{8,0},{16,24},{24,16},{1,9},{9,1},{17,25},{25,17},{2,10},{10... | collective-permute-start | bytes 86024 | tf_op jit(solution)/shard_map/ppermute | solution.py:936
  7.9 0.9 copy-start
  8.8 0.9 copy-start.1
  9.8 0.7 copy-start.2
  12.3 7.0 %collective-permute-start.3 = (bf16[4,112,128]{2,1,0:T(8,128)(2,1)S(1)}, bf16[4,112,128]{2,1,0:T(8,128)(2,1)S(1)}, u32[]{:S(2)}, u32[]{:S(2)}) collective-permute-start(bf16[4,112,128]{2,1,0:T(8,128)(2,1)S(1)} %pad_maximum_fusion.1.refs_0_), channel_id=1, source_target_pairs={{0,5},{1,4},{4,1},{5,0},{2,7},{3,6},{6,3},{7,2},{8,13},{9,12},{12,... | collective-permute-start | bytes 344072 | tf_op jit(solution)/shard_map/ppermute | solution.py:936
  14.8 5.2 %collective-permute-start.4 = (bf16[4,112,128]{2,1,0:T(8,128)(2,1)S(1)}, bf16[4,112,128]{2,1,0:T(8,128)(2,1)S(1)}, u32[]{:S(2)}, u32[]{:S(2)}) collective-permute-start(bf16[4,112,128]{2,1,0:T(8,128)(2,1)S(1)} %pad_maximum_fusion.1.refs_0_), channel_id=1, source_target_pairs={{0,4},{1,5},{4,0},{5,1},{2,6},{3,7},{6,2},{7,3},{8,12},{9,13},{12,... | collective-permute-start | bytes 344072 | tf_op jit(solution)/shard_map/ppermute | solution.py:936
  15.3 4.8 %collective-permute-start.5 = (bf16[4,112,128]{2,1,0:T(8,128)(2,1)S(1)}, bf16[4,112,128]{2,1,0:T(8,128)(2,1)S(1)}, u32[]{:S(2)}, u32[]{:S(2)}) collective-permute-start(bf16[4,112,128]{2,1,0:T(8,128)(2,1)S(1)} %pad_maximum_fusion.1.refs_0_), channel_id=1, source_target_pairs={{0,1},{1,0},{4,5},{5,4},{2,3},{3,2},{6,7},{7,6},{8,9},{9,8},{12,13... | collective-permute-start | bytes 344072 | tf_op jit(solution)/shard_map/ppermute | solution.py:936
  15.8 4.7 %collective-permute-start.6 = (bf16[4,112,128]{2,1,0:T(8,128)(2,1)S(1)}, bf16[4,112,128]{2,1,0:T(8,128)(2,1)S(1)}, u32[]{:S(2)}, u32[]{:S(2)}) collective-permute-start(bf16[4,112,128]{2,1,0:T(8,128)(2,1)S(1)} %pad_maximum_fusion.1.refs_0_), channel_id=1, source_target_pairs={{0,2},{2,0},{1,3},{3,1},{4,6},{6,4},{5,7},{7,5},{8,10},{10,8},{9,1... | collective-permute-start | bytes 344072 | tf_op jit(solution)/shard_map/ppermute | solution.py:926
  19.2 1.3 %collective-permute-start.7 = (bf16[4,112,128]{2,1,0:T(8,128)(2,1)S(1)}, bf16[4,112,128]{2,1,0:T(8,128)(2,1)S(1)}, u32[]{:S(2)}, u32[]{:S(2)}) collective-permute-start(bf16[4,112,128]{2,1,0:T(8,128)(2,1)S(1)} %collective-permute-done.3.refs_1_), channel_id=1, source_target_pairs={{0,2},{2,0},{1,3},{3,1},{4,6},{6,4},{5,7},{7,5},{8,10},{10,8},{9,1... | collective-permute-start | bytes 344072 | tf_op jit(solution)/shard_map/ppermute | solution.py:926
  20.0 1.3 %collective-permute-start.8 = (bf16[4,112,128]{2,1,0:T(8,128)(2,1)S(1)}, bf16[4,112,128]{2,1,0:T(8,128)(2,1)S(1)}, u32[]{:S(2)}, u32[]{:S(2)}) collective-permute-start(bf16[4,112,128]{2,1,0:T(8,128)(2,1)S(1)} %collective-permute-done.4.refs_2_), channel_id=1, source_target_pairs={{0,2},{2,0},{1,3},{3,1},{4,6},{6,4},{5,7},{7,5},{8,10},{10,8},{9,1... | collective-permute-start | bytes 344072 | tf_op jit(solution)/shard_map/ppermute | solution.py:926
  20.1 1.4 %collective-permute-start.9 = (bf16[4,112,128]{2,1,0:T(8,128)(2,1)S(1)}, bf16[4,112,128]{2,1,0:T(8,128)(2,1)S(1)}, u32[]{:S(2)}, u32[]{:S(2)}) collective-permute-start(bf16[4,112,128]{2,1,0:T(8,128)(2,1)S(1)} %collective-permute-done.5.refs_3_), channel_id=1, source_target_pairs={{0,2},{2,0},{1,3},{3,1},{4,6},{6,4},{5,7},{7,5},{8,10},{10,8},{9,1... | collective-permute-start | bytes 344072 | tf_op jit(solution)/shard_map/ppermute | solution.py:926
  23.9 5.7 %collective-permute-start.10 = (bf16[128,384]{1,0:T(8,128)(2,1)S(1)}, bf16[128,384]{1,0:T(8,128)(2,1)S(1)}, u32[]{:S(2)}, u32[]{:S(2)}) collective-permute-start(bf16[128,384]{1,0:T(8,128)(2,1)S(1)} %get-tuple-element.182), channel_id=1, source_target_pairs={{0,8},{4,12},{8,0},{12,4},{1,9},{5,13},{9,1},{13,5},{2,10},{6,14},... | collective-permute-start | bytes 294920 | tf_op jit(solution)/shard_map/ppermute | solution.py:1206
  23.9 7.7 %collective-permute-start.11 = (bf16[96,384]{1,0:T(8,128)(2,1)S(1)}, bf16[96,384]{1,0:T(8,128)(2,1)S(1)}, u32[]{:S(2)}, u32[]{:S(2)}) collective-permute-start(bf16[96,384]{1,0:T(8,128)(2,1)S(1)} %get-tuple-element.183), channel_id=1, source_target_pairs={{0,4},{4,0},{8,12},{12,8},{1,5},{5,1},{9,13},{13,9},{2,6},{6,2},{1... | collective-permute-start | bytes 221192 | tf_op jit(solution)/shard_map/ppermute | solution.py:1206
  25.4 6.3 %collective-permute-start.12 = (bf16[96,384]{1,0:T(8,128)(2,1)S(1)}, bf16[96,384]{1,0:T(8,128)(2,1)S(1)}, u32[]{:S(2)}, u32[]{:S(2)}) collective-permute-start(bf16[96,384]{1,0:T(8,128)(2,1)S(1)} %get-tuple-element.184), channel_id=1, source_target_pairs={{0,12},{4,8},{8,4},{12,0},{1,13},{5,9},{9,5},{13,1},{2,14},{6,10},... | collective-permute-start | bytes 221192 | tf_op jit(solution)/shard_map/ppermute | solution.py:1206
  29.6 6.9 %collective-permute-start.15 = (bf16[128,384]{1,0:T(8,128)(2,1)S(1)}, bf16[128,384]{1,0:T(8,128)(2,1)S(1)}, u32[]{:S(2)}, u32[]{:S(2)}) collective-permute-start(bf16[128,384]{1,0:T(8,128)(2,1)S(1)} %pad_maximum_fusion.2.refs_0_), channel_id=1, source_target_pairs={{0,16},{16,0},{1,17},{17,1},{2,18},{18,2},{3,19},{19,3},{4,20},{20... | collective-permute-start | bytes 294920 | tf_op jit(solution)/shard_map/ppermute | solution.py:926
  31.7 2.9 %collective-permute-start.13 = (bf16[128,384]{1,0:T(8,128)(2,1)S(1)}, bf16[128,384]{1,0:T(8,128)(2,1)S(1)}, u32[]{:S(2)}, u32[]{:S(2)}) collective-permute-start(bf16[128,384]{1,0:T(8,128)(2,1)S(1)} %pad_maximum_fusion.2.refs_0_), channel_id=1, source_target_pairs={{0,2},{2,0},{1,3},{3,1},{4,6},{6,4},{5,7},{7,5},{8,10},{10,8},{9,1... | collective-permute-start | bytes 294920 | tf_op jit(solution)/shard_map/ppermute | solution.py:926
  31.7 2.8 %collective-permute-start.14 = (bf16[128,384]{1,0:T(8,128)(2,1)S(1)}, bf16[128,384]{1,0:T(8,128)(2,1)S(1)}, u32[]{:S(2)}, u32[]{:S(2)}) collective-permute-start(bf16[128,384]{1,0:T(8,128)(2,1)S(1)} %pad_maximum_fusion.3.refs_1_), channel_id=1, source_target_pairs={{0,2},{2,0},{1,3},{3,1},{4,6},{6,4},{5,7},{7,5},{8,10},{10,8},{9,1... | collective-permute-start | bytes 294920 | tf_op jit(solution)/shard_map/ppermute | solution.py:926
  33.3 7.8 %collective-permute-start.17 = (bf16[128,384]{1,0:T(8,128)(2,1)S(1)}, bf16[128,384]{1,0:T(8,128)(2,1)S(1)}, u32[]{:S(2)}, u32[]{:S(2)}) collective-permute-start(bf16[128,384]{1,0:T(8,128)(2,1)S(1)} %pad_maximum_fusion.3.refs_1_), channel_id=1, source_target_pairs={{0,16},{16,0},{1,17},{17,1},{2,18},{18,2},{3,19},{19,3},{4,20},{20... | collective-permute-start | bytes 294920 | tf_op jit(solution)/shard_map/ppermute | solution.py:926
  36.5 1.3 %collective-permute-start.16 = (bf16[128,384]{1,0:T(8,128)(2,1)S(1)}, bf16[128,384]{1,0:T(8,128)(2,1)S(1)}, u32[]{:S(2)}, u32[]{:S(2)}) collective-permute-start(bf16[128,384]{1,0:T(8,128)(2,1)S(1)} %collective-permute-done.15.refs_0_.refs_4_), channel_id=1, source_target_pairs={{0,2},{2,0},{1,3},{3,1},{4,6},{6,4},{5,7},{7,5},{8,10},{10,8},{9,1... | collective-permute-start | bytes 294920 | tf_op jit(solution)/shard_map/ppermute | solution.py:926
  41.1 1.3 %collective-permute-start.18 = (bf16[128,384]{1,0:T(8,128)(2,1)S(1)}, bf16[128,384]{1,0:T(8,128)(2,1)S(1)}, u32[]{:S(2)}, u32[]{:S(2)}) collective-permute-start(bf16[128,384]{1,0:T(8,128)(2,1)S(1)} %collective-permute-done.17.refs_0_.refs_6_), channel_id=1, source_target_pairs={{0,2},{2,0},{1,3},{3,1},{4,6},{6,4},{5,7},{7,5},{8,10},{10,8},{9,1... | collective-permute-start | bytes 294920 | tf_op jit(solution)/shard_map/ppermute | solution.py:926
  43.5 4.0 %collective-permute-start.19 = (bf16[128,96]{1,0:T(8,128)(2,1)S(1)}, bf16[128,96]{1,0:T(8,128)(2,1)S(1)}, u32[]{:S(2)}, u32[]{:S(2)}) collective-permute-start(bf16[128,96]{1,0:T(8,128)(2,1)S(1)} %get-tuple-element.204), channel_id=1, source_target_pairs={{0,4},{4,0},{1,5},{5,1},{2,6},{6,2},{3,7},{7,3},{8,12},{12,8},{9,1... | collective-permute-start | bytes 73736 | tf_op jit(solution)/shard_map/ppermute | solution.py:1239
  49.0 4.0 %collective-permute-start.20 = (bf16[128,96]{1,0:T(8,128)(2,1)S(1)}, bf16[128,96]{1,0:T(8,128)(2,1)S(1)}, u32[]{:S(2)}, u32[]{:S(2)}) collective-permute-start(bf16[128,96]{1,0:T(8,128)(2,1)S(1)} %get-tuple-element.227), channel_id=1, source_target_pairs={{0,4},{4,0},{1,5},{5,1},{2,6},{6,2},{3,7},{7,3},{8,12},{12,8},{9,1... | collective-permute-start | bytes 73736 | tf_op jit(solution)/shard_map/ppermute | solution.py:1239
  55.3 1.4 %collective-permute-start.21 = (bf16[128,384]{1,0:T(8,128)(2,1)S(1)}, bf16[128,384]{1,0:T(8,128)(2,1)S(1)}, u32[]{:S(2)}, u32[]{:S(2)}) collective-permute-start(bf16[128,384]{1,0:T(8,128)(2,1)S(1)} %get-tuple-element.257), channel_id=1, source_target_pairs={{0,2},{2,0},{1,3},{3,1},{4,6},{6,4},{5,7},{7,5},{8,10},{10,8},{9,1... | collective-permute-start | bytes 294920 | tf_op jit(solution)/shard_map/ppermute | solution.py:926
  55.4 1.4 %collective-permute-start.22 = (bf16[128,384]{1,0:T(8,128)(2,1)S(1)}, bf16[128,384]{1,0:T(8,128)(2,1)S(1)}, u32[]{:S(2)}, u32[]{:S(2)}) collective-permute-start(bf16[128,384]{1,0:T(8,128)(2,1)S(1)} %get-tuple-element.258), channel_id=1, source_target_pairs={{0,2},{2,0},{1,3},{3,1},{4,6},{6,4},{5,7},{7,5},{8,10},{10,8},{9,1... | collective-permute-start | bytes 294920 | tf_op jit(solution)/shard_map/ppermute | solution.py:926
  56.9 6.6 %collective-permute-start.25 = (bf16[4,4,40,128]{3,2,1,0:T(8,128)(2,1)S(1)}, bf16[4,4,40,128]{3,2,1,0:T(8,128)(2,1)S(1)}, u32[]{:S(2)}, u32[]{:S(2)}) collective-permute-start(bf16[4,4,40,128]{3,2,1,0:T(8,128)(2,1)S(1)} %get-tuple-element.285), channel_id=1, source_target_pairs={{0,2},{2,0},{1,3},{3,1},{4,6},{6,4},{5,7},{7,5},{8,10},{10,8},{9,1... | collective-permute-start | bytes 491528 | tf_op jit(solution)/shard_map/ppermute | solution.py:926
  57.3 9.8 %collective-permute-start.23 = (bf16[128,384]{1,0:T(8,128)(2,1)S(1)}, bf16[128,384]{1,0:T(8,128)(2,1)S(1)}, u32[]{:S(2)}, u32[]{:S(2)}) collective-permute-start(bf16[128,384]{1,0:T(8,128)(2,1)S(1)} %get-tuple-element.267), channel_id=1, source_target_pairs={{0,16},{16,0},{1,17},{17,1},{2,18},{18,2},{3,19},{19,3},{4,20},{20... | collective-permute-start | bytes 294920 | tf_op jit(solution)/shard_map/ppermute | solution.py:926
  57.3 11.8 %collective-permute-start.24 = (bf16[128,384]{1,0:T(8,128)(2,1)S(1)}, bf16[128,384]{1,0:T(8,128)(2,1)S(1)}, u32[]{:S(2)}, u32[]{:S(2)}) collective-permute-start(bf16[128,384]{1,0:T(8,128)(2,1)S(1)} %get-tuple-element.268), channel_id=1, source_target_pairs={{0,16},{16,0},{1,17},{17,1},{2,18},{18,2},{3,19},{19,3},{4,20},{20... | collective-permute-start | bytes 294920 | tf_op jit(solution)/shard_map/ppermute | solution.py:926
  63.6 5.5 %collective-permute-start.28 = (bf16[4,40,128]{2,1,0:T(8,128)(2,1)S(1)}, bf16[4,40,128]{2,1,0:T(8,128)(2,1)S(1)}, u32[]{:S(2)}, u32[]{:S(2)}) collective-permute-start(bf16[4,40,128]{2,1,0:T(8,128)(2,1)S(1)} %get-tuple-element.328), channel_id=1, source_target_pairs={{0,5},{1,4},{4,1},{5,0},{2,7},{3,6},{6,3},{7,2},{8,13},{9,12},{12,... | collective-permute-start | bytes 122888 | tf_op jit(solution)/shard_map/ppermute | solution.py:936
  64.7 4.4 %collective-permute-start.27 = (bf16[4,40,128]{2,1,0:T(8,128)(2,1)S(1)}, bf16[4,40,128]{2,1,0:T(8,128)(2,1)S(1)}, u32[]{:S(2)}, u32[]{:S(2)}) collective-permute-start(bf16[4,40,128]{2,1,0:T(8,128)(2,1)S(1)} %get-tuple-element.329), channel_id=1, source_target_pairs={{0,4},{1,5},{4,0},{5,1},{2,6},{3,7},{6,2},{7,3},{8,12},{9,13},{12,... | collective-permute-start | bytes 122888 | tf_op jit(solution)/shard_map/ppermute | solution.py:936
  65.7 4.0 %collective-permute-start.26 = (bf16[4,40,128]{2,1,0:T(8,128)(2,1)S(1)}, bf16[4,40,128]{2,1,0:T(8,128)(2,1)S(1)}, u32[]{:S(2)}, u32[]{:S(2)}) collective-permute-start(bf16[4,40,128]{2,1,0:T(8,128)(2,1)S(1)} %get-tuple-element.330), channel_id=1, source_target_pairs={{0,1},{1,0},{4,5},{5,4},{2,3},{3,2},{6,7},{7,6},{8,9},{9,8},{12,13... | collective-permute-start | bytes 122888 | tf_op jit(solution)/shard_map/ppermute | solution.py:936
  69.7 1.3 %collective-permute-start.29 = (bf16[128,384]{1,0:T(8,128)(2,1)S(1)}, bf16[128,384]{1,0:T(8,128)(2,1)S(1)}, u32[]{:S(2)}, u32[]{:S(2)}) collective-permute-start(bf16[128,384]{1,0:T(8,128)(2,1)S(1)} %get-tuple-element.290), channel_id=1, source_target_pairs={{0,2},{2,0},{1,3},{3,1},{4,6},{6,4},{5,7},{7,5},{8,10},{10,8},{9,1... | collective-permute-start | bytes 294920 | tf_op jit(solution)/shard_map/ppermute | solution.py:926
  69.7 1.5 %collective-permute-start.31 = (bf16[128,384]{1,0:T(8,128)(2,1)S(1)}, bf16[128,384]{1,0:T(8,128)(2,1)S(1)}, u32[]{:S(2)}, u32[]{:S(2)}) collective-permute-start(bf16[128,384]{1,0:T(8,128)(2,1)S(1)} %get-tuple-element.294), channel_id=1, source_target_pairs={{0,2},{2,0},{1,3},{3,1},{4,6},{6,4},{5,7},{7,5},{8,10},{10,8},{9,1... | collective-permute-start | bytes 294920 | tf_op jit(solution)/shard_map/ppermute | solution.py:926
  71.1 7.0 %collective-permute-start.30 = (bf16[128,384]{1,0:T(8,128)(2,1)S(1)}, bf16[128,384]{1,0:T(8,128)(2,1)S(1)}, u32[]{:S(2)}, u32[]{:S(2)}) collective-permute-start(bf16[128,384]{1,0:T(8,128)(2,1)S(1)} %pad_maximum_fusion.4), channel_id=1, source_target_pairs={{0,8},{4,12},{8,0},{12,4},{1,9},{5,13},{9,1},{13,5},{2,10},{6,14},... | collective-permute-start | bytes 294920 | tf_op jit(solution)/shard_map/ppermute | solution.py:1206
  71.3 4.5 %collective-permute-start.32 = (bf16[96,384]{1,0:T(8,128)(2,1)S(1)}, bf16[96,384]{1,0:T(8,128)(2,1)S(1)}, u32[]{:S(2)}, u32[]{:S(2)}) collective-permute-start(bf16[96,384]{1,0:T(8,128)(2,1)S(1)} %pad_maximum_fusion.5), channel_id=1, source_target_pairs={{0,4},{4,0},{8,12},{12,8},{1,5},{5,1},{9,13},{13,9},{2,6},{6,2},{1... | collective-permute-start | bytes 221192 | tf_op jit(solution)/shard_map/ppermute | solution.py:1206
  72.4 5.7 %collective-permute-start.33 = (bf16[96,384]{1,0:T(8,128)(2,1)S(1)}, bf16[96,384]{1,0:T(8,128)(2,1)S(1)}, u32[]{:S(2)}, u32[]{:S(2)}) collective-permute-start(bf16[96,384]{1,0:T(8,128)(2,1)S(1)} %pad_maximum_fusion.6), channel_id=1, source_target_pairs={{0,12},{4,8},{8,4},{12,0},{1,13},{5,9},{9,5},{13,1},{2,14},{6,10},... | collective-permute-start | bytes 221192 | tf_op jit(solution)/shard_map/ppermute | solution.py:1206
  80.6 1.7 %collective-permute-start.34 = (bf16[4,4,80,128]{3,2,1,0:T(8,128)(2,1)S(1)}, bf16[4,4,80,128]{3,2,1,0:T(8,128)(2,1)S(1)}, u32[]{:S(2)}, u32[]{:S(2)}) collective-permute-start(bf16[4,4,80,128]{3,2,1,0:T(8,128)(2,1)S(1)} %get-tuple-element.309), channel_id=1, source_target_pairs={{0,2},{2,0},{1,3},{3,1},{4,6},{6,4},{5,7},{7,5},{8,10},{10,8},{9,1... | collective-permute-start | bytes 983048 | tf_op jit(solution)/shard_map/ppermute | solution.py:926
  82.4 6.0 %collective-permute-start.35 = (bf16[4,80,128]{2,1,0:T(8,128)(2,1)S(1)}, bf16[4,80,128]{2,1,0:T(8,128)(2,1)S(1)}, u32[]{:S(2)}, u32[]{:S(2)}) collective-permute-start(bf16[4,80,128]{2,1,0:T(8,128)(2,1)S(1)} %get-tuple-element.323), channel_id=1, source_target_pairs={{0,5},{1,4},{4,1},{5,0},{2,7},{3,6},{6,3},{7,2},{8,13},{9,12},{12,... | collective-permute-start | bytes 245768 | tf_op jit(solution)/shard_map/ppermute | solution.py:936
  84.3 4.7 %collective-permute-start.37 = (bf16[4,80,128]{2,1,0:T(8,128)(2,1)S(1)}, bf16[4,80,128]{2,1,0:T(8,128)(2,1)S(1)}, u32[]{:S(2)}, u32[]{:S(2)}) collective-permute-start(bf16[4,80,128]{2,1,0:T(8,128)(2,1)S(1)} %get-tuple-element.324), channel_id=1, source_target_pairs={{0,1},{1,0},{4,5},{5,4},{2,3},{3,2},{6,7},{7,6},{8,9},{9,8},{12,13... | collective-permute-start | bytes 245768 | tf_op jit(solution)/shard_map/ppermute | solution.py:936
  84.8 4.7 %collective-permute-start.36 = (bf16[4,80,128]{2,1,0:T(8,128)(2,1)S(1)}, bf16[4,80,128]{2,1,0:T(8,128)(2,1)S(1)}, u32[]{:S(2)}, u32[]{:S(2)}) collective-permute-start(bf16[4,80,128]{2,1,0:T(8,128)(2,1)S(1)} %get-tuple-element.325), channel_id=1, source_target_pairs={{0,4},{1,5},{4,0},{5,1},{2,6},{3,7},{6,2},{7,3},{8,12},{9,13},{12,... | collective-permute-start | bytes 245768 | tf_op jit(solution)/shard_map/ppermute | solution.py:936
  89.7 6.4 %collective-permute-start.38 = (bf16[120,128]{1,0:T(8,128)(2,1)S(1)}, bf16[120,128]{1,0:T(8,128)(2,1)S(1)}, u32[]{:S(2)}, u32[]{:S(2)}) collective-permute-start(bf16[120,128]{1,0:T(8,128)(2,1)S(1)} %get-tuple-element.317), channel_id=1, source_target_pairs={{0,24},{8,16},{16,8},{24,0},{1,25},{9,17},{17,9},{25,1},{2,26},{10... | collective-permute-start | bytes 92168 | tf_op jit(solution)/shard_map/ppermute | solution.py:936
  92.1 5.1 %collective-permute-start.39 = (bf16[120,128]{1,0:T(8,128)(2,1)S(1)}, bf16[120,128]{1,0:T(8,128)(2,1)S(1)}, u32[]{:S(2)}, u32[]{:S(2)}) collective-permute-start(bf16[120,128]{1,0:T(8,128)(2,1)S(1)} %get-tuple-element.318), channel_id=1, source_target_pairs={{0,16},{8,24},{16,0},{24,8},{1,17},{9,25},{17,1},{25,9},{2,18},{10... | collective-permute-start | bytes 92168 | tf_op jit(solution)/shard_map/ppermute | solution.py:936
  92.9 4.3 %collective-permute-start.40 = (bf16[120,128]{1,0:T(8,128)(2,1)S(1)}, bf16[120,128]{1,0:T(8,128)(2,1)S(1)}, u32[]{:S(2)}, u32[]{:S(2)}) collective-permute-start(bf16[120,128]{1,0:T(8,128)(2,1)S(1)} %get-tuple-element.319), channel_id=1, source_target_pairs={{0,8},{8,0},{16,24},{24,16},{1,9},{9,1},{17,25},{25,17},{2,10},{10... | collective-permute-start | bytes 92168 | tf_op jit(solution)/shard_map/ppermute | solution.py:936
